TPU v7x, 512 devices: a whole 4x4x16 slice. The times are simulated.
512 devices in a mesh: blk: 32 (over y, z_lo), wide: 16 (over z_hi, x, core).
Axes of the slice: x: 4, y: 4, z: 16 (z_hi: 2, z_lo: 8; z = z_hi * 8 + z_lo), core: 2. Of those that a mesh axis runs over, the one named last changes fastest.
Arguments:
- source_latent: bfloat16 [65536, 64], P('blk'), may hold values from -2.5 to 2.5
- source_logw: float32 [65536], P('blk'), may hold values from -1.5 to 1.5
- target_latent: bfloat16 [131072, 64], P(('wide', 'blk')), may hold values from -3 to 3
- target_logw: float32 [131072], P(('wide', 'blk')), may hold values from -1.5 to 5
- target_potential: float32 [131072], P(('wide', 'blk')), may hold values from -3 to 90
Outputs:
- source_potential: float32 [65536], P('blk')
- new_target_potential: float32 [131072], P(('wide', 'blk'))
All inputs are finite; a program needn't handle non-finite values.
Results may differ from a plain program's by a relative error of at most 0.0003.
Values may be sent and summed in bfloat16 or wider, within the bound.
No kernel may reach another device: no remote copies, remote signals or barrier semaphores. Data moves between devices by JAX's collectives and lax.ppermute only.
A program may use at most 64 MiB of HBM per device.

v0:
```python
import math

import jax
import jax.numpy as jnp
from jax import lax
from jax.sharding import PartitionSpec as P

epsilon = 0.5


def merged(x, axis, combine):
    everything = jax.tree.map(lambda part: lax.all_gather(part, axis), x)
    initial = jax.tree.map(lambda part: part[0], everything)

    def step(k, so_far):
        return combine(so_far, jax.tree.map(lambda part: part[k], everything))

    return lax.fori_loop(1, lax.axis_size(axis), step, initial)


def combine(first, second):
    highest = jnp.maximum(first[0], second[0])
    return (
        highest,
        first[1] * jnp.exp(first[0] - highest) + second[1] * jnp.exp(second[0] - highest),
    )


def partial_lse(row_latent, row_squares, col_latent, col_squares, col_offset):
    rows, width = row_latent.shape
    cols = col_latent.shape[0]
    row_block = math.gcd(rows, 512)
    col_block = math.gcd(cols, 512)
    col_parts = (
        col_latent.reshape(cols // col_block, col_block, width),
        col_squares.reshape(cols // col_block, col_block),
        col_offset.reshape(cols // col_block, col_block),
    )

    def one_rows(inputs):
        latent, squares = inputs

        def advance(running, portion):
            clatent, csquares, coffset = portion
            inner = jnp.einsum("rd,cd->rc", latent, clatent, preferred_element_type=jnp.float32)
            cost = 0.5 * (squares[:, None] + csquares[None, :]) - inner
            score = coffset[None, :] - cost / epsilon
            highest = jnp.max(score, axis=1)
            masses = jnp.sum(jnp.exp(score - highest[:, None]), axis=1)
            return (combine(running, (highest, masses)), None)

        initial = (jnp.full((row_block,), -1e30, jnp.float32), jnp.zeros((row_block,), jnp.float32))
        result, unused = lax.scan(advance, initial, col_parts)
        return result

    maxima, masses = lax.map(
        one_rows,
        (
            row_latent.reshape(rows // row_block, row_block, width),
            row_squares.reshape(rows // row_block, row_block),
        ),
    )
    return (maxima.reshape(rows), masses.reshape(rows))


def squares_of(latent):
    return jnp.sum(jnp.square(latent.astype(jnp.float32)), axis=1)


def merge_ranges(maxima, masses):
    maxima, masses = merged((maxima, masses), "wide", combine)
    return -epsilon * (maxima + jnp.log(masses))


def per_device(source_latent, source_logw, target_latent, target_logw, target_potential):
    source_sq = squares_of(source_latent)
    target_sq = squares_of(target_latent)
    src_count = source_latent.shape[0]
    tgt_count = target_latent.shape[0]
    range_offset = lax.all_gather(
        target_potential / epsilon + target_logw, "blk", axis=0, tiled=True
    )
    initial = (jnp.full((src_count,), -1e30, jnp.float32), jnp.zeros((src_count,), jnp.float32))
    portion = lax.all_gather(target_latent, "blk", axis=0, tiled=True)
    offset = range_offset
    maxima, masses = combine(
        initial, partial_lse(source_latent, source_sq, portion, squares_of(portion), offset)
    )
    source_potential = merge_ranges(maxima, masses)
    all_offsets = lax.all_gather(
        source_potential / epsilon + source_logw, "blk", axis=0, tiled=True
    )
    initial = (jnp.full((tgt_count,), -1e30, jnp.float32), jnp.zeros((tgt_count,), jnp.float32))
    portion = lax.all_gather(source_latent, "blk", axis=0, tiled=True)
    offset = all_offsets
    maxima, masses = combine(
        initial, partial_lse(target_latent, target_sq, portion, squares_of(portion), offset)
    )
    new_target_potential = -epsilon * (maxima + jnp.log(masses))
    return (source_potential, new_target_potential)


def solution(mesh):
    placed = (
        P("blk", None),
        P("blk"),
        P(("wide", "blk"), None),
        P(("wide", "blk")),
        P(("wide", "blk")),
    )
    return jax.shard_map(
        per_device,
        mesh=mesh,
        in_specs=placed,
        out_specs=(P("blk"), P(("wide", "blk"))),
        check_vma=False,
    )
```

profile of v0, /device:TPU:6, one launch (start us, length us, event | category | flops | bytes accessed | tf_op | source)
XLA Modules:
  0.0 652.6 jit_solution(657972316614009884)
XLA Ops:
  8.6 1.2 copy.10
  12.4 125.1 %all-gather = f32[32,1,256]{2,1,0:T(1,128)S(1)} all-gather(f32[1,1,256]{2,1,0:T(1,128)S(1)} %bitcast.109), channel_id=1, replica_groups=mesh['blk'=32,'wide'=16] {'blk'}, dimensions={0}, use_global_device_ids=true | all-gather | bytes 33792 | tf_op jit(solution)/shard_map/all_gather | solution.py:80
  137.7 57.9 %all-gather.6.cloned.1.call-done = bf16[8192,64]{0,1:T(8,128)(2,1)} async-done(((bf16[256,64]{0,1:T(8,128)(2,1)}), bf16[8192,64]{0,1:T(8,128)(2,1)}) %all-gather.6.cloned.1.call-update) | async-done | bytes 1048592 | tf_op jit(solution)/shard_map/all_gather | solution.py:84
  195.6 1.5 multiply_reduce_fusion.1
  197.1 2.0 copy.11
  199.1 41.8 %while.65 = (s32[]{:T(128)}, f32[4,512]{1,0:T(4,128)S(1)}, f32[4,512]{1,0:T(4,128)S(1)}, bf16[4,512,64]{2,1,0:T(8,128)(2,1)S(1)}, f32[4,512]{1,0:T(4,128)S(1)}, ...) while((s32[]{:T(128)}, f32[4,512]{1,0:T(4,128)S(1)}, ...), condition=%wide.region_7.8_spmd, body=%wide.region_2.7_spmd.sunk | while | flops 35654656 | bytes 2535764 | solution.py:56
  199.2 10.3 %while.68 = (s32[]{:T(128)}, f32[512]{0:T(512)S(1)}, f32[512]{0:T(512)S(1)}, f32[16,512]{1,0:T(8,128)S(1)}, f32[512]{0:T(512)S(1)}, /*index=5*/f32[16,512]{1,0:T...) while((s32[]{:T(128)}, f32[512]{0:T(512)S(1)}, ...), condition=%wide.region_6.6_spmd.clone, body=%wide.region_3.5_spmd.clone.sunk | while | flops 35654656 | bytes 2392183 | solution.py:53
  209.7 10.3 %while.68 = (s32[]{:T(128)}, f32[512]{0:T(512)S(1)}, f32[512]{0:T(512)S(1)}, f32[16,512]{1,0:T(8,128)S(1)}, f32[512]{0:T(512)S(1)}, /*index=5*/f32[16,512]{1,0:T...) while((s32[]{:T(128)}, f32[512]{0:T(512)S(1)}, ...), condition=%wide.region_6.6_spmd.clone, body=%wide.region_3.5_spmd.clone.sunk | while | flops 35654656 | bytes 2392183 | solution.py:53
  220.1 10.3 %while.68 = (s32[]{:T(128)}, f32[512]{0:T(512)S(1)}, f32[512]{0:T(512)S(1)}, f32[16,512]{1,0:T(8,128)S(1)}, f32[512]{0:T(512)S(1)}, /*index=5*/f32[16,512]{1,0:T...) while((s32[]{:T(128)}, f32[512]{0:T(512)S(1)}, ...), condition=%wide.region_6.6_spmd.clone, body=%wide.region_3.5_spmd.clone.sunk | while | flops 35654656 | bytes 2392183 | solution.py:53
  230.6 10.3 %while.68 = (s32[]{:T(128)}, f32[512]{0:T(512)S(1)}, f32[512]{0:T(512)S(1)}, f32[16,512]{1,0:T(8,128)S(1)}, f32[512]{0:T(512)S(1)}, /*index=5*/f32[16,512]{1,0:T...) while((s32[]{:T(128)}, f32[512]{0:T(512)S(1)}, ...), condition=%wide.region_6.6_spmd.clone, body=%wide.region_3.5_spmd.clone.sunk | while | flops 35654656 | bytes 2392183 | solution.py:53
  241.0 33.5 %all-gather.1 = f32[16,1,2048]{2,1,0:T(1,128)S(1)} all-gather(f32[1,1,2048]{2,1,0:T(1,128)S(1)} %get-tuple-element.425), channel_id=1, replica_groups=mesh['blk'=32,'wide'=16] {'wide'}, dimensions={0}, use_global_device_ids=true | all-gather | bytes 139264 | tf_op jit(solution)/shard_map/all_gather | solution.py:12
  274.5 36.6 %all-gather.2 = f32[16,1,2048]{2,1,0:T(1,128)S(1)} all-gather(f32[1,1,2048]{2,1,0:T(1,128)S(1)} %get-tuple-element.424), channel_id=1, replica_groups=mesh['blk'=32,'wide'=16] {'wide'}, dimensions={0}, use_global_device_ids=true | all-gather | bytes 139264 | tf_op jit(solution)/shard_map/all_gather | solution.py:12
  312.8 118.8 %all_gather.24 = f32[65536]{0:T(1024)S(1)} all-gather(f32[2048]{0:T(1024)S(1)} %get-tuple-element.422), channel_id=1, replica_groups=mesh['blk'=32,'wide'=16] {'blk'}, dimensions={0}, use_global_device_ids=true | all-gather | bytes 270336 | tf_op jit(solution)/shard_map/all_gather | solution.py:90
  431.6 19.5 %all-gather.8.cloned.1.call-done = bf16[65536,64]{0,1:T(8,128)(2,1)} async-done(((bf16[2048,64]{0,1:T(8,128)(2,1)}), bf16[65536,64]{0,1:T(8,128)(2,1)}) %all-gather.8.cloned.1.call-update) | async-done | bytes 8388624 | tf_op jit(solution)/shard_map/all_gather | solution.py:94
  451.2 5.4 multiply_reduce_fusion
  456.6 15.6 %copy.12 = bf16[65536,64]{1,0:T(8,128)(2,1)} copy(bf16[65536,64]{0,1:T(8,128)(2,1)} %all-gather.8.cloned.1.call-done) | data formatting | bytes 16777216 | tf_op jit(solution)/shard_map/all_gather | solution.py:94
  472.2 173.0 %while.67 = (s32[]{:T(128)}, f32[256]{0:T(256)S(1)}, f32[256]{0:T(256)S(1)}, f32[128,512]{1,0:T(8,128)S(1)}, f32[256]{0:T(256)S(1)}, /*index=5*/f32[128,512]{1,0...) while((s32[]{:T(128)}, f32[256]{0:T(256)S(1)}, ...), condition=%wide.region_15.16_spmd.clone, body=%wide.region_12.15_spmd.clone.sunk | while | flops 17827328 | bytes 1235571 | solution.py:53
  472.2 1.2 fusion.33
  473.6 1.2 fusion.33
  476.3 1.2 fusion.33
  479.0 1.2 fusion.33
  481.7 1.2 fusion.33
  492.5 1.2 fusion.33
  495.2 1.2 fusion.33
  (846 shorter events, 208.8 us)
Async XLA Ops:
  7.2 188.4 %all-gather.6.cloned.1.call-start = ((), (), s32[]{:S(2)}) async-start(), calls=%async_computation | async-start | bytes 1081344 | tf_op jit(solution)/shard_map/all_gather | solution.py:84
  7.9 443.3 %all-gather.8.cloned.1.call-start = ((), (), s32[]{:S(2)}) async-start(), calls=%async_computation.1 | async-start | bytes 8650752 | tf_op jit(solution)/shard_map/all_gather | solution.py:94
  199.1 113.1 %copy-start.1 = (f32[2048]{0:T(1024)S(1)}, f32[2048]{0:T(1024)}, u32[]{:S(2)}) copy-start(f32[2048]{0:T(1024)} %param.14) | copy-start | bytes 24580
  456.6 15.6 %copy-start = (bf16[256,64]{0,1:T(8,128)(2,1)S(1)}, bf16[256,64]{0,1:T(8,128)(2,1)}, u32[]{:S(2)}) copy-start(bf16[256,64]{0,1:T(8,128)(2,1)} %param.15) | copy-start | bytes 98308
Sparse Core Ops, SparseCore 0:
  10.0 185.5 all-gather.5
  197.7 253.4 all-gather.7
where the time goes:
time: 656 us; the launch traced here: 653 us
  blocking collectives  314 us (48%)
  matrix products  174 us (27%)
  waiting for transfers between devices  78.8 us (12%)
  other arithmetic  43.7 us (7%)
  local copies, waits for them, and re-layouts  22.1 us (3%)
  between operations  14.2 us (2%)
    dot_general x192, matrix products, advance(): jnp.einsum('rd,cd->rc', latent, clatent, preferred_element_type=jnp.float32)  174 us
    all_gather x1, blocking collectives, per_device(): lax.all_gather(target_potential / epsilon + target_logw, 'blk', axis=0, t...  125 us
    all_gather x1, blocking collectives, per_device(): lax.all_gather(source_potential / epsilon + source_logw, 'blk', axis=0, t...  119 us
    all_gather x2, blocking collectives, merged(): everything = jax.tree.map(lambda part: lax.all_gather(part, axis), x)  70 us
    all_gather x1, waiting for transfers between devices, per_device(): portion = lax.all_gather(target_latent, 'blk', axis=0, tiled=True)  57.9 us
    reduce_sum x192, other arithmetic, advance(): masses = jnp.sum(jnp.exp(score - highest[:, None]), axis=1)  28.7 us
    all_gather x1, waiting for transfers between devices, per_device(): portion = lax.all_gather(source_latent, 'blk', axis=0, tiled=True)  19.5 us
    all_gather x1, local copies, waits for them, and re-layouts, per_device(): portion = lax.all_gather(source_latent, 'blk', axis=0, tiled=True)  15.6 us
  transfers between devices with their start and end apart: 2, of which 2 were waited for; matrix products, arithmetic and copies ran while one was open for 7% of the time, Pallas kernels for 0%

commit v1 on v0

v1 whole, which is shorter than its diff:
```python
import functools

import jax
import jax.numpy as jnp
from jax import lax
from jax.experimental import pallas as pl
from jax.experimental.pallas import tpu as pltpu
from jax.sharding import PartitionSpec as P

ZRUN = 8
FEATURES = 64
EXTRA = 16
DEPTH = 128
LANES = 1024
STEP = 256
LOW = 2.0**-60
HIGH = 2.0**120


def three_parts(value):
    high = value.astype(jnp.bfloat16).astype(jnp.float32)
    rest = value - high
    middle = rest.astype(jnp.bfloat16).astype(jnp.float32)
    low = (rest - middle).astype(jnp.bfloat16).astype(jnp.float32)
    return high, middle, low


def extra_block(first, second):
    n = first[0].shape[1]
    row = lax.broadcasted_iota(jnp.int32, (EXTRA, n), 0)
    block = jnp.zeros((EXTRA, n), jnp.float32)
    for k, part in enumerate(tuple(first) + tuple(second)):
        block = jnp.where(row == k, part, block)
    return block


def ones_of(n):
    one = jnp.ones((1, n), jnp.float32)
    return one, one, one


def prepare_kernel(y_ref, logw_ref, potential_ref, out_ref, offset_ref):
    y = y_ref[...].astype(jnp.float32)
    offset = potential_ref[...] * 2.0 + logw_ref[...]
    bias = offset - jnp.sum(y * y, axis=0, keepdims=True)
    out_ref[0:FEATURES, :] = (y * 2.0).astype(jnp.bfloat16)
    out_ref[FEATURES : FEATURES + EXTRA, :] = extra_block(
        three_parts(bias), ones_of(bias.shape[1])
    ).astype(jnp.bfloat16)
    offset_ref[...] = offset


def lay_sources(x_refs, xs_ref):
    per = x_refs[0].shape[1]
    for r, x_ref in enumerate(x_refs):
        xs_ref[0:FEATURES, r * per : (r + 1) * per] = x_ref[...]


def weights_at(xs_ref, at):
    part = xs_ref[:, at]
    rest = jnp.zeros((DEPTH - part.shape[0], part.shape[1]), part.dtype)
    return jnp.concatenate([part, rest], axis=0)


def product(a, b):
    return jnp.dot(a, b, preferred_element_type=jnp.float32)


def folded(value, combine):
    rows, n = value.shape
    return combine(value.reshape(rows // 8, 8, n), axis=0)


def join(a, b):
    top = jnp.maximum(a, b)
    return top + jnp.log(1.0 + jnp.exp(jnp.minimum(a, b) - top))


def first_kernel(ny, last, *refs):
    y_ref, x_refs, refs = refs[0], refs[1 : 1 + ny], refs[1 + ny :]
    if last:
        place_ref, before_ref, logw_ref, refs = refs[0], refs[1], refs[2], refs[3:]
    yt_ref, l_ref, xs_ref, sums_ref = refs
    rows = yt_ref.shape[0]
    per = x_refs[0].shape[1]
    cols = ny * per
    wide = min(LANES, cols)
    row_step = min(STEP, rows)
    col_step = min(STEP, wide)

    extra = y_ref[FEATURES : FEATURES + EXTRA, :].astype(jnp.float32)
    bias = extra[0:1, :] + extra[1:2, :] + extra[2:3, :]
    shift = jnp.max(bias, axis=1, keepdims=True)
    for k in range(0, rows, row_step):
        block = jnp.concatenate(
            [
                y_ref[:, k : k + row_step].astype(jnp.float32),
                jnp.zeros((DEPTH - FEATURES - EXTRA, row_step), jnp.float32),
            ],
            axis=0,
        )
        yt_ref[k : k + row_step, :] = block.T.astype(jnp.bfloat16)
    lay_sources(x_refs, xs_ref)
    xs_ref[FEATURES : FEATURES + EXTRA, :] = extra_block(
        ones_of(cols), three_parts(jnp.broadcast_to(-shift, (1, cols)))
    ).astype(jnp.bfloat16)

    def store(row, value):
        if last:
            here = pl.ds(place_ref[0] ^ row, 1)
            l_ref[here, :] = join(before_ref[row : row + 1, :], value)
        else:
            l_ref[row : row + 1, :] = value

    if last:
        l_ref[...] = jnp.zeros(l_ref.shape, jnp.float32)
        l_ref[pl.ds(ny + place_ref[0], 1), :] = logw_ref[...]

    def main(g, carry):
        for t in range(wide // col_step):
            at = pl.ds(pl.multiple_of(g * wide + t * col_step, col_step), col_step)
            weights = weights_at(xs_ref, at)
            total = jnp.zeros((8, col_step), jnp.float32)
            for j in range(rows // row_step):
                score = product(yt_ref[j * row_step : (j + 1) * row_step, :], weights)
                total = total + folded(jnp.exp(score), jnp.sum)
            sums_ref[:, at] = total
        return carry

    lax.fori_loop(0, cols // wide, main, 0)
    total = jnp.sum(sums_ref[...], axis=0, keepdims=True)
    result = shift + jnp.log(total)
    for r in range(ny):
        store(r, result[:, r * per : (r + 1) * per])

    @pl.when(jnp.logical_not((jnp.min(total) > LOW) & (jnp.max(total) < HIGH)))
    def _():
        def again(g, carry):
            at = pl.ds(pl.multiple_of(g * col_step, col_step), col_step)
            weights = weights_at(xs_ref, at)

            def advance(j, state):
                top, total = state
                here = pl.ds(pl.multiple_of(j * row_step, row_step), row_step)
                score = product(yt_ref[here, :], weights)
                new = jnp.maximum(top, jnp.max(score, axis=0, keepdims=True))
                total = total * jnp.exp(top - new) + jnp.sum(
                    jnp.exp(score - new), axis=0, keepdims=True
                )
                return new, total

            start = (
                jnp.full((1, col_step), -1e30, jnp.float32),
                jnp.zeros((1, col_step), jnp.float32),
            )
            top, total = lax.fori_loop(0, rows // row_step, advance, start)
            sums_ref[0:1, at] = shift + top + jnp.log(total)
            return carry

        lax.fori_loop(0, cols // col_step, again, 0)
        for r in range(ny):
            store(r, sums_ref[0:1, r * per : (r + 1) * per])


def second_kernel(ny, *refs):
    yt_ref, x_refs, place_ref, c_ref = refs[0], refs[1 : 1 + ny], refs[1 + ny], refs[2 + ny]
    s_ref, xs_ref, acc_ref, top_ref = refs[3 + ny :]
    rows = yt_ref.shape[0]
    nz, each = s_ref.shape
    per = x_refs[0].shape[1]
    cols = ny * per
    row_step = min(STEP, rows)
    col_step = min(STEP, cols)

    lay_sources(x_refs, xs_ref)
    for r in range(ny):
        c = c_ref[pl.ds(place_ref[0] ^ r, 1), :]
        xs_ref[FEATURES : FEATURES + EXTRA, r * per : (r + 1) * per] = extra_block(
            ones_of(per), three_parts(c)
        ).astype(jnp.bfloat16)

    def lanes_folded(value, combine):
        out = value[:, 0:128]
        for k in range(1, value.shape[1] // 128):
            out = combine(out, value[:, k * 128 : (k + 1) * 128])
        return out

    def main(g, carry):
        here = pl.ds(pl.multiple_of(g * row_step, row_step), row_step)
        left = yt_ref[here, :]
        total = jnp.zeros((row_step, 128), jnp.float32)
        for t in range(cols // col_step):
            score = product(left, weights_at(xs_ref, slice(t * col_step, (t + 1) * col_step)))
            total = total + lanes_folded(jnp.exp(score), jnp.add)
        acc_ref[here, :] = total
        return carry

    lax.fori_loop(0, rows // row_step, main, 0)
    total = jnp.sum(acc_ref[...].T, axis=0, keepdims=True)
    result = jnp.log(total)
    for k in range(nz):
        s_ref[k : k + 1, :] = result[:, k * each : (k + 1) * each]

    @pl.when(jnp.logical_not((jnp.min(total) > LOW) & (jnp.max(total) < HIGH)))
    def _():
        def again(g, carry):
            here = pl.ds(pl.multiple_of(g * row_step, row_step), row_step)
            left = yt_ref[here, :]

            def advance(t, state):
                top, total = state
                at = pl.ds(pl.multiple_of(t * col_step, col_step), col_step)
                score = product(left, weights_at(xs_ref, at))
                new = jnp.maximum(top, lanes_folded(score, jnp.maximum))
                total = total * jnp.exp(top - new)
                for k in range(col_step // 128):
                    total = total + jnp.exp(score[:, k * 128 : (k + 1) * 128] - new)
                return new, total

            start = (
                jnp.full((row_step, 128), -1e30, jnp.float32),
                jnp.zeros((row_step, 128), jnp.float32),
            )
            top, total = lax.fori_loop(0, cols // col_step, advance, start)
            top_ref[here, :] = top
            acc_ref[here, :] = total
            return carry

        lax.fori_loop(0, rows // row_step, again, 0)
        tops = top_ref[...].T
        top = jnp.max(tops, axis=0, keepdims=True)
        total = jnp.sum(acc_ref[...].T * jnp.exp(tops - top), axis=0, keepdims=True)
        result = top + jnp.log(total)
        for k in range(nz):
            s_ref[k : k + 1, :] = result[:, k * each : (k + 1) * each]


def call(kernel, outs, scratch, flops, exps, *args, scalars=()):
    return pl.pallas_call(
        kernel,
        out_shape=outs,
        in_specs=[
            pl.BlockSpec(memory_space=pltpu.SMEM if k in scalars else pltpu.VMEM)
            for k in range(len(args))
        ],
        scratch_shapes=scratch,
        compiler_params=pltpu.CompilerParams(vmem_limit_bytes=40 * 2**20),
        cost_estimate=pl.CostEstimate(
            flops=flops, bytes_accessed=4 * 2**20, transcendentals=exps
        ),
    )(*args)


def per_device(nz, ny, nw, source_latent, source_logw, target_latent, target_logw, target_potential):
    f32, bf16 = jnp.float32, jnp.bfloat16
    per = source_latent.shape[0]
    each = target_latent.shape[0]
    cols, half = ny * per, nz // 2 * each
    pairs = cols * half
    place = lax.axis_index("blk") // nz
    place_in = place.astype(jnp.int32).reshape(1)
    depth = FEATURES + EXTRA

    def along_y(value, r):
        perm = [(y * nz + z, (y ^ r) * nz + z) for y in range(ny) for z in range(nz)]
        return lax.ppermute(value, "blk", perm)

    def along_z(value, k):
        perm = [(y * nz + z, y * nz + (z ^ k)) for y in range(ny) for z in range(nz)]
        return lax.ppermute(value, "blk", perm)

    def along_wide(value, k):
        return lax.ppermute(value, "wide", [(w, w ^ k) for w in range(nw)])

    y, offset = call(
        prepare_kernel,
        (jax.ShapeDtypeStruct((depth, each), bf16), jax.ShapeDtypeStruct((1, each), f32)),
        [],
        each * FEATURES * 4,
        0,
        target_latent.T,
        target_logw.reshape(1, each),
        target_potential.reshape(1, each),
    )
    x = source_latent.T
    xs = [x] + [along_y(x, r) for r in range(1, ny)]
    bit = nz // 2
    while bit > 1:
        y = jnp.concatenate([y, along_z(y, bit)], axis=1)
        bit //= 2
    *xs, y = lax.optimization_barrier((*xs, y))
    far = along_z(y, 1)

    def first(block, *more):
        last = len(more) > 0
        return call(
            functools.partial(first_kernel, ny, last),
            (
                jax.ShapeDtypeStruct((half, DEPTH), bf16),
                jax.ShapeDtypeStruct((2 * ny if last else ny, per), f32),
            ),
            [pltpu.VMEM((depth, cols), bf16), pltpu.VMEM((8, cols), f32)],
            2 * pairs * DEPTH,
            pairs,
            block,
            *xs,
            *more,
            scalars=(1 + ny,),
        )

    yt_near, total = first(y)
    yt_far, total = first(far, place_in, total, source_logw.reshape(1, per))
    bit = 1
    while bit < ny:
        other = along_y(total, bit)
        row = lax.broadcasted_iota(jnp.int32, total.shape, 0)
        total = jnp.where(row < ny, join(total, other), total + other)
        bit *= 2
    total, logw = total[:ny], total[ny:]
    bit = 1
    while bit < nw:
        total = join(total, along_wide(total, bit))
        bit *= 2
    c = logw - total
    sq = jnp.sum(jnp.square(x.astype(f32)), axis=0, keepdims=True)
    mine = lax.dynamic_slice(total, (place, 0), (1, per))
    source_potential = -0.5 * (mine - sq)

    def second(block):
        return call(
            functools.partial(second_kernel, ny),
            jax.ShapeDtypeStruct((nz // 2, each), f32),
            [
                pltpu.VMEM((depth, cols), bf16),
                pltpu.VMEM((half, 128), f32),
                pltpu.VMEM((half, 128), f32),
            ],
            2 * pairs * DEPTH,
            pairs,
            block,
            *xs,
            place_in,
            c,
            scalars=(1 + ny,),
        )

    away = second(yt_far)
    yt_near, away = lax.optimization_barrier((yt_near, away))
    other = along_z(away, 1)
    sums = join(second(yt_near), other)
    bit = 2
    while bit < nz:
        count = sums.shape[0] // 2
        sums = join(sums[:count], along_z(sums[count:], bit))
        bit *= 2
    new_target_potential = -0.5 * (sums - offset)
    return source_potential.reshape(per), new_target_potential.reshape(each)


def solution(mesh):
    nz = ZRUN
    ny = mesh.shape["blk"] // nz
    nw = mesh.shape["wide"]
    placed = (
        P("blk", None),
        P("blk"),
        P(("wide", "blk"), None),
        P(("wide", "blk")),
        P(("wide", "blk")),
    )
    return jax.shard_map(
        functools.partial(per_device, nz, ny, nw),
        mesh=mesh,
        in_specs=placed,
        out_specs=(P("blk"), P(("wide", "blk"))),
        check_vma=False,
    )
```

time: 656 us -> 183 us (0.28)
  blocking collectives: 314 us -> 0 us
  matrix products: 174 us -> 0 us
  Pallas kernels: 0 us -> 79.9 us
  starting transfers between devices: 0.08 us -> 61.3 us
  other arithmetic: 43.7 us -> 1.61 us
  waiting for transfers between devices: 78.8 us -> 37.1 us
  local copies, waits for them, and re-layouts: 22.1 us -> 1.46 us
  between operations: 14.2 us -> 0.96 us
    all_gather x4 -> x0, blocking collectives: 314 us -> none  [the longest x1 125 us: per_device(): lax.all_gather(target_potential / epsilon + target_logw, 'blk', axis=0, t...]
    dot_general x192 -> x0, matrix products: 174 us -> none  [advance(): jnp.einsum('rd,cd->rc', latent, clatent, preferred_element_type=jnp.float32)]
    pallas_call x0 -> x5, Pallas kernels: none -> 79.9 us  [call(): pl.pallas_call(kernel, out_shape=outs, in_specs=[pl.BlockSpec(memory_spac...]
    all_gather x2 -> x0, waiting for transfers between devices: 77.4 us -> none  [the longest x1 57.9 us: per_device(): portion = lax.all_gather(target_latent, 'blk', axis=0, tiled=True)]
    ppermute x0 -> x15, starting transfers between devices: none -> 61.3 us  [the longest x6 28.7 us: along_z(): return lax.ppermute(value, 'blk', perm)]
    reduce_sum x196 -> x1, other arithmetic: 37.4 us -> 0.07 us  [per_device(): sq = jnp.sum(jnp.square(x.astype(f32)), axis=0, keepdims=True)]
    ppermute x0 -> x15, waiting for transfers between devices: none -> 37.1 us  [the longest x5 14.5 us: along_y(): return lax.ppermute(value, 'blk', perm)]
    all_gather x2 -> x0, local copies, waits for them, and re-layouts: 17.6 us -> none  [the longest x1 15.6 us: per_device(): portion = lax.all_gather(source_latent, 'blk', axis=0, tiled=True)]
  transfers between devices with their start and end apart: 2 -> 15, of which waited for: 2 -> 10; matrix products, arithmetic and copies ran while one was open for 7% -> 0% of each run, Pallas kernels for 0% -> 22%
where the time goes in v1:
time: 183 us; the launch traced here: 182 us
  Pallas kernels  79.9 us (44%)
  starting transfers between devices  61.3 us (33%)
  waiting for transfers between devices  37.1 us (20%)
    pallas_call x5, Pallas kernels, call(): pl.pallas_call(kernel, out_shape=outs, in_specs=[pl.BlockSpec(memory_spac...  79.9 us
    ppermute x6, starting transfers between devices, along_z(): return lax.ppermute(value, 'blk', perm)  28.7 us
    ppermute x4, starting transfers between devices, along_wide(): return lax.ppermute(value, 'wide', [(w, w ^ k) for w in range(nw)])  18 us
    ppermute x5, starting transfers between devices, along_y(): return lax.ppermute(value, 'blk', perm)  14.6 us
    ppermute x5, waiting for transfers between devices, along_y(): return lax.ppermute(value, 'blk', perm)  14.5 us
    ppermute x4, waiting for transfers between devices, along_wide(): return lax.ppermute(value, 'wide', [(w, w ^ k) for w in range(nw)])  12.7 us
    ppermute x6, waiting for transfers between devices, along_z(): return lax.ppermute(value, 'blk', perm)  9.89 us
  transfers between devices with their start and end apart: 15, of which 10 were waited for; matrix products, arithmetic and copies ran while one was open for 0% of the time, Pallas kernels for 22%

profile of v1, /device:TPU:6, one launch (start us, length us, event | category | flops | bytes accessed | tf_op | source)
XLA Modules:
  0.0 182.4 jit_solution(5355109858050606291)
XLA Ops:
  2.1 9.1 %collective-permute-start.3 = (bf16[80,256]{1,0:T(8,128)(2,1)S(1)}, bf16[80,256]{1,0:T(8,128)(2,1)S(1)}, u32[]{:S(2)}, u32[]{:S(2)}) collective-permute-start(bf16[80,256]{1,0:T(8,128)(2,1)S(1)} %get-tuple-element.15), channel_id=1, source_target_pairs={{0,64},{16,80},{32,96},{48,112},{64,0},{80,16},{96,32},{112,48},{1... | collective-permute-start | bytes 122888 | tf_op jit(solution)/shard_map/ppermute | solution.py:270
  11.2 3.6 %collective-permute-start = (bf16[64,2048]{1,0:T(8,128)(2,1)}, bf16[64,2048]{1,0:T(8,128)(2,1)S(1)}, u32[]{:S(2)}, u32[]{:S(2)}) collective-permute-start(bf16[64,2048]{1,0:T(8,128)(2,1)} %bitcast.10), channel_id=1, source_target_pairs={{0,128},{16,144},{32,160},{48,176},{64,192},{80,208},{96,224},{112... | collective-permute-start | bytes 786440 | tf_op jit(solution)/shard_map/ppermute | solution.py:266
  14.9 4.8 %collective-permute-start.1 = (bf16[64,2048]{1,0:T(8,128)(2,1)}, bf16[64,2048]{1,0:T(8,128)(2,1)S(1)}, u32[]{:S(2)}, u32[]{:S(2)}) collective-permute-start(bf16[64,2048]{1,0:T(8,128)(2,1)} %bitcast.11), channel_id=1, source_target_pairs={{0,256},{16,272},{32,288},{48,304},{64,320},{80,336},{96,352},{112... | collective-permute-start | bytes 786440 | tf_op jit(solution)/shard_map/ppermute | solution.py:266
  21.9 5.2 %collective-permute-start.4 = (bf16[80,512]{1,0:T(8,128)(2,1)S(1)}, bf16[80,512]{1,0:T(8,128)(2,1)S(1)}, u32[]{:S(2)}, u32[]{:S(2)}) collective-permute-start(bf16[80,512]{1,0:T(8,128)(2,1)S(1)} %pad_maximum_fusion.1), channel_id=1, source_target_pairs={{0,32},{16,48},{32,0},{48,16},{64,96},{80,112},{96,64},{112,80},{1... | collective-permute-start | bytes 245768 | tf_op jit(solution)/shard_map/ppermute | solution.py:270
  27.1 2.7 %collective-permute-done.4 = bf16[80,512]{1,0:T(8,128)(2,1)S(1)} collective-permute-done((bf16[80,512]{1,0:T(8,128)(2,1)S(1)}, bf16[80,512]{1,0:T(8,128)(2,1)S(1)}, u32[]{:S(2)}, u32[]{:S(2)}) %collective-permute-start.4) | collective-permute-done | bytes 81952 | tf_op jit(solution)/shard_map/ppermute | solution.py:270
  29.8 4.8 %collective-permute-done.2.refs_4_ = bf16[64,2048]{1,0:T(8,128)(2,1)S(1)} collective-permute-done((bf16[64,2048]{1,0:T(8,128)(2,1)}, bf16[64,2048]{1,0:T(8,128)(2,1)S(1)}, u32[]{:S(2)}, u32[]{:S(2)}) %collective-permute-start.2) | collective-permute-done | bytes 262176 | tf_op jit(solution)/shard_map/ppermute | solution.py:266
  34.6 3.8 %collective-permute-start.5 = (bf16[80,1024]{1,0:T(8,128)(2,1)S(1)}, bf16[80,1024]{1,0:T(8,128)(2,1)S(1)}, u32[]{:S(2)}, u32[]{:S(2)}) collective-permute-start(bf16[80,1024]{1,0:T(8,128)(2,1)S(1)} %pad_maximum_fusion.refs_0_), channel_id=1, source_target_pairs={{0,16},{16,0},{32,48},{48,32},{64,80},{80,64},{96,112},{112,96},{1... | collective-permute-start | bytes 491528 | tf_op jit(solution)/shard_map/ppermute | solution.py:270
  38.5 6.0 %shard_map.69 = (bf16[1024,128]{1,0:T(8,128)(2,1)S(1)}, f32[4,2048]{1,0:T(4,128)S(1)}) custom-call(bf16[80,1024]{1,0:T(8,128)(2,1)S(1)} %pad_maximum_fusion.refs_0_, bf16[64,2048]{1,0:T(8,128)(2,1)S(1)} %bitcast.13, bf16[64,2048]{1,0:T(8,128)(2,1)S(1)} %collective-permute-done.refs_2_, bf16[64,2048]{1,0:T(8,128)(2,1)S(1)} %collective-permute-done.1.refs_3_, ...), custom_call_target="tpu_custom_call" | custom-call | flops 2147483648 | bytes 4194304 | tf_op jit(solution)/shard_map/pallas_call | solution.py:239
  44.5 6.0 %shard_map.70 = (bf16[1024,128]{1,0:T(8,128)(2,1)S(1)}, f32[8,2048]{1,0:T(8,128)S(1)}) custom-call(bf16[80,1024]{1,0:T(8,128)(2,1)S(1)} %collective-permute-done.5.refs_0_, bf16[64,2048]{1,0:T(8,128)(2,1)S(1)} %bitcast.14, bf16[64,2048]{1,0:T(8,128)(2,1)S(1)} %collective-permute-done.refs_2_, bf16[64,2048]{1,0:T(8,128)(2,1)S(1)} %collective-permute-done.1.refs_3_, ...), custom_call_target="tpu_custom_call" | custom-call | flops 2147483648 | bytes 4194304 | tf_op jit(solution)/shard_map/pallas_call | solution.py:239
  52.4 4.2 %collective-permute-done.6 = f32[8,2048]{1,0:T(8,128)S(1)} collective-permute-done((f32[8,2048]{1,0:T(8,128)S(1)}, f32[8,2048]{1,0:T(8,128)S(1)}, u32[]{:S(2)}, u32[]{:S(2)}) %collective-permute-start.6) | collective-permute-done | bytes 65568 | tf_op jit(solution)/shard_map/ppermute | solution.py:266
  56.7 2.1 %collective-permute-start.7 = (f32[8,2048]{1,0:T(8,128)S(1)}, f32[8,2048]{1,0:T(8,128)S(1)}, u32[]{:S(2)}, u32[]{:S(2)}) collective-permute-start(f32[8,2048]{1,0:T(8,128)S(1)} %add_select_fusion.1), channel_id=1, source_target_pairs={{0,256},{16,272},{32,288},{48,304},{64,320},{80,336},{96,352},{112... | collective-permute-start | bytes 196616 | tf_op jit(solution)/shard_map/ppermute | solution.py:266
  58.8 5.5 %collective-permute-done.7 = f32[8,2048]{1,0:T(8,128)S(1)} collective-permute-done((f32[8,2048]{1,0:T(8,128)S(1)}, f32[8,2048]{1,0:T(8,128)S(1)}, u32[]{:S(2)}, u32[]{:S(2)}) %collective-permute-start.7) | collective-permute-done | bytes 65568 | tf_op jit(solution)/shard_map/ppermute | solution.py:266
  67.5 2.7 %collective-permute-start.9 = (f32[4,2048]{1,0:T(4,128)S(1)}, f32[4,2048]{1,0:T(4,128)S(1)}, u32[]{:S(2)}, u32[]{:S(2)}) collective-permute-start(f32[4,2048]{1,0:T(4,128)S(1)} %log_add_fusion.3), channel_id=1, source_target_pairs={{0,2},{1,3},{2,0},{3,1},{4,6},{5,7},{6,4},{7,5},{8,10},{9,11},{10,... | collective-permute-start | bytes 98312 | tf_op jit(solution)/shard_map/ppermute | solution.py:273
  70.3 3.1 %collective-permute-done.9 = f32[4,2048]{1,0:T(4,128)S(1)} collective-permute-done((f32[4,2048]{1,0:T(4,128)S(1)}, f32[4,2048]{1,0:T(4,128)S(1)}, u32[]{:S(2)}, u32[]{:S(2)}) %collective-permute-start.9) | collective-permute-done | bytes 32800 | tf_op jit(solution)/shard_map/ppermute | solution.py:273
  73.4 3.3 %collective-permute-start.10 = (f32[4,2048]{1,0:T(4,128)S(1)}, f32[4,2048]{1,0:T(4,128)S(1)}, u32[]{:S(2)}, u32[]{:S(2)}) collective-permute-start(f32[4,2048]{1,0:T(4,128)S(1)} %log_add_fusion.2), channel_id=1, source_target_pairs={{0,4},{1,5},{2,6},{3,7},{4,0},{5,1},{6,2},{7,3},{8,12},{9,13},{10,... | collective-permute-start | bytes 98312 | tf_op jit(solution)/shard_map/ppermute | solution.py:273
  76.7 4.0 %collective-permute-done.10 = f32[4,2048]{1,0:T(4,128)S(1)} collective-permute-done((f32[4,2048]{1,0:T(4,128)S(1)}, f32[4,2048]{1,0:T(4,128)S(1)}, u32[]{:S(2)}, u32[]{:S(2)}) %collective-permute-start.10) | collective-permute-done | bytes 32800 | tf_op jit(solution)/shard_map/ppermute | solution.py:273
  80.7 10.0 %collective-permute-start.11 = (f32[4,2048]{1,0:T(4,128)S(1)}, f32[4,2048]{1,0:T(4,128)S(1)}, u32[]{:S(2)}, u32[]{:S(2)}) collective-permute-start(f32[4,2048]{1,0:T(4,128)S(1)} %log_add_fusion.1), channel_id=1, source_target_pairs={{0,8},{1,9},{2,10},{3,11},{4,12},{5,13},{6,14},{7,15},{8,0},{9,1},... | collective-permute-start | bytes 98312 | tf_op jit(solution)/shard_map/ppermute | solution.py:273
  90.8 4.5 %collective-permute-done.11 = f32[4,2048]{1,0:T(4,128)S(1)} collective-permute-done((f32[4,2048]{1,0:T(4,128)S(1)}, f32[4,2048]{1,0:T(4,128)S(1)}, u32[]{:S(2)}, u32[]{:S(2)}) %collective-permute-start.11) | collective-permute-done | bytes 32800 | tf_op jit(solution)/shard_map/ppermute | solution.py:273
  95.3 34.0 %shard_map.71 = f32[4,256]{1,0:T(4,128)S(1)} custom-call(bf16[1024,128]{1,0:T(8,128)(2,1)S(1)} %get-tuple-element.24.refs_0_, bf16[64,2048]{1,0:T(8,128)(2,1)S(1)} %bitcast.15, bf16[64,2048]{1,0:T(8,128)(2,1)S(1)} %collective-permute-done.refs_2_, bf16[64,2048]{1,0:T(8,128)(2,1)S(1)} %collective-permute-done.1.refs_3_, ...), custom_call_target="tpu_custom_call" | custom-call | flops 2147483648 | bytes 4194304 | tf_op jit(solution)/shard_map/pallas_call | solution.py:239
  129.3 2.3 %collective-permute-start.12 = (f32[4,256]{1,0:T(4,128)S(1)}, f32[4,256]{1,0:T(4,128)S(1)}, u32[]{:S(2)}, u32[]{:S(2)}) collective-permute-start(f32[4,256]{1,0:T(4,128)S(1)} %shard_map.71), channel_id=1, source_target_pairs={{0,16},{16,0},{32,48},{48,32},{64,80},{80,64},{96,112},{112,96},{1... | collective-permute-start | bytes 12296 | tf_op jit(solution)/shard_map/ppermute | solution.py:270
  131.6 34.0 %shard_map.72 = f32[4,256]{1,0:T(4,128)S(1)} custom-call(bf16[1024,128]{1,0:T(8,128)(2,1)S(1)} %get-tuple-element.25.refs_0_, bf16[64,2048]{1,0:T(8,128)(2,1)S(1)} %bitcast.16, bf16[64,2048]{1,0:T(8,128)(2,1)S(1)} %collective-permute-done.refs_2_, bf16[64,2048]{1,0:T(8,128)(2,1)S(1)} %collective-permute-done.1.refs_3_, ...), custom_call_target="tpu_custom_call" | custom-call | flops 2147483648 | bytes 4194304 | tf_op jit(solution)/shard_map/pallas_call | solution.py:239
  165.6 5.2 %collective-permute-start.13 = (f32[2,256]{1,0:T(2,128)S(1)}, f32[2,256]{1,0:T(2,128)S(1)}, u32[]{:S(2)}, u32[]{:S(2)}) collective-permute-start(f32[2,256]{1,0:T(2,128)S(1)} %slice.27), channel_id=1, source_target_pairs={{0,32},{16,48},{32,0},{48,16},{64,96},{80,112},{96,64},{112,80},{1... | collective-permute-start | bytes 6152 | tf_op jit(solution)/shard_map/ppermute | solution.py:270
  172.4 3.0 %collective-permute-start.14 = (f32[1,256]{1,0:T(1,128)S(1)}, f32[1,256]{1,0:T(1,128)S(1)}, u32[]{:S(2)}, u32[]{:S(2)}) collective-permute-start(f32[1,256]{1,0:T(1,128)S(1)} %slice.29), channel_id=1, source_target_pairs={{0,64},{16,80},{32,96},{48,112},{64,0},{80,16},{96,32},{112,48},{1... | collective-permute-start | bytes 3080 | tf_op jit(solution)/shard_map/ppermute | solution.py:270
  176.1 5.7 %collective-permute-done.14 = f32[1,256]{1,0:T(1,128)S(1)} collective-permute-done((f32[1,256]{1,0:T(1,128)S(1)}, f32[1,256]{1,0:T(1,128)S(1)}, u32[]{:S(2)}, u32[]{:S(2)}) %collective-permute-start.14) | collective-permute-done | bytes 1056 | tf_op jit(solution)/shard_map/ppermute | solution.py:270
  (38 shorter events, 11.7 us)
Async XLA Ops:
  0.6 0.7 copy-start.3
  0.6 0.7 copy-start.2
  1.3 0.8 copy-start.1
  2.1 19.7 %collective-permute-start.3 = (bf16[80,256]{1,0:T(8,128)(2,1)S(1)}, bf16[80,256]{1,0:T(8,128)(2,1)S(1)}, u32[]{:S(2)}, u32[]{:S(2)}) collective-permute-start(bf16[80,256]{1,0:T(8,128)(2,1)S(1)} %get-tuple-element.15), channel_id=1, source_target_pairs={{0,64},{16,80},{32,96},{48,112},{64,0},{80,16},{96,32},{112,48},{1... | collective-permute-start | bytes 122888 | tf_op jit(solution)/shard_map/ppermute | solution.py:270
  11.2 27.2 %copy-start = (bf16[2048,64]{0,1:T(8,128)(2,1)S(1)}, bf16[2048,64]{0,1:T(8,128)(2,1)}, u32[]{:S(2)}) copy-start(bf16[2048,64]{0,1:T(8,128)(2,1)} %param.5) | copy-start | bytes 786436
  11.2 18.6 %collective-permute-start = (bf16[64,2048]{1,0:T(8,128)(2,1)}, bf16[64,2048]{1,0:T(8,128)(2,1)S(1)}, u32[]{:S(2)}, u32[]{:S(2)}) collective-permute-start(bf16[64,2048]{1,0:T(8,128)(2,1)} %bitcast.10), channel_id=1, source_target_pairs={{0,128},{16,144},{32,160},{48,176},{64,192},{80,208},{96,224},{112... | collective-permute-start | bytes 786440 | tf_op jit(solution)/shard_map/ppermute | solution.py:266
  14.9 14.9 %collective-permute-start.1 = (bf16[64,2048]{1,0:T(8,128)(2,1)}, bf16[64,2048]{1,0:T(8,128)(2,1)S(1)}, u32[]{:S(2)}, u32[]{:S(2)}) collective-permute-start(bf16[64,2048]{1,0:T(8,128)(2,1)} %bitcast.11), channel_id=1, source_target_pairs={{0,256},{16,272},{32,288},{48,304},{64,320},{80,336},{96,352},{112... | collective-permute-start | bytes 786440 | tf_op jit(solution)/shard_map/ppermute | solution.py:266
  19.7 15.0 %collective-permute-start.2 = (bf16[64,2048]{1,0:T(8,128)(2,1)}, bf16[64,2048]{1,0:T(8,128)(2,1)S(1)}, u32[]{:S(2)}, u32[]{:S(2)}) collective-permute-start(bf16[64,2048]{1,0:T(8,128)(2,1)} %bitcast.12), channel_id=1, source_target_pairs={{0,384},{16,400},{32,416},{48,432},{64,448},{80,464},{96,480},{112... | collective-permute-start | bytes 786440 | tf_op jit(solution)/shard_map/ppermute | solution.py:266
  21.9 7.9 %collective-permute-start.4 = (bf16[80,512]{1,0:T(8,128)(2,1)S(1)}, bf16[80,512]{1,0:T(8,128)(2,1)S(1)}, u32[]{:S(2)}, u32[]{:S(2)}) collective-permute-start(bf16[80,512]{1,0:T(8,128)(2,1)S(1)} %pad_maximum_fusion.1), channel_id=1, source_target_pairs={{0,32},{16,48},{32,0},{48,16},{64,96},{80,112},{96,64},{112,80},{1... | collective-permute-start | bytes 245768 | tf_op jit(solution)/shard_map/ppermute | solution.py:270
  29.8 14.7 %copy-start.4 = (f32[2048]{0:T(1024)S(1)}, f32[2048]{0:T(1024)}, u32[]{:S(2)}) copy-start(f32[2048]{0:T(1024)} %param.6) | copy-start | bytes 24580
  34.6 9.8 %collective-permute-start.5 = (bf16[80,1024]{1,0:T(8,128)(2,1)S(1)}, bf16[80,1024]{1,0:T(8,128)(2,1)S(1)}, u32[]{:S(2)}, u32[]{:S(2)}) collective-permute-start(bf16[80,1024]{1,0:T(8,128)(2,1)S(1)} %pad_maximum_fusion.refs_0_), channel_id=1, source_target_pairs={{0,16},{16,0},{32,48},{48,32},{64,80},{80,64},{96,112},{112,96},{1... | collective-permute-start | bytes 491528 | tf_op jit(solution)/shard_map/ppermute | solution.py:270
  50.4 6.2 %collective-permute-start.6 = (f32[8,2048]{1,0:T(8,128)S(1)}, f32[8,2048]{1,0:T(8,128)S(1)}, u32[]{:S(2)}, u32[]{:S(2)}) collective-permute-start(f32[8,2048]{1,0:T(8,128)S(1)} %get-tuple-element.22), channel_id=1, source_target_pairs={{0,128},{16,144},{32,160},{48,176},{64,192},{80,208},{96,224},{112... | collective-permute-start | bytes 196616 | tf_op jit(solution)/shard_map/ppermute | solution.py:266
  56.7 7.7 %collective-permute-start.7 = (f32[8,2048]{1,0:T(8,128)S(1)}, f32[8,2048]{1,0:T(8,128)S(1)}, u32[]{:S(2)}, u32[]{:S(2)}) collective-permute-start(f32[8,2048]{1,0:T(8,128)S(1)} %add_select_fusion.1), channel_id=1, source_target_pairs={{0,256},{16,272},{32,288},{48,304},{64,320},{80,336},{96,352},{112... | collective-permute-start | bytes 196616 | tf_op jit(solution)/shard_map/ppermute | solution.py:266
  64.4 3.1 %collective-permute-start.8 = (f32[4,2048]{1,0:T(4,128)S(1)}, f32[4,2048]{1,0:T(4,128)S(1)}, u32[]{:S(2)}, u32[]{:S(2)}) collective-permute-start(f32[4,2048]{1,0:T(4,128)S(1)} %slice.24), channel_id=1, source_target_pairs={{0,1},{1,0},{2,3},{3,2},{4,5},{5,4},{6,7},{7,6},{8,9},{9,8},{10,11... | collective-permute-start | bytes 98312 | tf_op jit(solution)/shard_map/ppermute | solution.py:273
  67.5 5.8 %collective-permute-start.9 = (f32[4,2048]{1,0:T(4,128)S(1)}, f32[4,2048]{1,0:T(4,128)S(1)}, u32[]{:S(2)}, u32[]{:S(2)}) collective-permute-start(f32[4,2048]{1,0:T(4,128)S(1)} %log_add_fusion.3), channel_id=1, source_target_pairs={{0,2},{1,3},{2,0},{3,1},{4,6},{5,7},{6,4},{7,5},{8,10},{9,11},{10,... | collective-permute-start | bytes 98312 | tf_op jit(solution)/shard_map/ppermute | solution.py:273
  73.4 7.3 %collective-permute-start.10 = (f32[4,2048]{1,0:T(4,128)S(1)}, f32[4,2048]{1,0:T(4,128)S(1)}, u32[]{:S(2)}, u32[]{:S(2)}) collective-permute-start(f32[4,2048]{1,0:T(4,128)S(1)} %log_add_fusion.2), channel_id=1, source_target_pairs={{0,4},{1,5},{2,6},{3,7},{4,0},{5,1},{6,2},{7,3},{8,12},{9,13},{10,... | collective-permute-start | bytes 98312 | tf_op jit(solution)/shard_map/ppermute | solution.py:273
  80.7 14.5 %collective-permute-start.11 = (f32[4,2048]{1,0:T(4,128)S(1)}, f32[4,2048]{1,0:T(4,128)S(1)}, u32[]{:S(2)}, u32[]{:S(2)}) collective-permute-start(f32[4,2048]{1,0:T(4,128)S(1)} %log_add_fusion.1), channel_id=1, source_target_pairs={{0,8},{1,9},{2,10},{3,11},{4,12},{5,13},{6,14},{7,15},{8,0},{9,1},... | collective-permute-start | bytes 98312 | tf_op jit(solution)/shard_map/ppermute | solution.py:273
  129.3 36.3 %collective-permute-start.12 = (f32[4,256]{1,0:T(4,128)S(1)}, f32[4,256]{1,0:T(4,128)S(1)}, u32[]{:S(2)}, u32[]{:S(2)}) collective-permute-start(f32[4,256]{1,0:T(4,128)S(1)} %shard_map.71), channel_id=1, source_target_pairs={{0,16},{16,0},{32,48},{48,32},{64,80},{80,64},{96,112},{112,96},{1... | collective-permute-start | bytes 12296 | tf_op jit(solution)/shard_map/ppermute | solution.py:270
  165.6 6.8 %collective-permute-start.13 = (f32[2,256]{1,0:T(2,128)S(1)}, f32[2,256]{1,0:T(2,128)S(1)}, u32[]{:S(2)}, u32[]{:S(2)}) collective-permute-start(f32[2,256]{1,0:T(2,128)S(1)} %slice.27), channel_id=1, source_target_pairs={{0,32},{16,48},{32,0},{48,16},{64,96},{80,112},{96,64},{112,80},{1... | collective-permute-start | bytes 6152 | tf_op jit(solution)/shard_map/ppermute | solution.py:270
  172.4 9.4 %collective-permute-start.14 = (f32[1,256]{1,0:T(1,128)S(1)}, f32[1,256]{1,0:T(1,128)S(1)}, u32[]{:S(2)}, u32[]{:S(2)}) collective-permute-start(f32[1,256]{1,0:T(1,128)S(1)} %slice.29), channel_id=1, source_target_pairs={{0,64},{16,80},{32,96},{48,112},{64,0},{80,16},{96,32},{112,48},{1... | collective-permute-start | bytes 3080 | tf_op jit(solution)/shard_map/ppermute | solution.py:270

commit v2 on v1

--- a/solution.py
+++ b/solution.py
@@ -50,10 +50,10 @@
     offset_ref[...] = offset
 
 
-def lay_sources(x_refs, xs_ref):
-    per = x_refs[0].shape[1]
-    for r, x_ref in enumerate(x_refs):
-        xs_ref[0:FEATURES, r * per : (r + 1) * per] = x_ref[...]
+def lay_sources(x_ref, xs_ref):
+    per = x_ref.shape[2]
+    for r in range(x_ref.shape[0]):
+        xs_ref[0:FEATURES, r * per : (r + 1) * per] = x_ref[r]
 
 
 def weights_at(xs_ref, at):
@@ -76,13 +76,13 @@
     return top + jnp.log(1.0 + jnp.exp(jnp.minimum(a, b) - top))
 
 
-def first_kernel(ny, last, *refs):
-    y_ref, x_refs, refs = refs[0], refs[1 : 1 + ny], refs[1 + ny :]
+def first_kernel(last, *refs):
+    y_ref, x_ref, refs = refs[0], refs[1], refs[2:]
     if last:
-        place_ref, before_ref, logw_ref, refs = refs[0], refs[1], refs[2], refs[3:]
+        before_ref, logw_ref, refs = refs[0], refs[1], refs[2:]
     yt_ref, l_ref, xs_ref, sums_ref = refs
     rows = yt_ref.shape[0]
-    per = x_refs[0].shape[1]
+    ny, _, per = x_ref.shape
     cols = ny * per
     wide = min(LANES, cols)
     row_step = min(STEP, rows)
@@ -100,21 +100,18 @@
             axis=0,
         )
         yt_ref[k : k + row_step, :] = block.T.astype(jnp.bfloat16)
-    lay_sources(x_refs, xs_ref)
+    lay_sources(x_ref, xs_ref)
     xs_ref[FEATURES : FEATURES + EXTRA, :] = extra_block(
         ones_of(cols), three_parts(jnp.broadcast_to(-shift, (1, cols)))
     ).astype(jnp.bfloat16)
 
     def store(row, value):
         if last:
-            here = pl.ds(place_ref[0] ^ row, 1)
-            l_ref[here, :] = join(before_ref[row : row + 1, :], value)
-        else:
-            l_ref[row : row + 1, :] = value
+            value = join(before_ref[row : row + 1, :], value)
+        l_ref[row : row + 1, :] = value
 
     if last:
-        l_ref[...] = jnp.zeros(l_ref.shape, jnp.float32)
-        l_ref[pl.ds(ny + place_ref[0], 1), :] = logw_ref[...]
+        l_ref[ny : ny + 1, :] = logw_ref[...]
 
     def main(g, carry):
         for t in range(wide // col_step):
@@ -162,21 +159,18 @@
             store(r, sums_ref[0:1, r * per : (r + 1) * per])
 
 
-def second_kernel(ny, *refs):
-    yt_ref, x_refs, place_ref, c_ref = refs[0], refs[1 : 1 + ny], refs[1 + ny], refs[2 + ny]
-    s_ref, xs_ref, acc_ref, top_ref = refs[3 + ny :]
-    rows = yt_ref.shape[0]
+def second_kernel(slots, place_ref, near_ref, far_ref, x_ref, c_ref, s_ref, xs_ref, left_ref, acc_ref, top_ref):
     nz, each = s_ref.shape
-    per = x_refs[0].shape[1]
+    rows = nz * each
+    ny, _, per = x_ref.shape
     cols = ny * per
-    row_step = min(STEP, rows)
+    row_step = each
     col_step = min(STEP, cols)
 
-    lay_sources(x_refs, xs_ref)
+    lay_sources(x_ref, xs_ref)
     for r in range(ny):
-        c = c_ref[pl.ds(place_ref[0] ^ r, 1), :]
         xs_ref[FEATURES : FEATURES + EXTRA, r * per : (r + 1) * per] = extra_block(
-            ones_of(per), three_parts(c)
+            ones_of(per), three_parts(c_ref[r : r + 1, :])
         ).astype(jnp.bfloat16)
 
     def lanes_folded(value, combine):
@@ -185,27 +179,36 @@
             out = combine(out, value[:, k * 128 : (k + 1) * 128])
         return out
 
+    for g, (half, k, _) in enumerate(slots):
+        ref = far_ref if half else near_ref
+        left_ref[g * each : (g + 1) * each, :] = ref[k * each : (k + 1) * each, :]
+
     def main(g, carry):
         here = pl.ds(pl.multiple_of(g * row_step, row_step), row_step)
-        left = yt_ref[here, :]
+        left = left_ref[here, :]
         total = jnp.zeros((row_step, 128), jnp.float32)
         for t in range(cols // col_step):
-            score = product(left, weights_at(xs_ref, slice(t * col_step, (t + 1) * col_step)))
+            score = product(
+                left, weights_at(xs_ref, slice(t * col_step, (t + 1) * col_step))
+            )
             total = total + lanes_folded(jnp.exp(score), jnp.add)
         acc_ref[here, :] = total
         return carry
 
     lax.fori_loop(0, rows // row_step, main, 0)
+
+    def store(result):
+        for g, (_, _, row) in enumerate(slots):
+            s_ref[pl.ds(place_ref[0] ^ row, 1), :] = result[:, g * each : (g + 1) * each]
+
     total = jnp.sum(acc_ref[...].T, axis=0, keepdims=True)
-    result = jnp.log(total)
-    for k in range(nz):
-        s_ref[k : k + 1, :] = result[:, k * each : (k + 1) * each]
+    store(jnp.log(total))
 
     @pl.when(jnp.logical_not((jnp.min(total) > LOW) & (jnp.max(total) < HIGH)))
     def _():
         def again(g, carry):
             here = pl.ds(pl.multiple_of(g * row_step, row_step), row_step)
-            left = yt_ref[here, :]
+            left = left_ref[here, :]
 
             def advance(t, state):
                 top, total = state
@@ -230,9 +233,7 @@
         tops = top_ref[...].T
         top = jnp.max(tops, axis=0, keepdims=True)
         total = jnp.sum(acc_ref[...].T * jnp.exp(tops - top), axis=0, keepdims=True)
-        result = top + jnp.log(total)
-        for k in range(nz):
-            s_ref[k : k + 1, :] = result[:, k * each : (k + 1) * each]
+        store(top + jnp.log(total))
 
 
 def call(kernel, outs, scratch, flops, exps, *args, scalars=()):
@@ -251,19 +252,24 @@
     )(*args)
 
 
+def log_sum(parts):
+    top = jnp.max(parts, axis=0)
+    return top + jnp.log(jnp.sum(jnp.exp(parts - top), axis=0))
+
+
 def per_device(nz, ny, nw, source_latent, source_logw, target_latent, target_logw, target_potential):
     f32, bf16 = jnp.float32, jnp.bfloat16
     per = source_latent.shape[0]
     each = target_latent.shape[0]
     cols, half = ny * per, nz // 2 * each
     pairs = cols * half
-    place = lax.axis_index("blk") // nz
-    place_in = place.astype(jnp.int32).reshape(1)
+    place = lax.axis_index("blk")
+    my_y, my_z = place // nz, place % nz
     depth = FEATURES + EXTRA
-
-    def along_y(value, r):
-        perm = [(y * nz + z, (y ^ r) * nz + z) for y in range(ny) for z in range(nz)]
-        return lax.ppermute(value, "blk", perm)
+    y_groups = [[y * nz + z for y in range(ny)] for z in range(nz)]
+    quarters = [[g * (nz // 2) + z for z in range(nz // 2)] for g in range(2 * ny)]
+    nx = nw // 4
+    x_groups = [[(h * nx + x) * 2 + k for x in range(nx)] for h in range(2) for k in range(2)]
 
     def along_z(value, k):
         perm = [(y * nz + z, y * nz + (z ^ k)) for y in range(ny) for z in range(nz)]
@@ -271,6 +277,13 @@
 
     def along_wide(value, k):
         return lax.ppermute(value, "wide", [(w, w ^ k) for w in range(nw)])
+
+    def shared(value, axis, groups):
+        spread = jnp.broadcast_to(value[None], (len(groups[0]),) + value.shape)
+        return lax.all_to_all(spread, axis, 0, 0, axis_index_groups=groups, tiled=True)
+
+    def over_y(value):
+        return shared(value, "blk", y_groups)
 
     y, offset = call(
         prepare_kernel,
@@ -283,78 +296,78 @@
         target_potential.reshape(1, each),
     )
     x = source_latent.T
-    xs = [x] + [along_y(x, r) for r in range(1, ny)]
+    xs = over_y(x)
     bit = nz // 2
     while bit > 1:
         y = jnp.concatenate([y, along_z(y, bit)], axis=1)
         bit //= 2
-    *xs, y = lax.optimization_barrier((*xs, y))
+    xs, y = lax.optimization_barrier((xs, y))
     far = along_z(y, 1)
 
     def first(block, *more):
         last = len(more) > 0
         return call(
-            functools.partial(first_kernel, ny, last),
+            functools.partial(first_kernel, last),
             (
                 jax.ShapeDtypeStruct((half, DEPTH), bf16),
-                jax.ShapeDtypeStruct((2 * ny if last else ny, per), f32),
+                jax.ShapeDtypeStruct((ny + last, per), f32),
             ),
             [pltpu.VMEM((depth, cols), bf16), pltpu.VMEM((8, cols), f32)],
             2 * pairs * DEPTH,
             pairs,
             block,
-            *xs,
+            xs,
             *more,
-            scalars=(1 + ny,),
         )
 
     yt_near, total = first(y)
-    yt_far, total = first(far, place_in, total, source_logw.reshape(1, per))
-    bit = 1
-    while bit < ny:
-        other = along_y(total, bit)
-        row = lax.broadcasted_iota(jnp.int32, total.shape, 0)
-        total = jnp.where(row < ny, join(total, other), total + other)
-        bit *= 2
-    total, logw = total[:ny], total[ny:]
-    bit = 1
-    while bit < nw:
-        total = join(total, along_wide(total, bit))
-        bit *= 2
+    yt_far, total = first(far, total, source_logw.reshape(1, per))
+    got = over_y(total)
+    total, logw = log_sum(got[:, :ny]), got[:, ny]
+    total = log_sum(shared(total, "wide", x_groups))
+    total = join(total, along_wide(total, 1))
+    total = join(total, along_wide(total, nw // 2))
     c = logw - total
     sq = jnp.sum(jnp.square(x.astype(f32)), axis=0, keepdims=True)
-    mine = lax.dynamic_slice(total, (place, 0), (1, per))
+    mine = lax.dynamic_slice(total, (my_y, 0), (1, per))
     source_potential = -0.5 * (mine - sq)
 
-    def second(block):
+    count = nz // 2
+    width = count.bit_length() - 1
+    blocks = []
+    for h in range(2):
+        for k in range(count):
+            away = 2 * int(format(k, "b").zfill(width)[::-1], 2) + h
+            blocks.append((h, k, away))
+    place_in = (my_z % count).astype(jnp.int32).reshape(1)
+
+    def second(slots, near):
         return call(
-            functools.partial(second_kernel, ny),
-            jax.ShapeDtypeStruct((nz // 2, each), f32),
+            functools.partial(second_kernel, slots),
+            jax.ShapeDtypeStruct((count, each), f32),
             [
                 pltpu.VMEM((depth, cols), bf16),
+                pltpu.VMEM((half, DEPTH), bf16),
                 pltpu.VMEM((half, 128), f32),
                 pltpu.VMEM((half, 128), f32),
             ],
             2 * pairs * DEPTH,
             pairs,
-            block,
-            *xs,
             place_in,
+            near,
+            yt_far,
+            xs,
             c,
-            scalars=(1 + ny,),
+            scalars=(0,),
         )
 
-    away = second(yt_far)
-    yt_near, away = lax.optimization_barrier((yt_near, away))
-    other = along_z(away, 1)
-    sums = join(second(yt_near), other)
-    bit = 2
-    while bit < nz:
-        count = sums.shape[0] // 2
-        sums = join(sums[:count], along_z(sums[count:], bit))
-        bit *= 2
-    new_target_potential = -0.5 * (sums - offset)
-    return source_potential.reshape(per), new_target_potential.reshape(each)
+    sent = second(tuple((h, k, a - count) for h, k, a in blocks if a >= count), yt_near)
+    yt_near, sent = lax.optimization_barrier((yt_near, sent))
+    other = along_z(sent, count)
+    sums = join(second(tuple(b for b in blocks if b[2] < count), yt_near), other)
+    sums = lax.all_to_all(sums, "blk", 0, 0, axis_index_groups=quarters, tiled=True)
+    new_target_potential = -0.5 * (log_sum(sums) - offset[0])
+    return source_potential.reshape(per), new_target_potential
 
 
 def solution(mesh):

time: 183 us -> 170 us (0.929)
  waiting for transfers between devices: 37.1 us -> 15.3 us
  blocking collectives: 0 us -> 19.7 us
  starting transfers between devices: 61.3 us -> 47.7 us
  local copies, waits for them, and re-layouts: 1.46 us -> 3.43 us
    all_to_all x0 -> x2, blocking collectives: none -> 19.7 us  [shared(): lax.all_to_all(spread, axis, 0, 0, axis_index_groups=groups, tiled=True)]
    ppermute x5 -> x0, starting transfers between devices: 14.6 us -> none  [along_y(): return lax.ppermute(value, 'blk', perm)]
    ppermute x5 -> x0, waiting for transfers between devices: 14.5 us -> none  [along_y(): return lax.ppermute(value, 'blk', perm)]
    ppermute x4 -> x2, waiting for transfers between devices: 12.7 us -> 3.82 us  [along_wide(): return lax.ppermute(value, 'wide', [(w, w ^ k) for w in range(nw)])]
    all_to_all x0 -> x2, starting transfers between devices: none -> 8.83 us  [the longest x1 4.59 us: shared(): lax.all_to_all(spread, axis, 0, 0, axis_index_groups=groups, tiled=True)]
    ppermute x6 -> x4, starting transfers between devices: 28.7 us -> 23.7 us  [along_z(): return lax.ppermute(value, 'blk', perm)]
    all_to_all x0 -> x2, waiting for transfers between devices: none -> 4.96 us  [the longest x1 4.96 us: per_device(): lax.all_to_all(sums, 'blk', 0, 0, axis_index_groups=quarters, tiled=True)]
    ppermute x6 -> x4, waiting for transfers between devices: 9.89 us -> 6.49 us  [along_z(): return lax.ppermute(value, 'blk', perm)]
  transfers between devices with their start and end apart: 15 -> 8, of which waited for: 10 -> 5; matrix products, arithmetic and copies ran while one was open for 0% -> 0% of each run, Pallas kernels for 22% -> 24%
where the time goes in v2:
time: 170 us; the launch traced here: 168 us
  Pallas kernels  79.9 us (47%)
  starting transfers between devices  47.7 us (28%)
  blocking collectives  19.7 us (12%)
  waiting for transfers between devices  15.3 us (9%)
  local copies, waits for them, and re-layouts  3.43 us (2%)
    pallas_call x5, Pallas kernels, call(): pl.pallas_call(kernel, out_shape=outs, in_specs=[pl.BlockSpec(memory_spac...  79.9 us
    ppermute x4, starting transfers between devices, along_z(): return lax.ppermute(value, 'blk', perm)  23.7 us
    all_to_all x2, blocking collectives, shared(): lax.all_to_all(spread, axis, 0, 0, axis_index_groups=groups, tiled=True)  19.7 us
    ppermute x2, starting transfers between devices, along_wide(): return lax.ppermute(value, 'wide', [(w, w ^ k) for w in range(nw)])  15.2 us
    ppermute x4, waiting for transfers between devices, along_z(): return lax.ppermute(value, 'blk', perm)  6.49 us
    all_to_all x1, waiting for transfers between devices, per_device(): lax.all_to_all(sums, 'blk', 0, 0, axis_index_groups=quarters, tiled=True)  4.96 us
    all_to_all x1, starting transfers between devices, shared(): lax.all_to_all(spread, axis, 0, 0, axis_index_groups=groups, tiled=True)  4.59 us
    all_to_all x1, starting transfers between devices, per_device(): lax.all_to_all(sums, 'blk', 0, 0, axis_index_groups=quarters, tiled=True)  4.24 us
  transfers between devices with their start and end apart: 8, of which 5 were waited for; matrix products, arithmetic and copies ran while one was open for 0% of the time, Pallas kernels for 24%

profile of v2, /device:TPU:6, one launch (start us, length us, event | category | flops | bytes accessed | tf_op | source)
XLA Modules:
  0.0 168.5 jit_solution(9791953686734544374)
XLA Ops:
  0.6 2.1 %broadcast_in_dim.8 = bf16[4,64,2048]{2,1,0:T(8,128)(2,1)} broadcast(bf16[64,2048]{1,0:T(8,128)(2,1)} %bitcast.27), dimensions={1,2} | broadcast | bytes 1310720 | tf_op jit(solution)/shard_map/broadcast_in_dim | solution.py:282
  2.7 4.6 %all-to-all-start = ((bf16[4,64,2048]{2,1,0:T(8,128)(2,1)}), bf16[4,64,2048]{2,1,0:T(8,128)(2,1)S(1)}, u32[]{:S(2)}, u32[]{:S(2)}) async-start(bf16[4,64,2048]{2,1,0:T(8,128)(2,1)} %broadcast_in_dim.8), calls=%async_computation | async-start | bytes 2097152 | tf_op jit(solution)/shard_map/all_to_all | solution.py:283
  7.3 0.7 copy-done.1
  8.0 9.1 %collective-permute-start = (bf16[80,256]{1,0:T(8,128)(2,1)S(1)}, bf16[80,256]{1,0:T(8,128)(2,1)S(1)}, u32[]{:S(2)}, u32[]{:S(2)}) collective-permute-start(bf16[80,256]{1,0:T(8,128)(2,1)S(1)} %get-tuple-element.12), channel_id=1, source_target_pairs={{0,64},{16,80},{32,96},{48,112},{64,0},{80,16},{96,32},{112,48},{1... | collective-permute-start | bytes 122888 | tf_op jit(solution)/shard_map/ppermute | solution.py:276
  17.1 2.4 %collective-permute-done = bf16[80,256]{1,0:T(8,128)(2,1)S(1)} collective-permute-done((bf16[80,256]{1,0:T(8,128)(2,1)S(1)}, bf16[80,256]{1,0:T(8,128)(2,1)S(1)}, u32[]{:S(2)}, u32[]{:S(2)}) %collective-permute-start) | collective-permute-done | bytes 40992 | tf_op jit(solution)/shard_map/ppermute | solution.py:276
  19.5 5.2 %collective-permute-start.1 = (bf16[80,512]{1,0:T(8,128)(2,1)S(1)}, bf16[80,512]{1,0:T(8,128)(2,1)S(1)}, u32[]{:S(2)}, u32[]{:S(2)}) collective-permute-start(bf16[80,512]{1,0:T(8,128)(2,1)S(1)} %pad_maximum_fusion.1), channel_id=1, source_target_pairs={{0,32},{16,48},{32,0},{48,16},{64,96},{80,112},{96,64},{112,80},{1... | collective-permute-start | bytes 245768 | tf_op jit(solution)/shard_map/ppermute | solution.py:276
  24.7 4.1 %collective-permute-done.1 = bf16[80,512]{1,0:T(8,128)(2,1)S(1)} collective-permute-done((bf16[80,512]{1,0:T(8,128)(2,1)S(1)}, bf16[80,512]{1,0:T(8,128)(2,1)S(1)}, u32[]{:S(2)}, u32[]{:S(2)}) %collective-permute-start.1) | collective-permute-done | bytes 81952 | tf_op jit(solution)/shard_map/ppermute | solution.py:276
  28.8 2.1 %collective-permute-start.2 = (bf16[80,1024]{1,0:T(8,128)(2,1)S(1)}, bf16[80,1024]{1,0:T(8,128)(2,1)S(1)}, u32[]{:S(2)}, u32[]{:S(2)}) collective-permute-start(bf16[80,1024]{1,0:T(8,128)(2,1)S(1)} %pad_maximum_fusion.refs_0_), channel_id=1, source_target_pairs={{0,16},{16,0},{32,48},{48,32},{64,80},{80,64},{96,112},{112,96},{1... | collective-permute-start | bytes 491528 | tf_op jit(solution)/shard_map/ppermute | solution.py:276
  30.9 6.0 %shard_map.69 = (bf16[1024,128]{1,0:T(8,128)(2,1)S(1)}, f32[4,2048]{1,0:T(4,128)S(1)}) custom-call(bf16[80,1024]{1,0:T(8,128)(2,1)S(1)} %pad_maximum_fusion.refs_0_, bf16[4,64,2048]{2,1,0:T(8,128)(2,1)S(1)} %all-to-all-done.refs_1_.x_ref), custom_call_target="tpu_custom_call" | custom-call | flops 2147483648 | bytes 4194304 | tf_op jit(solution)/shard_map/pallas_call | solution.py:240
  36.9 6.0 %shard_map.70 = (bf16[1024,128]{1,0:T(8,128)(2,1)S(1)}, f32[5,2048]{1,0:T(8,128)S(1)}) custom-call(bf16[80,1024]{1,0:T(8,128)(2,1)S(1)} %collective-permute-done.2.refs_0_, bf16[4,64,2048]{2,1,0:T(8,128)(2,1)S(1)} %all-to-all-done.refs_1_.x_ref, f32[4,2048]{1,0:T(4,128)S(1)} %get-tuple-element.15.refs_2_, f32[1,2048]{1,0:T(1,128)S(1)} %bitcast.26), custom_call_target="tpu_custom_call" | custom-call | flops 2147483648 | bytes 4194304 | tf_op jit(solution)/shard_map/pallas_call | solution.py:240
  42.9 11.2 %all_to_all.27 = f32[4,5,2048]{2,1,0:T(8,128)S(1)} all-to-all(f32[4,5,2048]{2,1,0:T(8,128)S(1)} %broadcast_in_dim.9), channel_id=1, replica_groups={{0,128,256,384},{16,144,272,400},{32,160,288,416},{48,176,304,432},{64,..., dimensions={0} | all-to-all | bytes 327680 | tf_op jit(solution)/shard_map/all_to_all | solution.py:283
  54.3 8.5 %all_to_all.28 = f32[4,4,2048]{2,1,0:T(4,128)S(1)} all-to-all(f32[4,4,2048]{2,1,0:T(4,128)S(1)} %broadcast_in_dim.10), channel_id=1, replica_groups={{0,2,4,6},{1,3,5,7},{8,10,12,14},{9,11,13,15},{16,18,20,22},{17,19,21,2..., dimensions={0} | all-to-all | bytes 262144 | tf_op jit(solution)/shard_map/all_to_all | solution.py:283
  62.9 1.9 %collective-permute-start.3 = (f32[4,2048]{1,0:T(4,128)S(1)}, f32[4,2048]{1,0:T(4,128)S(1)}, u32[]{:S(2)}, u32[]{:S(2)}) collective-permute-start(f32[4,2048]{1,0:T(4,128)S(1)} %log_add_fusion.2), channel_id=1, source_target_pairs={{0,1},{1,0},{2,3},{3,2},{4,5},{5,4},{6,7},{7,6},{8,9},{9,8},{10,11... | collective-permute-start | bytes 98312 | tf_op jit(solution)/shard_map/ppermute | solution.py:279
  64.8 1.2 collective-permute-done.3
  66.1 13.2 %collective-permute-start.4 = (f32[4,2048]{1,0:T(4,128)S(1)}, f32[4,2048]{1,0:T(4,128)S(1)}, u32[]{:S(2)}, u32[]{:S(2)}) collective-permute-start(f32[4,2048]{1,0:T(4,128)S(1)} %log_add_fusion.1), channel_id=1, source_target_pairs={{0,8},{1,9},{2,10},{3,11},{4,12},{5,13},{6,14},{7,15},{8,0},{9,1},... | collective-permute-start | bytes 98312 | tf_op jit(solution)/shard_map/ppermute | solution.py:279
  79.5 2.7 %collective-permute-done.4 = f32[4,2048]{1,0:T(4,128)S(1)} collective-permute-done((f32[4,2048]{1,0:T(4,128)S(1)}, f32[4,2048]{1,0:T(4,128)S(1)}, u32[]{:S(2)}, u32[]{:S(2)}) %collective-permute-start.4) | collective-permute-done | bytes 32800 | tf_op jit(solution)/shard_map/ppermute | solution.py:279
  82.2 33.9 %shard_map.71 = f32[4,256]{1,0:T(4,128)S(1)} custom-call(s32[1]{0:T(128)} %bitcast.7.place_ref, bf16[1024,128]{1,0:T(8,128)(2,1)S(1)} %get-tuple-element.19.near_ref, bf16[1024,128]{1,0:T(8,128)(2,1)S(1)} %get-tuple-element.18.far_ref, bf16[4,64,2048]{2,1,0:T(8,128)(2,1)S(1)} %all-to-all-done.refs_1_.x_ref, f32[4,2048]{1,0:T(4,128)S(1)} %get-tuple-element.22.c_ref), custom_call_target="tpu_custom_call" | custom-call | flops 2147483648 | bytes 4194304 | tf_op jit(solution)/shard_map/pallas_call | solution.py:240
  116.1 7.3 %collective-permute-start.5 = (f32[4,256]{1,0:T(4,128)S(1)}, f32[4,256]{1,0:T(4,128)S(1)}, u32[]{:S(2)}, u32[]{:S(2)}) collective-permute-start(f32[4,256]{1,0:T(4,128)S(1)} %shard_map.71), channel_id=1, source_target_pairs={{0,64},{16,80},{32,96},{48,112},{64,0},{80,16},{96,32},{112,48},{1... | collective-permute-start | bytes 12296 | tf_op jit(solution)/shard_map/ppermute | solution.py:276
  123.4 33.9 %shard_map.72 = f32[4,256]{1,0:T(4,128)S(1)} custom-call(s32[1]{0:T(128)} %bitcast.7.place_ref, bf16[1024,128]{1,0:T(8,128)(2,1)S(1)} %get-tuple-element.19.near_ref, bf16[1024,128]{1,0:T(8,128)(2,1)S(1)} %get-tuple-element.18.far_ref, bf16[4,64,2048]{2,1,0:T(8,128)(2,1)S(1)} %all-to-all-done.refs_1_.x_ref, f32[4,2048]{1,0:T(4,128)S(1)} %get-tuple-element.22.c_ref), custom_call_target="tpu_custom_call" | custom-call | flops 2147483648 | bytes 4194304 | tf_op jit(solution)/shard_map/pallas_call | solution.py:240
  157.4 0.6 copy.10
  158.0 4.2 %all-to-all-start.3 = ((f32[4,1,256]{2,1,0:T(1,128)}), f32[4,1,256]{2,1,0:T(1,128)S(1)}, u32[]{:S(2)}, u32[]{:S(2)}) async-start(f32[4,1,256]{2,1,0:T(1,128)} %copy.10), calls=%async_computation.3 | async-start | bytes 8192 | tf_op jit(solution)/shard_map/all_to_all | solution.py:368
  162.3 0.6 subtract_multiply_fusion
  162.9 5.0 %all-to-all-done.3 = f32[4,1,256]{2,1,0:T(1,128)S(1)} async-done(((f32[4,1,256]{2,1,0:T(1,128)}), f32[4,1,256]{2,1,0:T(1,128)S(1)}, u32[]{:S(2)}, u32[]{:S(2)}) %all-to-all-start.3) | async-done | bytes 4128 | tf_op jit(solution)/shard_map/all_to_all | solution.py:368
  167.9 0.6 subtract_multiply_fusion.1
  (30 shorter events, 0.6 us)
Async XLA Ops:
  2.7 4.6 %copy-start = (bf16[256,64]{0,1:T(8,128)(2,1)S(1)}, bf16[256,64]{0,1:T(8,128)(2,1)}, u32[]{:S(2)}) copy-start(bf16[256,64]{0,1:T(8,128)(2,1)} %param.7) | copy-start | bytes 98308
  2.7 4.6 %copy-start.2 = (f32[256]{0:T(256)S(1)}, f32[256]{0:T(256)}, u32[]{:S(2)}) copy-start(f32[256]{0:T(256)} %param.9) | copy-start | bytes 3076
  2.7 26.1 %all-to-all-start = ((bf16[4,64,2048]{2,1,0:T(8,128)(2,1)}), bf16[4,64,2048]{2,1,0:T(8,128)(2,1)S(1)}, u32[]{:S(2)}, u32[]{:S(2)}) async-start(bf16[4,64,2048]{2,1,0:T(8,128)(2,1)} %broadcast_in_dim.8), calls=%async_computation | async-start | bytes 2097152 | tf_op jit(solution)/shard_map/all_to_all | solution.py:283
  7.3 0.7 copy-start.1
  8.0 11.5 %collective-permute-start = (bf16[80,256]{1,0:T(8,128)(2,1)S(1)}, bf16[80,256]{1,0:T(8,128)(2,1)S(1)}, u32[]{:S(2)}, u32[]{:S(2)}) collective-permute-start(bf16[80,256]{1,0:T(8,128)(2,1)S(1)} %get-tuple-element.12), channel_id=1, source_target_pairs={{0,64},{16,80},{32,96},{48,112},{64,0},{80,16},{96,32},{112,48},{1... | collective-permute-start | bytes 122888 | tf_op jit(solution)/shard_map/ppermute | solution.py:276
  19.5 9.3 %collective-permute-start.1 = (bf16[80,512]{1,0:T(8,128)(2,1)S(1)}, bf16[80,512]{1,0:T(8,128)(2,1)S(1)}, u32[]{:S(2)}, u32[]{:S(2)}) collective-permute-start(bf16[80,512]{1,0:T(8,128)(2,1)S(1)} %pad_maximum_fusion.1), channel_id=1, source_target_pairs={{0,32},{16,48},{32,0},{48,16},{64,96},{80,112},{96,64},{112,80},{1... | collective-permute-start | bytes 245768 | tf_op jit(solution)/shard_map/ppermute | solution.py:276
  28.8 8.1 %copy-start.3 = (f32[2048]{0:T(1024)S(1)}, f32[2048]{0:T(1024)}, u32[]{:S(2)}) copy-start(f32[2048]{0:T(1024)} %param.6) | copy-start | bytes 24580
  28.8 8.1 %collective-permute-start.2 = (bf16[80,1024]{1,0:T(8,128)(2,1)S(1)}, bf16[80,1024]{1,0:T(8,128)(2,1)S(1)}, u32[]{:S(2)}, u32[]{:S(2)}) collective-permute-start(bf16[80,1024]{1,0:T(8,128)(2,1)S(1)} %pad_maximum_fusion.refs_0_), channel_id=1, source_target_pairs={{0,16},{16,0},{32,48},{48,32},{64,80},{80,64},{96,112},{112,96},{1... | collective-permute-start | bytes 491528 | tf_op jit(solution)/shard_map/ppermute | solution.py:276
  62.8 16.5 %copy-start.4 = (bf16[2048,64]{0,1:T(8,128)(2,1)S(1)}, bf16[2048,64]{0,1:T(8,128)(2,1)}, u32[]{:S(2)}) copy-start(bf16[2048,64]{0,1:T(8,128)(2,1)} %param.5) | copy-start | bytes 786436
  62.9 3.1 %collective-permute-start.3 = (f32[4,2048]{1,0:T(4,128)S(1)}, f32[4,2048]{1,0:T(4,128)S(1)}, u32[]{:S(2)}, u32[]{:S(2)}) collective-permute-start(f32[4,2048]{1,0:T(4,128)S(1)} %log_add_fusion.2), channel_id=1, source_target_pairs={{0,1},{1,0},{2,3},{3,2},{4,5},{5,4},{6,7},{7,6},{8,9},{9,8},{10,11... | collective-permute-start | bytes 98312 | tf_op jit(solution)/shard_map/ppermute | solution.py:279
  66.1 16.1 %collective-permute-start.4 = (f32[4,2048]{1,0:T(4,128)S(1)}, f32[4,2048]{1,0:T(4,128)S(1)}, u32[]{:S(2)}, u32[]{:S(2)}) collective-permute-start(f32[4,2048]{1,0:T(4,128)S(1)} %log_add_fusion.1), channel_id=1, source_target_pairs={{0,8},{1,9},{2,10},{3,11},{4,12},{5,13},{6,14},{7,15},{8,0},{9,1},... | collective-permute-start | bytes 98312 | tf_op jit(solution)/shard_map/ppermute | solution.py:279
  116.1 41.3 %collective-permute-start.5 = (f32[4,256]{1,0:T(4,128)S(1)}, f32[4,256]{1,0:T(4,128)S(1)}, u32[]{:S(2)}, u32[]{:S(2)}) collective-permute-start(f32[4,256]{1,0:T(4,128)S(1)} %shard_map.71), channel_id=1, source_target_pairs={{0,64},{16,80},{32,96},{48,112},{64,0},{80,16},{96,32},{112,48},{1... | collective-permute-start | bytes 12296 | tf_op jit(solution)/shard_map/ppermute | solution.py:276
  158.0 9.8 %all-to-all-start.3 = ((f32[4,1,256]{2,1,0:T(1,128)}), f32[4,1,256]{2,1,0:T(1,128)S(1)}, u32[]{:S(2)}, u32[]{:S(2)}) async-start(f32[4,1,256]{2,1,0:T(1,128)} %copy.10), calls=%async_computation.3 | async-start | bytes 8192 | tf_op jit(solution)/shard_map/all_to_all | solution.py:368

commit v3 on v2

--- a/solution.py
+++ b/solution.py
@@ -11,8 +11,8 @@
 FEATURES = 64
 EXTRA = 16
 DEPTH = 128
-LANES = 1024
-STEP = 256
+ROWS = 512
+LANES = 256
 LOW = 2.0**-60
 HIGH = 2.0**120
 
@@ -50,16 +50,9 @@
     offset_ref[...] = offset
 
 
-def lay_sources(x_ref, xs_ref):
-    per = x_ref.shape[2]
-    for r in range(x_ref.shape[0]):
-        xs_ref[0:FEATURES, r * per : (r + 1) * per] = x_ref[r]
-
-
-def weights_at(xs_ref, at):
-    part = xs_ref[:, at]
-    rest = jnp.zeros((DEPTH - part.shape[0], part.shape[1]), part.dtype)
-    return jnp.concatenate([part, rest], axis=0)
+def weights_of(features, extra):
+    rest = jnp.zeros((DEPTH - FEATURES - EXTRA, features.shape[1]), features.dtype)
+    return jnp.concatenate([features, extra, rest], axis=0)
 
 
 def product(a, b):
@@ -80,13 +73,12 @@
     y_ref, x_ref, refs = refs[0], refs[1], refs[2:]
     if last:
         before_ref, logw_ref, refs = refs[0], refs[1], refs[2:]
-    yt_ref, l_ref, xs_ref, sums_ref = refs
+    yt_ref, l_ref, sums_ref = refs
     rows = yt_ref.shape[0]
     ny, _, per = x_ref.shape
-    cols = ny * per
-    wide = min(LANES, cols)
-    row_step = min(STEP, rows)
-    col_step = min(STEP, wide)
+    row_step = min(ROWS, rows)
+    col_step = min(LANES, per)
+    together = 2
 
     extra = y_ref[FEATURES : FEATURES + EXTRA, :].astype(jnp.float32)
     bias = extra[0:1, :] + extra[1:2, :] + extra[2:3, :]
@@ -100,9 +92,8 @@
             axis=0,
         )
         yt_ref[k : k + row_step, :] = block.T.astype(jnp.bfloat16)
-    lay_sources(x_ref, xs_ref)
-    xs_ref[FEATURES : FEATURES + EXTRA, :] = extra_block(
-        ones_of(cols), three_parts(jnp.broadcast_to(-shift, (1, cols)))
+    extra = extra_block(
+        ones_of(col_step), three_parts(jnp.broadcast_to(-shift, (1, col_step)))
     ).astype(jnp.bfloat16)
 
     def store(row, value):
@@ -114,64 +105,69 @@
         l_ref[ny : ny + 1, :] = logw_ref[...]
 
     def main(g, carry):
-        for t in range(wide // col_step):
-            at = pl.ds(pl.multiple_of(g * wide + t * col_step, col_step), col_step)
-            weights = weights_at(xs_ref, at)
-            total = jnp.zeros((8, col_step), jnp.float32)
-            for j in range(rows // row_step):
-                score = product(yt_ref[j * row_step : (j + 1) * row_step, :], weights)
-                total = total + folded(jnp.exp(score), jnp.sum)
-            sums_ref[:, at] = total
+        for s in range(together):
+            r = g * together + s
+            for t in range(0, per, col_step):
+                weights = weights_of(x_ref[r, :, t : t + col_step], extra)
+                total = jnp.zeros((8, col_step), jnp.float32)
+                for j in range(0, rows, row_step):
+                    score = product(yt_ref[j : j + row_step, :], weights)
+                    total = total + folded(jnp.exp(score), jnp.sum)
+                sums_ref[r, :, t : t + col_step] = total
         return carry
 
-    lax.fori_loop(0, cols // wide, main, 0)
-    total = jnp.sum(sums_ref[...], axis=0, keepdims=True)
+    lax.fori_loop(0, ny // together, main, 0)
+    total = jnp.sum(sums_ref[...], axis=1)
     result = shift + jnp.log(total)
     for r in range(ny):
-        store(r, result[:, r * per : (r + 1) * per])
+        store(r, result[r : r + 1, :])
 
     @pl.when(jnp.logical_not((jnp.min(total) > LOW) & (jnp.max(total) < HIGH)))
     def _():
         def again(g, carry):
             at = pl.ds(pl.multiple_of(g * col_step, col_step), col_step)
-            weights = weights_at(xs_ref, at)
-
-            def advance(j, state):
-                top, total = state
-                here = pl.ds(pl.multiple_of(j * row_step, row_step), row_step)
-                score = product(yt_ref[here, :], weights)
-                new = jnp.maximum(top, jnp.max(score, axis=0, keepdims=True))
-                total = total * jnp.exp(top - new) + jnp.sum(
-                    jnp.exp(score - new), axis=0, keepdims=True
+            for r in range(ny):
+                weights = weights_of(x_ref[r, :, at], extra)
+
+                def advance(j, state):
+                    top, total = state
+                    here = pl.ds(pl.multiple_of(j * row_step, row_step), row_step)
+                    score = product(yt_ref[here, :], weights)
+                    new = jnp.maximum(top, jnp.max(score, axis=0, keepdims=True))
+                    total = total * jnp.exp(top - new) + jnp.sum(
+                        jnp.exp(score - new), axis=0, keepdims=True
+                    )
+                    return new, total
+
+                start = (
+                    jnp.full((1, col_step), -1e30, jnp.float32),
+                    jnp.zeros((1, col_step), jnp.float32),
                 )
-                return new, total
-
-            start = (
-                jnp.full((1, col_step), -1e30, jnp.float32),
-                jnp.zeros((1, col_step), jnp.float32),
-            )
-            top, total = lax.fori_loop(0, rows // row_step, advance, start)
-            sums_ref[0:1, at] = shift + top + jnp.log(total)
+                top, total = lax.fori_loop(0, rows // row_step, advance, start)
+                sums_ref[r, 0:1, at] = shift + top + jnp.log(total)
             return carry
 
-        lax.fori_loop(0, cols // col_step, again, 0)
+        lax.fori_loop(0, per // col_step, again, 0)
         for r in range(ny):
-            store(r, sums_ref[0:1, r * per : (r + 1) * per])
-
-
-def second_kernel(slots, place_ref, near_ref, far_ref, x_ref, c_ref, s_ref, xs_ref, left_ref, acc_ref, top_ref):
+            store(r, sums_ref[r, 0:1, :])
+
+
+def second_kernel(
+    slots, place_ref, near_ref, far_ref, x_ref, c_ref, s_ref, extra_ref, left_ref, acc_ref, top_ref
+):
     nz, each = s_ref.shape
     rows = nz * each
     ny, _, per = x_ref.shape
-    cols = ny * per
-    row_step = each
-    col_step = min(STEP, cols)
-
-    lay_sources(x_ref, xs_ref)
+    row_step = min(ROWS, rows)
+    col_step = min(LANES, per)
+
     for r in range(ny):
-        xs_ref[FEATURES : FEATURES + EXTRA, r * per : (r + 1) * per] = extra_block(
+        extra_ref[r] = extra_block(
             ones_of(per), three_parts(c_ref[r : r + 1, :])
         ).astype(jnp.bfloat16)
+    for g, (half, k, _) in enumerate(slots):
+        ref = far_ref if half else near_ref
+        left_ref[g * each : (g + 1) * each, :] = ref[k * each : (k + 1) * each, :]
 
     def lanes_folded(value, combine):
         out = value[:, 0:128]
@@ -179,20 +175,18 @@
             out = combine(out, value[:, k * 128 : (k + 1) * 128])
         return out
 
-    for g, (half, k, _) in enumerate(slots):
-        ref = far_ref if half else near_ref
-        left_ref[g * each : (g + 1) * each, :] = ref[k * each : (k + 1) * each, :]
-
     def main(g, carry):
         here = pl.ds(pl.multiple_of(g * row_step, row_step), row_step)
         left = left_ref[here, :]
-        total = jnp.zeros((row_step, 128), jnp.float32)
-        for t in range(cols // col_step):
-            score = product(
-                left, weights_at(xs_ref, slice(t * col_step, (t + 1) * col_step))
-            )
-            total = total + lanes_folded(jnp.exp(score), jnp.add)
-        acc_ref[here, :] = total
+        for r in range(ny):
+            for t in range(0, per, col_step):
+                at = slice(t, t + col_step)
+                score = product(left, weights_of(x_ref[r, :, at], extra_ref[r, :, at]))
+                part = lanes_folded(jnp.exp(score), jnp.add)
+                if r == 0 and t == 0:
+                    acc_ref[here, :] = part
+                else:
+                    acc_ref[here, :] = acc_ref[here, :] + part
         return carry
 
     lax.fori_loop(0, rows // row_step, main, 0)
@@ -207,42 +201,42 @@
     @pl.when(jnp.logical_not((jnp.min(total) > LOW) & (jnp.max(total) < HIGH)))
     def _():
         def again(g, carry):
-            here = pl.ds(pl.multiple_of(g * row_step, row_step), row_step)
+            here = pl.ds(pl.multiple_of(g * each, each), each)
             left = left_ref[here, :]
-
-            def advance(t, state):
-                top, total = state
-                at = pl.ds(pl.multiple_of(t * col_step, col_step), col_step)
-                score = product(left, weights_at(xs_ref, at))
-                new = jnp.maximum(top, lanes_folded(score, jnp.maximum))
-                total = total * jnp.exp(top - new)
-                for k in range(col_step // 128):
-                    total = total + jnp.exp(score[:, k * 128 : (k + 1) * 128] - new)
-                return new, total
-
-            start = (
-                jnp.full((row_step, 128), -1e30, jnp.float32),
-                jnp.zeros((row_step, 128), jnp.float32),
+            state = (
+                jnp.full((each, 128), -1e30, jnp.float32),
+                jnp.zeros((each, 128), jnp.float32),
             )
-            top, total = lax.fori_loop(0, cols // col_step, advance, start)
-            top_ref[here, :] = top
-            acc_ref[here, :] = total
+            for r in range(ny):
+
+                def advance(t, state):
+                    top, total = state
+                    at = pl.ds(pl.multiple_of(t * col_step, col_step), col_step)
+                    score = product(left, weights_of(x_ref[r, :, at], extra_ref[r, :, at]))
+                    new = jnp.maximum(top, lanes_folded(score, jnp.maximum))
+                    total = total * jnp.exp(top - new)
+                    for k in range(col_step // 128):
+                        total = total + jnp.exp(score[:, k * 128 : (k + 1) * 128] - new)
+                    return new, total
+
+                state = lax.fori_loop(0, per // col_step, advance, state)
+            top_ref[here, :] = state[0]
+            acc_ref[here, :] = state[1]
             return carry
 
-        lax.fori_loop(0, rows // row_step, again, 0)
+        lax.fori_loop(0, rows // each, again, 0)
         tops = top_ref[...].T
         top = jnp.max(tops, axis=0, keepdims=True)
         total = jnp.sum(acc_ref[...].T * jnp.exp(tops - top), axis=0, keepdims=True)
         store(top + jnp.log(total))
 
 
-def call(kernel, outs, scratch, flops, exps, *args, scalars=()):
+def call(kernel, outs, scratch, flops, exps, *args, spaces=None):
     return pl.pallas_call(
         kernel,
         out_shape=outs,
         in_specs=[
-            pl.BlockSpec(memory_space=pltpu.SMEM if k in scalars else pltpu.VMEM)
-            for k in range(len(args))
+            pl.BlockSpec(memory_space=space) for space in spaces or [pltpu.VMEM] * len(args)
         ],
         scratch_shapes=scratch,
         compiler_params=pltpu.CompilerParams(vmem_limit_bytes=40 * 2**20),
@@ -282,9 +276,6 @@
         spread = jnp.broadcast_to(value[None], (len(groups[0]),) + value.shape)
         return lax.all_to_all(spread, axis, 0, 0, axis_index_groups=groups, tiled=True)
 
-    def over_y(value):
-        return shared(value, "blk", y_groups)
-
     y, offset = call(
         prepare_kernel,
         (jax.ShapeDtypeStruct((depth, each), bf16), jax.ShapeDtypeStruct((1, each), f32)),
@@ -296,7 +287,7 @@
         target_potential.reshape(1, each),
     )
     x = source_latent.T
-    xs = over_y(x)
+    xs = shared(x, "blk", y_groups)
     bit = nz // 2
     while bit > 1:
         y = jnp.concatenate([y, along_z(y, bit)], axis=1)
@@ -312,7 +303,7 @@
                 jax.ShapeDtypeStruct((half, DEPTH), bf16),
                 jax.ShapeDtypeStruct((ny + last, per), f32),
             ),
-            [pltpu.VMEM((depth, cols), bf16), pltpu.VMEM((8, cols), f32)],
+            [pltpu.VMEM((ny, 8, per), f32)],
             2 * pairs * DEPTH,
             pairs,
             block,
@@ -322,7 +313,7 @@
 
     yt_near, total = first(y)
     yt_far, total = first(far, total, source_logw.reshape(1, per))
-    got = over_y(total)
+    got = shared(total, "blk", y_groups)
     total, logw = log_sum(got[:, :ny]), got[:, ny]
     total = log_sum(shared(total, "wide", x_groups))
     total = join(total, along_wide(total, 1))
@@ -346,7 +337,7 @@
             functools.partial(second_kernel, slots),
             jax.ShapeDtypeStruct((count, each), f32),
             [
-                pltpu.VMEM((depth, cols), bf16),
+                pltpu.VMEM((ny, EXTRA, per), bf16),
                 pltpu.VMEM((half, DEPTH), bf16),
                 pltpu.VMEM((half, 128), f32),
                 pltpu.VMEM((half, 128), f32),
@@ -358,7 +349,7 @@
             yt_far,
             xs,
             c,
-            scalars=(0,),
+            spaces=[pltpu.SMEM] + [pltpu.VMEM] * 4,
         )
 
     sent = second(tuple((h, k, a - count) for h, k, a in blocks if a >= count), yt_near)

time: 170 us -> 168 us (0.988)
  Pallas kernels: 79.9 us -> 77.4 us
    pallas_call x5, Pallas kernels: 79.9 us -> 77.4 us  [call(): pl.pallas_call(kernel, out_shape=outs, in_specs=[pl.BlockSpec(memory_spac...]
  transfers between devices with their start and end apart: 8 -> 8, of which waited for: 5 -> 6; matrix products, arithmetic and copies ran while one was open for 0% -> 0% of each run, Pallas kernels for 24% -> 23%
where the time goes in v3:
time: 168 us; the launch traced here: 166 us
  Pallas kernels  77.4 us (46%)
  starting transfers between devices  48.2 us (29%)
  blocking collectives  19.6 us (12%)
  waiting for transfers between devices  15.2 us (9%)
  local copies, waits for them, and re-layouts  3.43 us (2%)
    pallas_call x5, Pallas kernels, call(): pl.pallas_call(kernel, out_shape=outs, in_specs=[pl.BlockSpec(memory_spac...  77.4 us
    ppermute x4, starting transfers between devices, along_z(): return lax.ppermute(value, 'blk', perm)  23.9 us
    all_to_all x2, blocking collectives, shared(): lax.all_to_all(spread, axis, 0, 0, axis_index_groups=groups, tiled=True)  19.6 us
    ppermute x2, starting transfers between devices, along_wide(): return lax.ppermute(value, 'wide', [(w, w ^ k) for w in range(nw)])  15.5 us
    ppermute x4, waiting for transfers between devices, along_z(): return lax.ppermute(value, 'blk', perm)  6.59 us
    all_to_all x1, waiting for transfers between devices, per_device(): lax.all_to_all(sums, 'blk', 0, 0, axis_index_groups=quarters, tiled=True)  4.96 us
    all_to_all x1, starting transfers between devices, shared(): lax.all_to_all(spread, axis, 0, 0, axis_index_groups=groups, tiled=True)  4.59 us
    all_to_all x1, starting transfers between devices, per_device(): lax.all_to_all(sums, 'blk', 0, 0, axis_index_groups=quarters, tiled=True)  4.25 us
  transfers between devices with their start and end apart: 8, of which 6 were waited for; matrix products, arithmetic and copies ran while one was open for 0% of the time, Pallas kernels for 23%

profile of v3, /device:TPU:6, one launch (start us, length us, event | category | flops | bytes accessed | tf_op | source)
XLA Modules:
  0.0 166.3 jit_solution(8693397732932276488)
XLA Ops:
  0.6 2.1 %broadcast_in_dim.8 = bf16[4,64,2048]{2,1,0:T(8,128)(2,1)} broadcast(bf16[64,2048]{1,0:T(8,128)(2,1)} %bitcast.27), dimensions={1,2} | broadcast | bytes 1310720 | tf_op jit(solution)/shard_map/broadcast_in_dim | solution.py:276
  2.7 4.6 %all-to-all-start = ((bf16[4,64,2048]{2,1,0:T(8,128)(2,1)}), bf16[4,64,2048]{2,1,0:T(8,128)(2,1)S(1)}, u32[]{:S(2)}, u32[]{:S(2)}) async-start(bf16[4,64,2048]{2,1,0:T(8,128)(2,1)} %broadcast_in_dim.8), calls=%async_computation | async-start | bytes 2097152 | tf_op jit(solution)/shard_map/all_to_all | solution.py:277
  7.3 0.7 copy-done.1
  8.0 9.1 %collective-permute-start = (bf16[80,256]{1,0:T(8,128)(2,1)S(1)}, bf16[80,256]{1,0:T(8,128)(2,1)S(1)}, u32[]{:S(2)}, u32[]{:S(2)}) collective-permute-start(bf16[80,256]{1,0:T(8,128)(2,1)S(1)} %get-tuple-element.12), channel_id=1, source_target_pairs={{0,64},{16,80},{32,96},{48,112},{64,0},{80,16},{96,32},{112,48},{1... | collective-permute-start | bytes 122888 | tf_op jit(solution)/shard_map/ppermute | solution.py:270
  17.1 2.4 %collective-permute-done = bf16[80,256]{1,0:T(8,128)(2,1)S(1)} collective-permute-done((bf16[80,256]{1,0:T(8,128)(2,1)S(1)}, bf16[80,256]{1,0:T(8,128)(2,1)S(1)}, u32[]{:S(2)}, u32[]{:S(2)}) %collective-permute-start) | collective-permute-done | bytes 40992 | tf_op jit(solution)/shard_map/ppermute | solution.py:270
  19.5 5.2 %collective-permute-start.1 = (bf16[80,512]{1,0:T(8,128)(2,1)S(1)}, bf16[80,512]{1,0:T(8,128)(2,1)S(1)}, u32[]{:S(2)}, u32[]{:S(2)}) collective-permute-start(bf16[80,512]{1,0:T(8,128)(2,1)S(1)} %pad_maximum_fusion.1), channel_id=1, source_target_pairs={{0,32},{16,48},{32,0},{48,16},{64,96},{80,112},{96,64},{112,80},{1... | collective-permute-start | bytes 245768 | tf_op jit(solution)/shard_map/ppermute | solution.py:270
  24.7 4.1 %collective-permute-done.1 = bf16[80,512]{1,0:T(8,128)(2,1)S(1)} collective-permute-done((bf16[80,512]{1,0:T(8,128)(2,1)S(1)}, bf16[80,512]{1,0:T(8,128)(2,1)S(1)}, u32[]{:S(2)}, u32[]{:S(2)}) %collective-permute-start.1) | collective-permute-done | bytes 81952 | tf_op jit(solution)/shard_map/ppermute | solution.py:270
  28.8 2.1 %collective-permute-start.2 = (bf16[80,1024]{1,0:T(8,128)(2,1)S(1)}, bf16[80,1024]{1,0:T(8,128)(2,1)S(1)}, u32[]{:S(2)}, u32[]{:S(2)}) collective-permute-start(bf16[80,1024]{1,0:T(8,128)(2,1)S(1)} %pad_maximum_fusion.refs_0_), channel_id=1, source_target_pairs={{0,16},{16,0},{32,48},{48,32},{64,80},{80,64},{96,112},{112,96},{1... | collective-permute-start | bytes 491528 | tf_op jit(solution)/shard_map/ppermute | solution.py:270
  30.9 5.0 %shard_map.69 = (bf16[1024,128]{1,0:T(8,128)(2,1)S(1)}, f32[4,2048]{1,0:T(4,128)S(1)}) custom-call(bf16[80,1024]{1,0:T(8,128)(2,1)S(1)} %pad_maximum_fusion.refs_0_, bf16[4,64,2048]{2,1,0:T(8,128)(2,1)S(1)} %all-to-all-done.refs_1_.x_ref), custom_call_target="tpu_custom_call" | custom-call | flops 2147483648 | bytes 4194304 | tf_op jit(solution)/shard_map/pallas_call | solution.py:235
  36.0 5.0 %shard_map.70 = (bf16[1024,128]{1,0:T(8,128)(2,1)S(1)}, f32[5,2048]{1,0:T(8,128)S(1)}) custom-call(bf16[80,1024]{1,0:T(8,128)(2,1)S(1)} %collective-permute-done.2.refs_0_, bf16[4,64,2048]{2,1,0:T(8,128)(2,1)S(1)} %all-to-all-done.refs_1_.x_ref, f32[4,2048]{1,0:T(4,128)S(1)} %get-tuple-element.15.refs_2_, f32[1,2048]{1,0:T(1,128)S(1)} %bitcast.26), custom_call_target="tpu_custom_call" | custom-call | flops 2147483648 | bytes 4194304 | tf_op jit(solution)/shard_map/pallas_call | solution.py:235
  41.1 11.1 %all_to_all.27 = f32[4,5,2048]{2,1,0:T(8,128)S(1)} all-to-all(f32[4,5,2048]{2,1,0:T(8,128)S(1)} %broadcast_in_dim.9), channel_id=1, replica_groups={{0,128,256,384},{16,144,272,400},{32,160,288,416},{48,176,304,432},{64,..., dimensions={0} | all-to-all | bytes 327680 | tf_op jit(solution)/shard_map/all_to_all | solution.py:277
  52.3 8.5 %all_to_all.28 = f32[4,4,2048]{2,1,0:T(4,128)S(1)} all-to-all(f32[4,4,2048]{2,1,0:T(4,128)S(1)} %broadcast_in_dim.10), channel_id=1, replica_groups={{0,2,4,6},{1,3,5,7},{8,10,12,14},{9,11,13,15},{16,18,20,22},{17,19,21,2..., dimensions={0} | all-to-all | bytes 262144 | tf_op jit(solution)/shard_map/all_to_all | solution.py:277
  60.9 1.9 %collective-permute-start.3 = (f32[4,2048]{1,0:T(4,128)S(1)}, f32[4,2048]{1,0:T(4,128)S(1)}, u32[]{:S(2)}, u32[]{:S(2)}) collective-permute-start(f32[4,2048]{1,0:T(4,128)S(1)} %log_add_fusion.2), channel_id=1, source_target_pairs={{0,1},{1,0},{2,3},{3,2},{4,5},{5,4},{6,7},{7,6},{8,9},{9,8},{10,11... | collective-permute-start | bytes 98312 | tf_op jit(solution)/shard_map/ppermute | solution.py:273
  62.9 1.2 collective-permute-done.3
  64.1 13.6 %collective-permute-start.4 = (f32[4,2048]{1,0:T(4,128)S(1)}, f32[4,2048]{1,0:T(4,128)S(1)}, u32[]{:S(2)}, u32[]{:S(2)}) collective-permute-start(f32[4,2048]{1,0:T(4,128)S(1)} %log_add_fusion.1), channel_id=1, source_target_pairs={{0,8},{1,9},{2,10},{3,11},{4,12},{5,13},{6,14},{7,15},{8,0},{9,1},... | collective-permute-start | bytes 98312 | tf_op jit(solution)/shard_map/ppermute | solution.py:273
  77.8 2.5 %collective-permute-done.4 = f32[4,2048]{1,0:T(4,128)S(1)} collective-permute-done((f32[4,2048]{1,0:T(4,128)S(1)}, f32[4,2048]{1,0:T(4,128)S(1)}, u32[]{:S(2)}, u32[]{:S(2)}) %collective-permute-start.4) | collective-permute-done | bytes 32800 | tf_op jit(solution)/shard_map/ppermute | solution.py:273
  80.3 33.7 %shard_map.71 = f32[4,256]{1,0:T(4,128)S(1)} custom-call(s32[1]{0:T(128)} %bitcast.7.place_ref, bf16[1024,128]{1,0:T(8,128)(2,1)S(1)} %get-tuple-element.19.near_ref, bf16[1024,128]{1,0:T(8,128)(2,1)S(1)} %get-tuple-element.18.far_ref, bf16[4,64,2048]{2,1,0:T(8,128)(2,1)S(1)} %all-to-all-done.refs_1_.x_ref, f32[4,2048]{1,0:T(4,128)S(1)} %get-tuple-element.22.c_ref), custom_call_target="tpu_custom_call" | custom-call | flops 2147483648 | bytes 4194304 | tf_op jit(solution)/shard_map/pallas_call | solution.py:235
  114.0 7.5 %collective-permute-start.5 = (f32[4,256]{1,0:T(4,128)S(1)}, f32[4,256]{1,0:T(4,128)S(1)}, u32[]{:S(2)}, u32[]{:S(2)}) collective-permute-start(f32[4,256]{1,0:T(4,128)S(1)} %shard_map.71), channel_id=1, source_target_pairs={{0,64},{16,80},{32,96},{48,112},{64,0},{80,16},{96,32},{112,48},{1... | collective-permute-start | bytes 12296 | tf_op jit(solution)/shard_map/ppermute | solution.py:270
  121.5 33.7 %shard_map.72 = f32[4,256]{1,0:T(4,128)S(1)} custom-call(s32[1]{0:T(128)} %bitcast.7.place_ref, bf16[1024,128]{1,0:T(8,128)(2,1)S(1)} %get-tuple-element.19.near_ref, bf16[1024,128]{1,0:T(8,128)(2,1)S(1)} %get-tuple-element.18.far_ref, bf16[4,64,2048]{2,1,0:T(8,128)(2,1)S(1)} %all-to-all-done.refs_1_.x_ref, f32[4,2048]{1,0:T(4,128)S(1)} %get-tuple-element.22.c_ref), custom_call_target="tpu_custom_call" | custom-call | flops 2147483648 | bytes 4194304 | tf_op jit(solution)/shard_map/pallas_call | solution.py:235
  155.2 0.6 copy.10
  155.8 4.2 %all-to-all-start.3 = ((f32[4,1,256]{2,1,0:T(1,128)}), f32[4,1,256]{2,1,0:T(1,128)S(1)}, u32[]{:S(2)}, u32[]{:S(2)}) async-start(f32[4,1,256]{2,1,0:T(1,128)} %copy.10), calls=%async_computation.3 | async-start | bytes 8192 | tf_op jit(solution)/shard_map/all_to_all | solution.py:359
  160.1 0.6 subtract_multiply_fusion
  160.7 5.0 %all-to-all-done.3 = f32[4,1,256]{2,1,0:T(1,128)S(1)} async-done(((f32[4,1,256]{2,1,0:T(1,128)}), f32[4,1,256]{2,1,0:T(1,128)S(1)}, u32[]{:S(2)}, u32[]{:S(2)}) %all-to-all-start.3) | async-done | bytes 4128 | tf_op jit(solution)/shard_map/all_to_all | solution.py:359
  165.7 0.6 subtract_multiply_fusion.1
  (30 shorter events, 0.7 us)
Async XLA Ops:
  2.7 4.6 %copy-start = (bf16[256,64]{0,1:T(8,128)(2,1)S(1)}, bf16[256,64]{0,1:T(8,128)(2,1)}, u32[]{:S(2)}) copy-start(bf16[256,64]{0,1:T(8,128)(2,1)} %param.7) | copy-start | bytes 98308
  2.7 4.6 %copy-start.2 = (f32[256]{0:T(256)S(1)}, f32[256]{0:T(256)}, u32[]{:S(2)}) copy-start(f32[256]{0:T(256)} %param.9) | copy-start | bytes 3076
  2.7 26.1 %all-to-all-start = ((bf16[4,64,2048]{2,1,0:T(8,128)(2,1)}), bf16[4,64,2048]{2,1,0:T(8,128)(2,1)S(1)}, u32[]{:S(2)}, u32[]{:S(2)}) async-start(bf16[4,64,2048]{2,1,0:T(8,128)(2,1)} %broadcast_in_dim.8), calls=%async_computation | async-start | bytes 2097152 | tf_op jit(solution)/shard_map/all_to_all | solution.py:277
  7.3 0.7 copy-start.1
  8.0 11.5 %collective-permute-start = (bf16[80,256]{1,0:T(8,128)(2,1)S(1)}, bf16[80,256]{1,0:T(8,128)(2,1)S(1)}, u32[]{:S(2)}, u32[]{:S(2)}) collective-permute-start(bf16[80,256]{1,0:T(8,128)(2,1)S(1)} %get-tuple-element.12), channel_id=1, source_target_pairs={{0,64},{16,80},{32,96},{48,112},{64,0},{80,16},{96,32},{112,48},{1... | collective-permute-start | bytes 122888 | tf_op jit(solution)/shard_map/ppermute | solution.py:270
  19.5 9.3 %collective-permute-start.1 = (bf16[80,512]{1,0:T(8,128)(2,1)S(1)}, bf16[80,512]{1,0:T(8,128)(2,1)S(1)}, u32[]{:S(2)}, u32[]{:S(2)}) collective-permute-start(bf16[80,512]{1,0:T(8,128)(2,1)S(1)} %pad_maximum_fusion.1), channel_id=1, source_target_pairs={{0,32},{16,48},{32,0},{48,16},{64,96},{80,112},{96,64},{112,80},{1... | collective-permute-start | bytes 245768 | tf_op jit(solution)/shard_map/ppermute | solution.py:270
  28.8 7.2 %copy-start.3 = (f32[2048]{0:T(1024)S(1)}, f32[2048]{0:T(1024)}, u32[]{:S(2)}) copy-start(f32[2048]{0:T(1024)} %param.6) | copy-start | bytes 24580
  28.8 7.2 %collective-permute-start.2 = (bf16[80,1024]{1,0:T(8,128)(2,1)S(1)}, bf16[80,1024]{1,0:T(8,128)(2,1)S(1)}, u32[]{:S(2)}, u32[]{:S(2)}) collective-permute-start(bf16[80,1024]{1,0:T(8,128)(2,1)S(1)} %pad_maximum_fusion.refs_0_), channel_id=1, source_target_pairs={{0,16},{16,0},{32,48},{48,32},{64,80},{80,64},{96,112},{112,96},{1... | collective-permute-start | bytes 491528 | tf_op jit(solution)/shard_map/ppermute | solution.py:270
  60.8 16.8 %copy-start.4 = (bf16[2048,64]{0,1:T(8,128)(2,1)S(1)}, bf16[2048,64]{0,1:T(8,128)(2,1)}, u32[]{:S(2)}) copy-start(bf16[2048,64]{0,1:T(8,128)(2,1)} %param.5) | copy-start | bytes 786436
  60.9 3.1 %collective-permute-start.3 = (f32[4,2048]{1,0:T(4,128)S(1)}, f32[4,2048]{1,0:T(4,128)S(1)}, u32[]{:S(2)}, u32[]{:S(2)}) collective-permute-start(f32[4,2048]{1,0:T(4,128)S(1)} %log_add_fusion.2), channel_id=1, source_target_pairs={{0,1},{1,0},{2,3},{3,2},{4,5},{5,4},{6,7},{7,6},{8,9},{9,8},{10,11... | collective-permute-start | bytes 98312 | tf_op jit(solution)/shard_map/ppermute | solution.py:273
  64.1 16.2 %collective-permute-start.4 = (f32[4,2048]{1,0:T(4,128)S(1)}, f32[4,2048]{1,0:T(4,128)S(1)}, u32[]{:S(2)}, u32[]{:S(2)}) collective-permute-start(f32[4,2048]{1,0:T(4,128)S(1)} %log_add_fusion.1), channel_id=1, source_target_pairs={{0,8},{1,9},{2,10},{3,11},{4,12},{5,13},{6,14},{7,15},{8,0},{9,1},... | collective-permute-start | bytes 98312 | tf_op jit(solution)/shard_map/ppermute | solution.py:273
  114.0 41.2 %collective-permute-start.5 = (f32[4,256]{1,0:T(4,128)S(1)}, f32[4,256]{1,0:T(4,128)S(1)}, u32[]{:S(2)}, u32[]{:S(2)}) collective-permute-start(f32[4,256]{1,0:T(4,128)S(1)} %shard_map.71), channel_id=1, source_target_pairs={{0,64},{16,80},{32,96},{48,112},{64,0},{80,16},{96,32},{112,48},{1... | collective-permute-start | bytes 12296 | tf_op jit(solution)/shard_map/ppermute | solution.py:270
  155.8 9.8 %all-to-all-start.3 = ((f32[4,1,256]{2,1,0:T(1,128)}), f32[4,1,256]{2,1,0:T(1,128)S(1)}, u32[]{:S(2)}, u32[]{:S(2)}) async-start(f32[4,1,256]{2,1,0:T(1,128)} %copy.10), calls=%async_computation.3 | async-start | bytes 8192 | tf_op jit(solution)/shard_map/all_to_all | solution.py:359

commit v4 on v3

--- a/solution.py
+++ b/solution.py
@@ -155,7 +155,7 @@
 def second_kernel(
     slots, place_ref, near_ref, far_ref, x_ref, c_ref, s_ref, extra_ref, left_ref, acc_ref, top_ref
 ):
-    nz, each = s_ref.shape
+    nz, _, each = s_ref.shape
     rows = nz * each
     ny, _, per = x_ref.shape
     row_step = min(ROWS, rows)
@@ -193,7 +193,7 @@
 
     def store(result):
         for g, (_, _, row) in enumerate(slots):
-            s_ref[pl.ds(place_ref[0] ^ row, 1), :] = result[:, g * each : (g + 1) * each]
+            s_ref[place_ref[0] ^ row] = result[:, g * each : (g + 1) * each]
 
     total = jnp.sum(acc_ref[...].T, axis=0, keepdims=True)
     store(jnp.log(total))
@@ -261,9 +261,8 @@
     my_y, my_z = place // nz, place % nz
     depth = FEATURES + EXTRA
     y_groups = [[y * nz + z for y in range(ny)] for z in range(nz)]
-    quarters = [[g * (nz // 2) + z for z in range(nz // 2)] for g in range(2 * ny)]
-    nx = nw // 4
-    x_groups = [[(h * nx + x) * 2 + k for x in range(nx)] for h in range(2) for k in range(2)]
+    z_groups = [[y * nz + z for z in range(nz)] for y in range(ny)]
+    x_groups = [[h * (nw // 2) + k for k in range(nw // 2)] for h in range(2)]
 
     def along_z(value, k):
         perm = [(y * nz + z, y * nz + (z ^ k)) for y in range(ny) for z in range(nz)]
@@ -292,7 +291,6 @@
     while bit > 1:
         y = jnp.concatenate([y, along_z(y, bit)], axis=1)
         bit //= 2
-    xs, y = lax.optimization_barrier((xs, y))
     far = along_z(y, 1)
 
     def first(block, *more):
@@ -316,7 +314,6 @@
     got = shared(total, "blk", y_groups)
     total, logw = log_sum(got[:, :ny]), got[:, ny]
     total = log_sum(shared(total, "wide", x_groups))
-    total = join(total, along_wide(total, 1))
     total = join(total, along_wide(total, nw // 2))
     c = logw - total
     sq = jnp.sum(jnp.square(x.astype(f32)), axis=0, keepdims=True)
@@ -325,39 +322,31 @@
 
     count = nz // 2
     width = count.bit_length() - 1
-    blocks = []
+    slots = []
     for h in range(2):
         for k in range(count):
-            away = 2 * int(format(k, "b").zfill(width)[::-1], 2) + h
-            blocks.append((h, k, away))
-    place_in = (my_z % count).astype(jnp.int32).reshape(1)
-
-    def second(slots, near):
-        return call(
-            functools.partial(second_kernel, slots),
-            jax.ShapeDtypeStruct((count, each), f32),
-            [
-                pltpu.VMEM((ny, EXTRA, per), bf16),
-                pltpu.VMEM((half, DEPTH), bf16),
-                pltpu.VMEM((half, 128), f32),
-                pltpu.VMEM((half, 128), f32),
-            ],
-            2 * pairs * DEPTH,
-            pairs,
-            place_in,
-            near,
-            yt_far,
-            xs,
-            c,
-            spaces=[pltpu.SMEM] + [pltpu.VMEM] * 4,
-        )
-
-    sent = second(tuple((h, k, a - count) for h, k, a in blocks if a >= count), yt_near)
-    yt_near, sent = lax.optimization_barrier((yt_near, sent))
-    other = along_z(sent, count)
-    sums = join(second(tuple(b for b in blocks if b[2] < count), yt_near), other)
-    sums = lax.all_to_all(sums, "blk", 0, 0, axis_index_groups=quarters, tiled=True)
-    new_target_potential = -0.5 * (log_sum(sums) - offset[0])
+            slots.append((h, k, 2 * int(format(k, "b").zfill(width)[::-1], 2) + h))
+    rows = nz * each
+    sums = call(
+        functools.partial(second_kernel, slots),
+        jax.ShapeDtypeStruct((nz, 1, each), f32),
+        [
+            pltpu.VMEM((ny, EXTRA, per), bf16),
+            pltpu.VMEM((rows, DEPTH), bf16),
+            pltpu.VMEM((rows, 128), f32),
+            pltpu.VMEM((rows, 128), f32),
+        ],
+        2 * cols * rows * DEPTH,
+        cols * rows,
+        my_z.astype(jnp.int32).reshape(1),
+        yt_near,
+        yt_far,
+        xs,
+        c,
+        spaces=[pltpu.SMEM] + [pltpu.VMEM] * 4,
+    )
+    sums = lax.all_to_all(sums, "blk", 0, 0, axis_index_groups=z_groups, tiled=True)
+    new_target_potential = -0.5 * (log_sum(sums)[0] - offset[0])
     return source_potential.reshape(per), new_target_potential
 
 

time: 168 us -> 167 us (level)
  starting transfers between devices: 48.2 us -> 43.6 us
  waiting for transfers between devices: 15.2 us -> 18.2 us
    ppermute x4 -> x3, starting transfers between devices: 23.9 us -> 16.4 us  [along_z(): return lax.ppermute(value, 'blk', perm)]
    all_to_all x1, waiting for transfers between devices: 4.96 us -> 9.82 us  [per_device(): lax.all_to_all(sums, 'blk', 0, 0, axis_index_groups=z_groups, tiled=True)]
    all_to_all x1, starting transfers between devices: 4.25 us -> 9.07 us  [per_device(): lax.all_to_all(sums, 'blk', 0, 0, axis_index_groups=z_groups, tiled=True)]
    ppermute x2 -> x1, starting transfers between devices: 15.5 us -> 13.6 us  [along_wide(): return lax.ppermute(value, 'wide', [(w, w ^ k) for w in range(nw)])]
    ppermute x2 -> x1, waiting for transfers between devices: 3.66 us -> 1.79 us  [along_wide(): return lax.ppermute(value, 'wide', [(w, w ^ k) for w in range(nw)])]
    pallas_call x5 -> x4, Pallas kernels: 77.4 us -> 77.6 us  [call(): pl.pallas_call(kernel, out_shape=outs, in_specs=[pl.BlockSpec(memory_spac...]
    ppermute x4 -> x3, waiting for transfers between devices: 6.59 us -> 6.55 us  [along_z(): return lax.ppermute(value, 'blk', perm)]
  transfers between devices with their start and end apart: 8 -> 6, of which waited for: 6 -> 5; matrix products, arithmetic and copies ran while one was open for 0% -> 0% of each run, Pallas kernels for 23% -> 3%
where the time goes in v4:
time: 167 us; the launch traced here: 166 us
  Pallas kernels  77.6 us (46%)
  starting transfers between devices  43.6 us (26%)
  blocking collectives  21.2 us (13%)
  waiting for transfers between devices  18.2 us (11%)
  local copies, waits for them, and re-layouts  2.85 us (2%)
    pallas_call x4, Pallas kernels, call(): pl.pallas_call(kernel, out_shape=outs, in_specs=[pl.BlockSpec(memory_spac...  77.6 us
    all_to_all x2, blocking collectives, shared(): lax.all_to_all(spread, axis, 0, 0, axis_index_groups=groups, tiled=True)  21.2 us
    ppermute x3, starting transfers between devices, along_z(): return lax.ppermute(value, 'blk', perm)  16.4 us
    ppermute x1, starting transfers between devices, along_wide(): return lax.ppermute(value, 'wide', [(w, w ^ k) for w in range(nw)])  13.6 us
    all_to_all x1, waiting for transfers between devices, per_device(): lax.all_to_all(sums, 'blk', 0, 0, axis_index_groups=z_groups, tiled=True)  9.82 us
    all_to_all x1, starting transfers between devices, per_device(): lax.all_to_all(sums, 'blk', 0, 0, axis_index_groups=z_groups, tiled=True)  9.07 us
    ppermute x3, waiting for transfers between devices, along_z(): return lax.ppermute(value, 'blk', perm)  6.55 us
    all_to_all x1, starting transfers between devices, shared(): lax.all_to_all(spread, axis, 0, 0, axis_index_groups=groups, tiled=True)  4.59 us
  transfers between devices with their start and end apart: 6, of which 5 were waited for; matrix products, arithmetic and copies ran while one was open for 0% of the time, Pallas kernels for 3%

profile of v4, /device:TPU:6, one launch (start us, length us, event | category | flops | bytes accessed | tf_op | source)
XLA Modules:
  0.0 165.9 jit_solution(3323241364498029841)
XLA Ops:
  0.6 2.1 %broadcast_in_dim.8 = bf16[4,64,2048]{2,1,0:T(8,128)(2,1)} broadcast(bf16[64,2048]{1,0:T(8,128)(2,1)} %bitcast.19), dimensions={1,2} | broadcast | bytes 1310720 | tf_op jit(solution)/shard_map/broadcast_in_dim | solution.py:275
  2.7 4.6 %all-to-all-start = ((bf16[4,64,2048]{2,1,0:T(8,128)(2,1)}), bf16[4,64,2048]{2,1,0:T(8,128)(2,1)S(1)}, u32[]{:S(2)}, u32[]{:S(2)}) async-start(bf16[4,64,2048]{2,1,0:T(8,128)(2,1)} %broadcast_in_dim.8), calls=%async_computation | async-start | bytes 2097152 | tf_op jit(solution)/shard_map/all_to_all | solution.py:276
  7.3 0.7 copy-done.1
  8.0 9.1 %collective-permute-start = (bf16[80,256]{1,0:T(8,128)(2,1)S(1)}, bf16[80,256]{1,0:T(8,128)(2,1)S(1)}, u32[]{:S(2)}, u32[]{:S(2)}) collective-permute-start(bf16[80,256]{1,0:T(8,128)(2,1)S(1)} %get-tuple-element.8), channel_id=1, source_target_pairs={{0,64},{16,80},{32,96},{48,112},{64,0},{80,16},{96,32},{112,48},{1... | collective-permute-start | bytes 122888 | tf_op jit(solution)/shard_map/ppermute | solution.py:269
  17.1 2.4 %collective-permute-done = bf16[80,256]{1,0:T(8,128)(2,1)S(1)} collective-permute-done((bf16[80,256]{1,0:T(8,128)(2,1)S(1)}, bf16[80,256]{1,0:T(8,128)(2,1)S(1)}, u32[]{:S(2)}, u32[]{:S(2)}) %collective-permute-start) | collective-permute-done | bytes 40992 | tf_op jit(solution)/shard_map/ppermute | solution.py:269
  19.5 5.2 %collective-permute-start.1 = (bf16[80,512]{1,0:T(8,128)(2,1)S(1)}, bf16[80,512]{1,0:T(8,128)(2,1)S(1)}, u32[]{:S(2)}, u32[]{:S(2)}) collective-permute-start(bf16[80,512]{1,0:T(8,128)(2,1)S(1)} %pad_maximum_fusion), channel_id=1, source_target_pairs={{0,32},{16,48},{32,0},{48,16},{64,96},{80,112},{96,64},{112,80},{1... | collective-permute-start | bytes 245768 | tf_op jit(solution)/shard_map/ppermute | solution.py:269
  24.7 4.1 %collective-permute-done.1 = bf16[80,512]{1,0:T(8,128)(2,1)S(1)} collective-permute-done((bf16[80,512]{1,0:T(8,128)(2,1)S(1)}, bf16[80,512]{1,0:T(8,128)(2,1)S(1)}, u32[]{:S(2)}, u32[]{:S(2)}) %collective-permute-start.1) | collective-permute-done | bytes 81952 | tf_op jit(solution)/shard_map/ppermute | solution.py:269
  28.8 2.1 %collective-permute-start.2 = (bf16[80,1024]{1,0:T(8,128)(2,1)S(1)}, bf16[80,1024]{1,0:T(8,128)(2,1)S(1)}, u32[]{:S(2)}, u32[]{:S(2)}) collective-permute-start(bf16[80,1024]{1,0:T(8,128)(2,1)S(1)} %constant_dynamic-update-slice_fusion.refs_0_), channel_id=1, source_target_pairs={{0,16},{16,0},{32,48},{48,32},{64,80},{80,64},{96,112},{112,96},{1... | collective-permute-start | bytes 491528 | tf_op jit(solution)/shard_map/ppermute | solution.py:269
  30.9 5.0 %shard_map.69 = (bf16[1024,128]{1,0:T(8,128)(2,1)S(1)}, f32[4,2048]{1,0:T(4,128)S(1)}) custom-call(bf16[80,1024]{1,0:T(8,128)(2,1)S(1)} %constant_dynamic-update-slice_fusion.refs_0_, bf16[4,64,2048]{2,1,0:T(8,128)(2,1)S(1)} %all-to-all-done.refs_1_.x_ref), custom_call_target="tpu_custom_call" | custom-call | flops 2147483648 | bytes 4194304 | tf_op jit(solution)/shard_map/pallas_call | solution.py:235
  35.9 0.1 collective-permute-done.2.refs_0_
  36.0 5.0 %shard_map.70 = (bf16[1024,128]{1,0:T(8,128)(2,1)S(1)}, f32[5,2048]{1,0:T(8,128)S(1)}) custom-call(bf16[80,1024]{1,0:T(8,128)(2,1)S(1)} %collective-permute-done.2.refs_0_, bf16[4,64,2048]{2,1,0:T(8,128)(2,1)S(1)} %all-to-all-done.refs_1_.x_ref, f32[4,2048]{1,0:T(4,128)S(1)} %get-tuple-element.9.refs_2_, f32[1,2048]{1,0:T(1,128)S(1)} %bitcast.18), custom_call_target="tpu_custom_call" | custom-call | flops 2147483648 | bytes 4194304 | tf_op jit(solution)/shard_map/pallas_call | solution.py:235
  41.0 11.1 %all_to_all.20 = f32[4,5,2048]{2,1,0:T(8,128)S(1)} all-to-all(f32[4,5,2048]{2,1,0:T(8,128)S(1)} %broadcast_in_dim.9), channel_id=1, replica_groups={{0,128,256,384},{16,144,272,400},{32,160,288,416},{48,176,304,432},{64,..., dimensions={0} | all-to-all | bytes 327680 | tf_op jit(solution)/shard_map/all_to_all | solution.py:276
  52.2 0.1 exponential_reduce_fusion.1
  52.3 10.0 %all_to_all.21 = f32[8,4,2048]{2,1,0:T(4,128)S(1)} all-to-all(f32[8,4,2048]{2,1,0:T(4,128)S(1)} %broadcast_in_dim.10), channel_id=1, replica_groups={{0,1,2,3,4,5,6,7},{8,9,10,11,12,13,14,15},{16,17,18,19,20,21,22,23},{24..., dimensions={0} | all-to-all | bytes 524288 | tf_op jit(solution)/shard_map/all_to_all | solution.py:276
  62.4 0.1 reduce_max.28
  62.4 0.1 exponential_reduce_fusion
  62.6 13.6 %collective-permute-start.3 = (f32[4,2048]{1,0:T(4,128)S(1)}, f32[4,2048]{1,0:T(4,128)S(1)}, u32[]{:S(2)}, u32[]{:S(2)}) collective-permute-start(f32[4,2048]{1,0:T(4,128)S(1)} %log_add_fusion.1), channel_id=1, source_target_pairs={{0,8},{1,9},{2,10},{3,11},{4,12},{5,13},{6,14},{7,15},{8,0},{9,1},... | collective-permute-start | bytes 98312 | tf_op jit(solution)/shard_map/ppermute | solution.py:272
  76.1 0.1 multiply_reduce_fusion
  76.3 1.8 %collective-permute-done.3 = f32[4,2048]{1,0:T(4,128)S(1)} collective-permute-done((f32[4,2048]{1,0:T(4,128)S(1)}, f32[4,2048]{1,0:T(4,128)S(1)}, u32[]{:S(2)}, u32[]{:S(2)}) %collective-permute-start.3) | collective-permute-done | bytes 32800 | tf_op jit(solution)/shard_map/ppermute | solution.py:272
  78.1 67.6 %shard_map.71 = f32[8,1,256]{2,1,0:T(1,128)} custom-call(s32[1]{0:T(128)} %bitcast.7.place_ref, bf16[1024,128]{1,0:T(8,128)(2,1)S(1)} %get-tuple-element.11.near_ref, bf16[1024,128]{1,0:T(8,128)(2,1)S(1)} %get-tuple-element.12.far_ref, bf16[4,64,2048]{2,1,0:T(8,128)(2,1)S(1)} %all-to-all-done.refs_1_.x_ref, f32[4,2048]{1,0:T(4,128)S(1)} %get-tuple-element.14.c_ref), custom_call_target="tpu_custom_call" | custom-call | flops 4294967296 | bytes 4194304 | tf_op jit(solution)/shard_map/pallas_call | solution.py:235
  145.7 9.1 %all-to-all-start.3 = ((f32[8,1,256]{2,1,0:T(1,128)}), f32[8,1,256]{2,1,0:T(1,128)S(1)}, u32[]{:S(2)}, u32[]{:S(2)}) async-start(f32[8,1,256]{2,1,0:T(1,128)} %shard_map.71), calls=%async_computation.3 | async-start | bytes 16384 | tf_op jit(solution)/shard_map/all_to_all | solution.py:348
  154.8 0.6 subtract_multiply_fusion
  155.4 9.8 %all-to-all-done.3 = f32[8,1,256]{2,1,0:T(1,128)S(1)} async-done(((f32[8,1,256]{2,1,0:T(1,128)}), f32[8,1,256]{2,1,0:T(1,128)S(1)}, u32[]{:S(2)}, u32[]{:S(2)}) %all-to-all-start.3) | async-done | bytes 8224 | tf_op jit(solution)/shard_map/all_to_all | solution.py:348
  165.3 0.6 subtract_multiply_fusion.1
  (24 shorter events, 0.4 us)
Async XLA Ops:
  2.7 4.6 %copy-start = (bf16[256,64]{0,1:T(8,128)(2,1)S(1)}, bf16[256,64]{0,1:T(8,128)(2,1)}, u32[]{:S(2)}) copy-start(bf16[256,64]{0,1:T(8,128)(2,1)} %param.7) | copy-start | bytes 98308
  2.7 4.6 %copy-start.2 = (f32[256]{0:T(256)S(1)}, f32[256]{0:T(256)}, u32[]{:S(2)}) copy-start(f32[256]{0:T(256)} %param.9) | copy-start | bytes 3076
  2.7 28.2 %all-to-all-start = ((bf16[4,64,2048]{2,1,0:T(8,128)(2,1)}), bf16[4,64,2048]{2,1,0:T(8,128)(2,1)S(1)}, u32[]{:S(2)}, u32[]{:S(2)}) async-start(bf16[4,64,2048]{2,1,0:T(8,128)(2,1)} %broadcast_in_dim.8), calls=%async_computation | async-start | bytes 2097152 | tf_op jit(solution)/shard_map/all_to_all | solution.py:276
  7.3 0.7 copy-start.1
  8.0 11.5 %collective-permute-start = (bf16[80,256]{1,0:T(8,128)(2,1)S(1)}, bf16[80,256]{1,0:T(8,128)(2,1)S(1)}, u32[]{:S(2)}, u32[]{:S(2)}) collective-permute-start(bf16[80,256]{1,0:T(8,128)(2,1)S(1)} %get-tuple-element.8), channel_id=1, source_target_pairs={{0,64},{16,80},{32,96},{48,112},{64,0},{80,16},{96,32},{112,48},{1... | collective-permute-start | bytes 122888 | tf_op jit(solution)/shard_map/ppermute | solution.py:269
  19.5 9.3 %collective-permute-start.1 = (bf16[80,512]{1,0:T(8,128)(2,1)S(1)}, bf16[80,512]{1,0:T(8,128)(2,1)S(1)}, u32[]{:S(2)}, u32[]{:S(2)}) collective-permute-start(bf16[80,512]{1,0:T(8,128)(2,1)S(1)} %pad_maximum_fusion), channel_id=1, source_target_pairs={{0,32},{16,48},{32,0},{48,16},{64,96},{80,112},{96,64},{112,80},{1... | collective-permute-start | bytes 245768 | tf_op jit(solution)/shard_map/ppermute | solution.py:269
  28.8 7.2 %copy-start.3 = (f32[2048]{0:T(1024)S(1)}, f32[2048]{0:T(1024)}, u32[]{:S(2)}) copy-start(f32[2048]{0:T(1024)} %param.6) | copy-start | bytes 24580
  28.8 7.2 %collective-permute-start.2 = (bf16[80,1024]{1,0:T(8,128)(2,1)S(1)}, bf16[80,1024]{1,0:T(8,128)(2,1)S(1)}, u32[]{:S(2)}, u32[]{:S(2)}) collective-permute-start(bf16[80,1024]{1,0:T(8,128)(2,1)S(1)} %constant_dynamic-update-slice_fusion.refs_0_), channel_id=1, source_target_pairs={{0,16},{16,0},{32,48},{48,32},{64,80},{80,64},{96,112},{112,96},{1... | collective-permute-start | bytes 491528 | tf_op jit(solution)/shard_map/ppermute | solution.py:269
  62.4 13.7 %copy-start.4 = (bf16[2048,64]{0,1:T(8,128)(2,1)S(1)}, bf16[2048,64]{0,1:T(8,128)(2,1)}, u32[]{:S(2)}) copy-start(bf16[2048,64]{0,1:T(8,128)(2,1)} %param.5) | copy-start | bytes 786436
  62.6 15.5 %collective-permute-start.3 = (f32[4,2048]{1,0:T(4,128)S(1)}, f32[4,2048]{1,0:T(4,128)S(1)}, u32[]{:S(2)}, u32[]{:S(2)}) collective-permute-start(f32[4,2048]{1,0:T(4,128)S(1)} %log_add_fusion.1), channel_id=1, source_target_pairs={{0,8},{1,9},{2,10},{3,11},{4,12},{5,13},{6,14},{7,15},{8,0},{9,1},... | collective-permute-start | bytes 98312 | tf_op jit(solution)/shard_map/ppermute | solution.py:272
  145.7 19.5 %all-to-all-start.3 = ((f32[8,1,256]{2,1,0:T(1,128)}), f32[8,1,256]{2,1,0:T(1,128)S(1)}, u32[]{:S(2)}, u32[]{:S(2)}) async-start(f32[8,1,256]{2,1,0:T(1,128)} %shard_map.71), calls=%async_computation.3 | async-start | bytes 16384 | tf_op jit(solution)/shard_map/all_to_all | solution.py:348

commit v5 on v3

--- a/solution.py
+++ b/solution.py
@@ -39,20 +39,24 @@
     return one, one, one
 
 
-def prepare_kernel(y_ref, logw_ref, potential_ref, out_ref, offset_ref):
+def prepare_kernel(core_ref, y_ref, logw_ref, potential_ref, out_ref, offset_ref):
     y = y_ref[...].astype(jnp.float32)
     offset = potential_ref[...] * 2.0 + logw_ref[...]
     bias = offset - jnp.sum(y * y, axis=0, keepdims=True)
-    out_ref[0:FEATURES, :] = (y * 2.0).astype(jnp.bfloat16)
+    half = FEATURES // 2
+    first, second = y[0:half, :] * 2.0, y[half:FEATURES, :] * 2.0
+    swap = core_ref[0] != 0
+    out_ref[0:half, :] = jnp.where(swap, second, first).astype(jnp.bfloat16)
+    out_ref[half:FEATURES, :] = jnp.where(swap, first, second).astype(jnp.bfloat16)
     out_ref[FEATURES : FEATURES + EXTRA, :] = extra_block(
         three_parts(bias), ones_of(bias.shape[1])
     ).astype(jnp.bfloat16)
     offset_ref[...] = offset
 
 
-def weights_of(features, extra):
-    rest = jnp.zeros((DEPTH - FEATURES - EXTRA, features.shape[1]), features.dtype)
-    return jnp.concatenate([features, extra, rest], axis=0)
+def weights_of(own_ref, other_ref, r, at, extra):
+    rest = jnp.zeros((DEPTH - FEATURES - EXTRA, extra.shape[1]), extra.dtype)
+    return jnp.concatenate([own_ref[r, :, at], other_ref[r, :, at], extra, rest], axis=0)
 
 
 def product(a, b):
@@ -70,12 +74,12 @@
 
 
 def first_kernel(last, *refs):
-    y_ref, x_ref, refs = refs[0], refs[1], refs[2:]
+    y_ref, own_ref, other_ref, refs = refs[0], refs[1], refs[2], refs[3:]
     if last:
         before_ref, logw_ref, refs = refs[0], refs[1], refs[2:]
     yt_ref, l_ref, sums_ref = refs
     rows = yt_ref.shape[0]
-    ny, _, per = x_ref.shape
+    ny, _, per = own_ref.shape
     row_step = min(ROWS, rows)
     col_step = min(LANES, per)
     together = 2
@@ -99,16 +103,18 @@
     def store(row, value):
         if last:
             value = join(before_ref[row : row + 1, :], value)
-        l_ref[row : row + 1, :] = value
+        l_ref[row : row + 1, 0:per] = value
 
     if last:
-        l_ref[ny : ny + 1, :] = logw_ref[...]
+        part = per // ny
+        for k in range(ny):
+            l_ref[k : k + 1, per:] = logw_ref[:, k * part : (k + 1) * part]
 
     def main(g, carry):
         for s in range(together):
             r = g * together + s
             for t in range(0, per, col_step):
-                weights = weights_of(x_ref[r, :, t : t + col_step], extra)
+                weights = weights_of(own_ref, other_ref, r, slice(t, t + col_step), extra)
                 total = jnp.zeros((8, col_step), jnp.float32)
                 for j in range(0, rows, row_step):
                     score = product(yt_ref[j : j + row_step, :], weights)
@@ -127,7 +133,7 @@
         def again(g, carry):
             at = pl.ds(pl.multiple_of(g * col_step, col_step), col_step)
             for r in range(ny):
-                weights = weights_of(x_ref[r, :, at], extra)
+                weights = weights_of(own_ref, other_ref, r, at, extra)
 
                 def advance(j, state):
                     top, total = state
@@ -153,18 +159,30 @@
 
 
 def second_kernel(
-    slots, place_ref, near_ref, far_ref, x_ref, c_ref, s_ref, extra_ref, left_ref, acc_ref, top_ref
+    slots,
+    place_ref,
+    near_ref,
+    far_ref,
+    own_ref,
+    other_ref,
+    total_ref,
+    logw_ref,
+    s_ref,
+    extra_ref,
+    left_ref,
+    acc_ref,
+    top_ref,
 ):
     nz, each = s_ref.shape
     rows = nz * each
-    ny, _, per = x_ref.shape
+    ny, _, per = own_ref.shape
     row_step = min(ROWS, rows)
     col_step = min(LANES, per)
 
     for r in range(ny):
-        extra_ref[r] = extra_block(
-            ones_of(per), three_parts(c_ref[r : r + 1, :])
-        ).astype(jnp.bfloat16)
+        logw = jnp.concatenate([logw_ref[r, k : k + 1, per:] for k in range(ny)], axis=1)
+        c = logw - total_ref[r : r + 1, :]
+        extra_ref[r] = extra_block(ones_of(per), three_parts(c)).astype(jnp.bfloat16)
     for g, (half, k, _) in enumerate(slots):
         ref = far_ref if half else near_ref
         left_ref[g * each : (g + 1) * each, :] = ref[k * each : (k + 1) * each, :]
@@ -181,7 +199,7 @@
         for r in range(ny):
             for t in range(0, per, col_step):
                 at = slice(t, t + col_step)
-                score = product(left, weights_of(x_ref[r, :, at], extra_ref[r, :, at]))
+                score = product(left, weights_of(own_ref, other_ref, r, at, extra_ref[r, :, at]))
                 part = lanes_folded(jnp.exp(score), jnp.add)
                 if r == 0 and t == 0:
                     acc_ref[here, :] = part
@@ -212,7 +230,7 @@
                 def advance(t, state):
                     top, total = state
                     at = pl.ds(pl.multiple_of(t * col_step, col_step), col_step)
-                    score = product(left, weights_of(x_ref[r, :, at], extra_ref[r, :, at]))
+                    score = product(left, weights_of(own_ref, other_ref, r, at, extra_ref[r, :, at]))
                     new = jnp.maximum(top, lanes_folded(score, jnp.maximum))
                     total = total * jnp.exp(top - new)
                     for k in range(col_step // 128):
@@ -259,11 +277,11 @@
     pairs = cols * half
     place = lax.axis_index("blk")
     my_y, my_z = place // nz, place % nz
+    core = (lax.axis_index("wide") % 2).astype(jnp.int32)
     depth = FEATURES + EXTRA
     y_groups = [[y * nz + z for y in range(ny)] for z in range(nz)]
     quarters = [[g * (nz // 2) + z for z in range(nz // 2)] for g in range(2 * ny)]
-    nx = nw // 4
-    x_groups = [[(h * nx + x) * 2 + k for x in range(nx)] for h in range(2) for k in range(2)]
+    x_groups = [[h * (nw // 2) + k for k in range(nw // 2)] for h in range(2)]
 
     def along_z(value, k):
         perm = [(y * nz + z, y * nz + (z ^ k)) for y in range(ny) for z in range(nz)]
@@ -282,17 +300,22 @@
         [],
         each * FEATURES * 4,
         0,
+        core.reshape(1),
         target_latent.T,
         target_logw.reshape(1, each),
         target_potential.reshape(1, each),
+        spaces=[pltpu.SMEM] + [pltpu.VMEM] * 3,
     )
     x = source_latent.T
-    xs = shared(x, "blk", y_groups)
+    part = lax.dynamic_slice(x, (core * (FEATURES // 2), 0), (FEATURES // 2, per))
+    own = shared(part, "blk", y_groups)
     bit = nz // 2
     while bit > 1:
         y = jnp.concatenate([y, along_z(y, bit)], axis=1)
+        if bit == nz // 2:
+            own, _ = lax.optimization_barrier((own, y))
+            other = along_wide(own, 1)
         bit //= 2
-    xs, y = lax.optimization_barrier((xs, y))
     far = along_z(y, 1)
 
     def first(block, *more):
@@ -301,24 +324,23 @@
             functools.partial(first_kernel, last),
             (
                 jax.ShapeDtypeStruct((half, DEPTH), bf16),
-                jax.ShapeDtypeStruct((ny + last, per), f32),
+                jax.ShapeDtypeStruct((ny, per + per // ny if last else per), f32),
             ),
             [pltpu.VMEM((ny, 8, per), f32)],
             2 * pairs * DEPTH,
             pairs,
             block,
-            xs,
+            own,
+            other,
             *more,
         )
 
     yt_near, total = first(y)
     yt_far, total = first(far, total, source_logw.reshape(1, per))
     got = shared(total, "blk", y_groups)
-    total, logw = log_sum(got[:, :ny]), got[:, ny]
+    total = log_sum(got[:, :, :per])
     total = log_sum(shared(total, "wide", x_groups))
-    total = join(total, along_wide(total, 1))
     total = join(total, along_wide(total, nw // 2))
-    c = logw - total
     sq = jnp.sum(jnp.square(x.astype(f32)), axis=0, keepdims=True)
     mine = lax.dynamic_slice(total, (my_y, 0), (1, per))
     source_potential = -0.5 * (mine - sq)
@@ -328,8 +350,7 @@
     blocks = []
     for h in range(2):
         for k in range(count):
-            away = 2 * int(format(k, "b").zfill(width)[::-1], 2) + h
-            blocks.append((h, k, away))
+            blocks.append((h, k, 2 * int(format(k, "b").zfill(width)[::-1], 2) + h))
     place_in = (my_z % count).astype(jnp.int32).reshape(1)
 
     def second(slots, near):
@@ -347,15 +368,17 @@
             place_in,
             near,
             yt_far,
-            xs,
-            c,
-            spaces=[pltpu.SMEM] + [pltpu.VMEM] * 4,
+            own,
+            other,
+            total,
+            got,
+            spaces=[pltpu.SMEM] + [pltpu.VMEM] * 6,
         )
 
     sent = second(tuple((h, k, a - count) for h, k, a in blocks if a >= count), yt_near)
     yt_near, sent = lax.optimization_barrier((yt_near, sent))
-    other = along_z(sent, count)
-    sums = join(second(tuple(b for b in blocks if b[2] < count), yt_near), other)
+    arrived = along_z(sent, count)
+    sums = join(second(tuple(b for b in blocks if b[2] < count), yt_near), arrived)
     sums = lax.all_to_all(sums, "blk", 0, 0, axis_index_groups=quarters, tiled=True)
     new_target_potential = -0.5 * (log_sum(sums) - offset[0])
     return source_potential.reshape(per), new_target_potential

time: 168 us -> 168 us (level)
    ppermute x2, waiting for transfers between devices: 3.66 us -> 1.76 us  [along_wide(): return lax.ppermute(value, 'wide', [(w, w ^ k) for w in range(nw)])]
  transfers between devices with their start and end apart: 8 -> 8, of which waited for: 6 -> 5; matrix products, arithmetic and copies ran while one was open for 0% -> 0% of each run, Pallas kernels for 23% -> 23%
where the time goes in v5:
time: 168 us; the launch traced here: 167 us
  Pallas kernels  77.4 us (46%)
  starting transfers between devices  48.7 us (29%)
  blocking collectives  20.7 us (12%)
  waiting for transfers between devices  14.2 us (8%)
  local copies, waits for them, and re-layouts  3.13 us (2%)
    pallas_call x5, Pallas kernels, call(): pl.pallas_call(kernel, out_shape=outs, in_specs=[pl.BlockSpec(memory_spac...  77.4 us
    ppermute x4, starting transfers between devices, along_z(): return lax.ppermute(value, 'blk', perm)  24 us
    all_to_all x2, blocking collectives, shared(): lax.all_to_all(spread, axis, 0, 0, axis_index_groups=groups, tiled=True)  20.7 us
    ppermute x2, starting transfers between devices, along_wide(): return lax.ppermute(value, 'wide', [(w, w ^ k) for w in range(nw)])  16 us
    ppermute x4, waiting for transfers between devices, along_z(): return lax.ppermute(value, 'blk', perm)  7.49 us
    all_to_all x1, waiting for transfers between devices, per_device(): lax.all_to_all(sums, 'blk', 0, 0, axis_index_groups=quarters, tiled=True)  4.96 us
    all_to_all x1, starting transfers between devices, shared(): lax.all_to_all(spread, axis, 0, 0, axis_index_groups=groups, tiled=True)  4.59 us
    all_to_all x1, starting transfers between devices, per_device(): lax.all_to_all(sums, 'blk', 0, 0, axis_index_groups=quarters, tiled=True)  4.21 us
  transfers between devices with their start and end apart: 8, of which 5 were waited for; matrix products, arithmetic and copies ran while one was open for 0% of the time, Pallas kernels for 23%

profile of v5, /device:TPU:6, one launch (start us, length us, event | category | flops | bytes accessed | tf_op | source)
XLA Modules:
  0.0 166.7 jit_solution(3371964612558214881)
XLA Ops:
  0.6 0.9 dynamic-slice_bitcast_fusion
  1.6 0.8 broadcast_in_dim.8
  2.4 4.6 %all-to-all-start = ((bf16[4,32,2048]{2,1,0:T(8,128)(2,1)}), bf16[4,32,2048]{2,1,0:T(8,128)(2,1)S(1)}, u32[]{:S(2)}, u32[]{:S(2)}) async-start(bf16[4,32,2048]{2,1,0:T(8,128)(2,1)} %broadcast_in_dim.8), calls=%async_computation | async-start | bytes 1048576 | tf_op jit(solution)/shard_map/all_to_all | solution.py:295
  7.0 0.7 copy-done.1
  7.7 9.1 %collective-permute-start = (bf16[80,256]{1,0:T(8,128)(2,1)S(1)}, bf16[80,256]{1,0:T(8,128)(2,1)S(1)}, u32[]{:S(2)}, u32[]{:S(2)}) collective-permute-start(bf16[80,256]{1,0:T(8,128)(2,1)S(1)} %get-tuple-element.11), channel_id=1, source_target_pairs={{0,64},{16,80},{32,96},{48,112},{64,0},{80,16},{96,32},{112,48},{1... | collective-permute-start | bytes 122888 | tf_op jit(solution)/shard_map/ppermute | solution.py:288
  16.9 2.4 %collective-permute-done = bf16[80,256]{1,0:T(8,128)(2,1)S(1)} collective-permute-done((bf16[80,256]{1,0:T(8,128)(2,1)S(1)}, bf16[80,256]{1,0:T(8,128)(2,1)S(1)}, u32[]{:S(2)}, u32[]{:S(2)}) %collective-permute-start) | collective-permute-done | bytes 40992 | tf_op jit(solution)/shard_map/ppermute | solution.py:288
  19.3 1.9 %collective-permute-start.3 = (bf16[4,32,2048]{2,1,0:T(8,128)(2,1)S(1)}, bf16[4,32,2048]{2,1,0:T(8,128)(2,1)S(1)}, u32[]{:S(2)}, u32[]{:S(2)}) collective-permute-start(bf16[4,32,2048]{2,1,0:T(8,128)(2,1)S(1)} %all-to-all-done.refs_1_.own_ref), channel_id=1, source_target_pairs={{0,1},{1,0},{2,3},{3,2},{4,5},{5,4},{6,7},{7,6},{8,9},{9,8},{10,11... | collective-permute-start | bytes 1572872 | tf_op jit(solution)/shard_map/ppermute | solution.py:291
  21.2 5.2 %collective-permute-start.1 = (bf16[80,512]{1,0:T(8,128)(2,1)S(1)}, bf16[80,512]{1,0:T(8,128)(2,1)S(1)}, u32[]{:S(2)}, u32[]{:S(2)}) collective-permute-start(bf16[80,512]{1,0:T(8,128)(2,1)S(1)} %get-tuple-element.20), channel_id=1, source_target_pairs={{0,32},{16,48},{32,0},{48,16},{64,96},{80,112},{96,64},{112,80},{1... | collective-permute-start | bytes 245768 | tf_op jit(solution)/shard_map/ppermute | solution.py:288
  26.4 4.8 %collective-permute-done.1 = bf16[80,512]{1,0:T(8,128)(2,1)S(1)} collective-permute-done((bf16[80,512]{1,0:T(8,128)(2,1)S(1)}, bf16[80,512]{1,0:T(8,128)(2,1)S(1)}, u32[]{:S(2)}, u32[]{:S(2)}) %collective-permute-start.1) | collective-permute-done | bytes 81952 | tf_op jit(solution)/shard_map/ppermute | solution.py:288
  31.2 2.6 %collective-permute-start.2 = (bf16[80,1024]{1,0:T(8,128)(2,1)S(1)}, bf16[80,1024]{1,0:T(8,128)(2,1)S(1)}, u32[]{:S(2)}, u32[]{:S(2)}) collective-permute-start(bf16[80,1024]{1,0:T(8,128)(2,1)S(1)} %constant_dynamic-update-slice_fusion.2.refs_0_), channel_id=1, source_target_pairs={{0,16},{16,0},{32,48},{48,32},{64,80},{80,64},{96,112},{112,96},{1... | collective-permute-start | bytes 491528 | tf_op jit(solution)/shard_map/ppermute | solution.py:288
  33.9 5.0 %shard_map.69 = (bf16[1024,128]{1,0:T(8,128)(2,1)S(1)}, f32[4,2048]{1,0:T(4,128)S(1)}) custom-call(bf16[80,1024]{1,0:T(8,128)(2,1)S(1)} %constant_dynamic-update-slice_fusion.2.refs_0_, bf16[4,32,2048]{2,1,0:T(8,128)(2,1)S(1)} %all-to-all-done.refs_1_.own_ref, bf16[4,32,2048]{2,1,0:T(8,128)(2,1)S(1)} %collective-permute-done.3.refs_2_.other_ref), custom_call_target="tpu_custom_call" | custom-call | flops 2147483648 | bytes 4194304 | tf_op jit(solution)/shard_map/pallas_call | solution.py:253
  39.1 5.0 %shard_map.70 = (bf16[1024,128]{1,0:T(8,128)(2,1)S(1)}, f32[4,2560]{1,0:T(4,128)S(1)}) custom-call(bf16[80,1024]{1,0:T(8,128)(2,1)S(1)} %collective-permute-done.2.refs_0_, bf16[4,32,2048]{2,1,0:T(8,128)(2,1)S(1)} %all-to-all-done.refs_1_.own_ref, bf16[4,32,2048]{2,1,0:T(8,128)(2,1)S(1)} %collective-permute-done.3.refs_2_.other_ref, ...), custom_call_target="tpu_custom_call" | custom-call | flops 2147483648 | bytes 4194304 | tf_op jit(solution)/shard_map/pallas_call | solution.py:253
  44.2 10.7 %all_to_all.27.logw_ref = f32[4,4,2560]{2,1,0:T(4,128)S(1)} all-to-all(f32[4,4,2560]{2,1,0:T(4,128)S(1)} %broadcast_in_dim.9), channel_id=1, replica_groups={{0,128,256,384},{16,144,272,400},{32,160,288,416},{48,176,304,432},{64,..., dimensions={0} | all-to-all | bytes 327680 | tf_op jit(solution)/shard_map/all_to_all | solution.py:295
  55.0 10.0 %all_to_all.28 = f32[8,4,2048]{2,1,0:T(4,128)S(1)} all-to-all(f32[8,4,2048]{2,1,0:T(4,128)S(1)} %broadcast_in_dim.10), channel_id=1, replica_groups={{0,1,2,3,4,5,6,7},{8,9,10,11,12,13,14,15},{16,17,18,19,20,21,22,23},{24..., dimensions={0} | all-to-all | bytes 524288 | tf_op jit(solution)/shard_map/all_to_all | solution.py:295
  65.3 14.1 %collective-permute-start.4 = (f32[4,2048]{1,0:T(4,128)S(1)}, f32[4,2048]{1,0:T(4,128)S(1)}, u32[]{:S(2)}, u32[]{:S(2)}) collective-permute-start(f32[4,2048]{1,0:T(4,128)S(1)} %log_add_fusion.1), channel_id=1, source_target_pairs={{0,8},{1,9},{2,10},{3,11},{4,12},{5,13},{6,14},{7,15},{8,0},{9,1},... | collective-permute-start | bytes 98312 | tf_op jit(solution)/shard_map/ppermute | solution.py:291
  79.5 1.8 %collective-permute-done.4 = f32[4,2048]{1,0:T(4,128)S(1)} collective-permute-done((f32[4,2048]{1,0:T(4,128)S(1)}, f32[4,2048]{1,0:T(4,128)S(1)}, u32[]{:S(2)}, u32[]{:S(2)}) %collective-permute-start.4) | collective-permute-done | bytes 32800 | tf_op jit(solution)/shard_map/ppermute | solution.py:291
  81.2 33.7 %shard_map.71 = f32[4,256]{1,0:T(4,128)S(1)} custom-call(s32[1]{0:T(128)} %bitcast.8.place_ref, bf16[1024,128]{1,0:T(8,128)(2,1)S(1)} %get-tuple-element.17.near_ref, bf16[1024,128]{1,0:T(8,128)(2,1)S(1)} %get-tuple-element.16.far_ref, bf16[4,32,2048]{2,1,0:T(8,128)(2,1)S(1)} %all-to-all-done.refs_1_.own_ref, ...), custom_call_target="tpu_custom_call" | custom-call | flops 2147483648 | bytes 4194304 | tf_op jit(solution)/shard_map/pallas_call | solution.py:253
  115.0 7.0 %collective-permute-start.5 = (f32[4,256]{1,0:T(4,128)S(1)}, f32[4,256]{1,0:T(4,128)S(1)}, u32[]{:S(2)}, u32[]{:S(2)}) collective-permute-start(f32[4,256]{1,0:T(4,128)S(1)} %shard_map.71), channel_id=1, source_target_pairs={{0,64},{16,80},{32,96},{48,112},{64,0},{80,16},{96,32},{112,48},{1... | collective-permute-start | bytes 12296 | tf_op jit(solution)/shard_map/ppermute | solution.py:288
  122.0 33.7 %shard_map.72 = f32[4,256]{1,0:T(4,128)S(1)} custom-call(s32[1]{0:T(128)} %bitcast.8.place_ref, bf16[1024,128]{1,0:T(8,128)(2,1)S(1)} %get-tuple-element.17.near_ref, bf16[1024,128]{1,0:T(8,128)(2,1)S(1)} %get-tuple-element.16.far_ref, bf16[4,32,2048]{2,1,0:T(8,128)(2,1)S(1)} %all-to-all-done.refs_1_.own_ref, ...), custom_call_target="tpu_custom_call" | custom-call | flops 2147483648 | bytes 4194304 | tf_op jit(solution)/shard_map/pallas_call | solution.py:253
  155.7 0.6 copy.11
  156.3 4.2 %all-to-all-start.3 = ((f32[4,1,256]{2,1,0:T(1,128)}), f32[4,1,256]{2,1,0:T(1,128)S(1)}, u32[]{:S(2)}, u32[]{:S(2)}) async-start(f32[4,1,256]{2,1,0:T(1,128)} %copy.11), calls=%async_computation.3 | async-start | bytes 8192 | tf_op jit(solution)/shard_map/all_to_all | solution.py:382
  160.5 0.6 subtract_multiply_fusion
  161.1 5.0 %all-to-all-done.3 = f32[4,1,256]{2,1,0:T(1,128)S(1)} async-done(((f32[4,1,256]{2,1,0:T(1,128)}), f32[4,1,256]{2,1,0:T(1,128)S(1)}, u32[]{:S(2)}, u32[]{:S(2)}) %all-to-all-start.3) | async-done | bytes 4128 | tf_op jit(solution)/shard_map/all_to_all | solution.py:382
  166.1 0.6 subtract_multiply_fusion.1
  (30 shorter events, 0.8 us)
Async XLA Ops:
  2.4 4.6 %copy-start = (bf16[256,64]{0,1:T(8,128)(2,1)S(1)}, bf16[256,64]{0,1:T(8,128)(2,1)}, u32[]{:S(2)}) copy-start(bf16[256,64]{0,1:T(8,128)(2,1)} %param.7) | copy-start | bytes 98308
  2.4 4.6 %copy-start.2 = (f32[256]{0:T(256)S(1)}, f32[256]{0:T(256)}, u32[]{:S(2)}) copy-start(f32[256]{0:T(256)} %param.9) | copy-start | bytes 3076
  2.4 16.8 %all-to-all-start = ((bf16[4,32,2048]{2,1,0:T(8,128)(2,1)}), bf16[4,32,2048]{2,1,0:T(8,128)(2,1)S(1)}, u32[]{:S(2)}, u32[]{:S(2)}) async-start(bf16[4,32,2048]{2,1,0:T(8,128)(2,1)} %broadcast_in_dim.8), calls=%async_computation | async-start | bytes 1048576 | tf_op jit(solution)/shard_map/all_to_all | solution.py:295
  7.0 0.7 copy-start.1
  7.7 11.5 %collective-permute-start = (bf16[80,256]{1,0:T(8,128)(2,1)S(1)}, bf16[80,256]{1,0:T(8,128)(2,1)S(1)}, u32[]{:S(2)}, u32[]{:S(2)}) collective-permute-start(bf16[80,256]{1,0:T(8,128)(2,1)S(1)} %get-tuple-element.11), channel_id=1, source_target_pairs={{0,64},{16,80},{32,96},{48,112},{64,0},{80,16},{96,32},{112,48},{1... | collective-permute-start | bytes 122888 | tf_op jit(solution)/shard_map/ppermute | solution.py:288
  19.3 14.6 %collective-permute-start.3 = (bf16[4,32,2048]{2,1,0:T(8,128)(2,1)S(1)}, bf16[4,32,2048]{2,1,0:T(8,128)(2,1)S(1)}, u32[]{:S(2)}, u32[]{:S(2)}) collective-permute-start(bf16[4,32,2048]{2,1,0:T(8,128)(2,1)S(1)} %all-to-all-done.refs_1_.own_ref), channel_id=1, source_target_pairs={{0,1},{1,0},{2,3},{3,2},{4,5},{5,4},{6,7},{7,6},{8,9},{9,8},{10,11... | collective-permute-start | bytes 1572872 | tf_op jit(solution)/shard_map/ppermute | solution.py:291
  21.2 10.0 %collective-permute-start.1 = (bf16[80,512]{1,0:T(8,128)(2,1)S(1)}, bf16[80,512]{1,0:T(8,128)(2,1)S(1)}, u32[]{:S(2)}, u32[]{:S(2)}) collective-permute-start(bf16[80,512]{1,0:T(8,128)(2,1)S(1)} %get-tuple-element.20), channel_id=1, source_target_pairs={{0,32},{16,48},{32,0},{48,16},{64,96},{80,112},{96,64},{112,80},{1... | collective-permute-start | bytes 245768 | tf_op jit(solution)/shard_map/ppermute | solution.py:288
  31.2 7.9 %copy-start.3 = (f32[2048]{0:T(1024)S(1)}, f32[2048]{0:T(1024)}, u32[]{:S(2)}) copy-start(f32[2048]{0:T(1024)} %param.6) | copy-start | bytes 24580
  31.2 7.9 %collective-permute-start.2 = (bf16[80,1024]{1,0:T(8,128)(2,1)S(1)}, bf16[80,1024]{1,0:T(8,128)(2,1)S(1)}, u32[]{:S(2)}, u32[]{:S(2)}) collective-permute-start(bf16[80,1024]{1,0:T(8,128)(2,1)S(1)} %constant_dynamic-update-slice_fusion.2.refs_0_), channel_id=1, source_target_pairs={{0,16},{16,0},{32,48},{48,32},{64,80},{80,64},{96,112},{112,96},{1... | collective-permute-start | bytes 491528 | tf_op jit(solution)/shard_map/ppermute | solution.py:288
  65.1 14.2 %copy-start.4 = (bf16[2048,64]{0,1:T(8,128)(2,1)S(1)}, bf16[2048,64]{0,1:T(8,128)(2,1)}, u32[]{:S(2)}) copy-start(bf16[2048,64]{0,1:T(8,128)(2,1)} %param.5) | copy-start | bytes 786436
  65.3 15.9 %collective-permute-start.4 = (f32[4,2048]{1,0:T(4,128)S(1)}, f32[4,2048]{1,0:T(4,128)S(1)}, u32[]{:S(2)}, u32[]{:S(2)}) collective-permute-start(f32[4,2048]{1,0:T(4,128)S(1)} %log_add_fusion.1), channel_id=1, source_target_pairs={{0,8},{1,9},{2,10},{3,11},{4,12},{5,13},{6,14},{7,15},{8,0},{9,1},... | collective-permute-start | bytes 98312 | tf_op jit(solution)/shard_map/ppermute | solution.py:291
  115.0 40.7 %collective-permute-start.5 = (f32[4,256]{1,0:T(4,128)S(1)}, f32[4,256]{1,0:T(4,128)S(1)}, u32[]{:S(2)}, u32[]{:S(2)}) collective-permute-start(f32[4,256]{1,0:T(4,128)S(1)} %shard_map.71), channel_id=1, source_target_pairs={{0,64},{16,80},{32,96},{48,112},{64,0},{80,16},{96,32},{112,48},{1... | collective-permute-start | bytes 12296 | tf_op jit(solution)/shard_map/ppermute | solution.py:288
  156.3 9.8 %all-to-all-start.3 = ((f32[4,1,256]{2,1,0:T(1,128)}), f32[4,1,256]{2,1,0:T(1,128)S(1)}, u32[]{:S(2)}, u32[]{:S(2)}) async-start(f32[4,1,256]{2,1,0:T(1,128)} %copy.11), calls=%async_computation.3 | async-start | bytes 8192 | tf_op jit(solution)/shard_map/all_to_all | solution.py:382

commit v6 on v5

--- a/solution.py
+++ b/solution.py
@@ -39,24 +39,30 @@
     return one, one, one
 
 
-def prepare_kernel(core_ref, y_ref, logw_ref, potential_ref, out_ref, offset_ref):
+def prepare_kernel(y_ref, logw_ref, potential_ref, out_ref, offset_ref):
     y = y_ref[...].astype(jnp.float32)
     offset = potential_ref[...] * 2.0 + logw_ref[...]
     bias = offset - jnp.sum(y * y, axis=0, keepdims=True)
-    half = FEATURES // 2
-    first, second = y[0:half, :] * 2.0, y[half:FEATURES, :] * 2.0
-    swap = core_ref[0] != 0
-    out_ref[0:half, :] = jnp.where(swap, second, first).astype(jnp.bfloat16)
-    out_ref[half:FEATURES, :] = jnp.where(swap, first, second).astype(jnp.bfloat16)
+    out_ref[0:FEATURES, :] = (y * 2.0).astype(jnp.bfloat16)
     out_ref[FEATURES : FEATURES + EXTRA, :] = extra_block(
         three_parts(bias), ones_of(bias.shape[1])
     ).astype(jnp.bfloat16)
     offset_ref[...] = offset
 
 
-def weights_of(own_ref, other_ref, r, at, extra):
-    rest = jnp.zeros((DEPTH - FEATURES - EXTRA, extra.shape[1]), extra.dtype)
-    return jnp.concatenate([own_ref[r, :, at], other_ref[r, :, at], extra, rest], axis=0)
+def copies_kernel(x_ref, out_ref, sem):
+    moves = [
+        pltpu.make_async_copy(x_ref, out_ref.at[k], sem.at[k]) for k in range(out_ref.shape[0])
+    ]
+    for move in moves:
+        move.start()
+    for move in moves:
+        move.wait()
+
+
+def weights_of(features, extra):
+    rest = jnp.zeros((DEPTH - FEATURES - EXTRA, features.shape[1]), features.dtype)
+    return jnp.concatenate([features, extra, rest], axis=0)
 
 
 def product(a, b):
@@ -74,12 +80,12 @@
 
 
 def first_kernel(last, *refs):
-    y_ref, own_ref, other_ref, refs = refs[0], refs[1], refs[2], refs[3:]
+    y_ref, x_ref, refs = refs[0], refs[1], refs[2:]
     if last:
         before_ref, logw_ref, refs = refs[0], refs[1], refs[2:]
     yt_ref, l_ref, sums_ref = refs
     rows = yt_ref.shape[0]
-    ny, _, per = own_ref.shape
+    ny, _, per = x_ref.shape
     row_step = min(ROWS, rows)
     col_step = min(LANES, per)
     together = 2
@@ -114,7 +120,7 @@
         for s in range(together):
             r = g * together + s
             for t in range(0, per, col_step):
-                weights = weights_of(own_ref, other_ref, r, slice(t, t + col_step), extra)
+                weights = weights_of(x_ref[r, :, t : t + col_step], extra)
                 total = jnp.zeros((8, col_step), jnp.float32)
                 for j in range(0, rows, row_step):
                     score = product(yt_ref[j : j + row_step, :], weights)
@@ -133,7 +139,7 @@
         def again(g, carry):
             at = pl.ds(pl.multiple_of(g * col_step, col_step), col_step)
             for r in range(ny):
-                weights = weights_of(own_ref, other_ref, r, at, extra)
+                weights = weights_of(x_ref[r, :, at], extra)
 
                 def advance(j, state):
                     top, total = state
@@ -163,8 +169,7 @@
     place_ref,
     near_ref,
     far_ref,
-    own_ref,
-    other_ref,
+    x_ref,
     total_ref,
     logw_ref,
     s_ref,
@@ -175,7 +180,7 @@
 ):
     nz, each = s_ref.shape
     rows = nz * each
-    ny, _, per = own_ref.shape
+    ny, _, per = x_ref.shape
     row_step = min(ROWS, rows)
     col_step = min(LANES, per)
 
@@ -199,7 +204,7 @@
         for r in range(ny):
             for t in range(0, per, col_step):
                 at = slice(t, t + col_step)
-                score = product(left, weights_of(own_ref, other_ref, r, at, extra_ref[r, :, at]))
+                score = product(left, weights_of(x_ref[r, :, at], extra_ref[r, :, at]))
                 part = lanes_folded(jnp.exp(score), jnp.add)
                 if r == 0 and t == 0:
                     acc_ref[here, :] = part
@@ -230,7 +235,7 @@
                 def advance(t, state):
                     top, total = state
                     at = pl.ds(pl.multiple_of(t * col_step, col_step), col_step)
-                    score = product(left, weights_of(own_ref, other_ref, r, at, extra_ref[r, :, at]))
+                    score = product(left, weights_of(x_ref[r, :, at], extra_ref[r, :, at]))
                     new = jnp.maximum(top, lanes_folded(score, jnp.maximum))
                     total = total * jnp.exp(top - new)
                     for k in range(col_step // 128):
@@ -249,15 +254,16 @@
         store(top + jnp.log(total))
 
 
-def call(kernel, outs, scratch, flops, exps, *args, spaces=None):
+def call(kernel, outs, scratch, flops, exps, *args, spaces=None, out=None, limit=40):
     return pl.pallas_call(
         kernel,
         out_shape=outs,
         in_specs=[
             pl.BlockSpec(memory_space=space) for space in spaces or [pltpu.VMEM] * len(args)
         ],
+        out_specs=jax.tree.map(lambda _: pl.BlockSpec(memory_space=out or pltpu.VMEM), outs),
         scratch_shapes=scratch,
-        compiler_params=pltpu.CompilerParams(vmem_limit_bytes=40 * 2**20),
+        compiler_params=pltpu.CompilerParams(vmem_limit_bytes=limit * 2**20),
         cost_estimate=pl.CostEstimate(
             flops=flops, bytes_accessed=4 * 2**20, transcendentals=exps
         ),
@@ -277,7 +283,6 @@
     pairs = cols * half
     place = lax.axis_index("blk")
     my_y, my_z = place // nz, place % nz
-    core = (lax.axis_index("wide") % 2).astype(jnp.int32)
     depth = FEATURES + EXTRA
     y_groups = [[y * nz + z for y in range(ny)] for z in range(nz)]
     quarters = [[g * (nz // 2) + z for z in range(nz // 2)] for g in range(2 * ny)]
@@ -300,21 +305,26 @@
         [],
         each * FEATURES * 4,
         0,
-        core.reshape(1),
         target_latent.T,
         target_logw.reshape(1, each),
         target_potential.reshape(1, each),
-        spaces=[pltpu.SMEM] + [pltpu.VMEM] * 3,
     )
     x = source_latent.T
-    part = lax.dynamic_slice(x, (core * (FEATURES // 2), 0), (FEATURES // 2, per))
-    own = shared(part, "blk", y_groups)
+    copies = call(
+        copies_kernel,
+        jax.ShapeDtypeStruct((ny, FEATURES, per), bf16),
+        [pltpu.SemaphoreType.DMA((ny,))],
+        0,
+        0,
+        x,
+        spaces=[pl.ANY],
+        out=pl.ANY,
+        limit=60,
+    )
+    xs = lax.all_to_all(copies, "blk", 0, 0, axis_index_groups=y_groups, tiled=True)
     bit = nz // 2
     while bit > 1:
         y = jnp.concatenate([y, along_z(y, bit)], axis=1)
-        if bit == nz // 2:
-            own, _ = lax.optimization_barrier((own, y))
-            other = along_wide(own, 1)
         bit //= 2
     far = along_z(y, 1)
 
@@ -330,8 +340,7 @@
             2 * pairs * DEPTH,
             pairs,
             block,
-            own,
-            other,
+            xs,
             *more,
         )
 
@@ -368,11 +377,10 @@
             place_in,
             near,
             yt_far,
-            own,
-            other,
+            xs,
             total,
             got,
-            spaces=[pltpu.SMEM] + [pltpu.VMEM] * 6,
+            spaces=[pltpu.SMEM] + [pltpu.VMEM] * 5,
         )
 
     sent = second(tuple((h, k, a - count) for h, k, a in blocks if a >= count), yt_near)

time: 168 us -> 195 us (1.16)
  Pallas kernels: 77.4 us -> 110 us
  starting transfers between devices: 48.7 us -> 46.1 us
    pallas_call x5 -> x6, Pallas kernels: 77.4 us -> 110 us  [call(): pl.pallas_call(kernel, out_shape=outs, in_specs=[pl.BlockSpec(memory_spac...]
    ppermute x2 -> x1, starting transfers between devices: 16 us -> 13.6 us  [along_wide(): return lax.ppermute(value, 'wide', [(w, w ^ k) for w in range(nw)])]
  transfers between devices with their start and end apart: 8 -> 7, of which waited for: 5 -> 5; matrix products, arithmetic and copies ran while one was open for 0% -> 0% of each run, Pallas kernels for 23% -> 20%
where the time goes in v6:
time: 195 us; the launch traced here: 194 us
  Pallas kernels  110 us (56%)
  starting transfers between devices  46.1 us (24%)
  blocking collectives  20.7 us (11%)
  waiting for transfers between devices  13.3 us (7%)
    pallas_call x6, Pallas kernels, call(): pl.pallas_call(kernel, out_shape=outs, in_specs=[pl.BlockSpec(memory_spac...  110 us
    ppermute x4, starting transfers between devices, along_z(): return lax.ppermute(value, 'blk', perm)  23.4 us
    all_to_all x2, blocking collectives, shared(): lax.all_to_all(spread, axis, 0, 0, axis_index_groups=groups, tiled=True)  20.7 us
    ppermute x1, starting transfers between devices, along_wide(): return lax.ppermute(value, 'wide', [(w, w ^ k) for w in range(nw)])  13.6 us
    ppermute x4, waiting for transfers between devices, along_z(): return lax.ppermute(value, 'blk', perm)  6.56 us
    all_to_all x1, waiting for transfers between devices, per_device(): lax.all_to_all(sums, 'blk', 0, 0, axis_index_groups=quarters, tiled=True)  4.96 us
    all_to_all x1, starting transfers between devices, per_device(): lax.all_to_all(sums, 'blk', 0, 0, axis_index_groups=quarters, tiled=True)  4.72 us
    all_to_all x1, starting transfers between devices, per_device(): lax.all_to_all(copies, 'blk', 0, 0, axis_index_groups=y_groups, tiled=True)  4.48 us
  transfers between devices with their start and end apart: 7, of which 5 were waited for; matrix products, arithmetic and copies ran while one was open for 0% of the time, Pallas kernels for 20%

profile of v6, /device:TPU:6, one launch (start us, length us, event | category | flops | bytes accessed | tf_op | source)
XLA Modules:
  0.0 194.3 jit_solution(7820098641987384271)
XLA Ops:
  0.6 32.9 %shard_map.69 = bf16[4,64,2048]{2,1,0:T(8,128)(2,1)} custom-call(bf16[64,2048]{1,0:T(8,128)(2,1)} %bitcast.23), custom_call_target="tpu_custom_call" | custom-call | bytes 4194304 | tf_op jit(solution)/shard_map/pallas_call | solution.py:258
  33.6 4.5 %all-to-all-start = ((bf16[4,64,2048]{2,1,0:T(8,128)(2,1)}), bf16[4,64,2048]{2,1,0:T(8,128)(2,1)S(1)}, u32[]{:S(2)}, u32[]{:S(2)}) async-start(bf16[4,64,2048]{2,1,0:T(8,128)(2,1)} %shard_map.69), calls=%async_computation | async-start | bytes 2097152 | tf_op jit(solution)/shard_map/all_to_all | solution.py:324
  38.0 0.7 copy-done.1
  38.8 9.1 %collective-permute-start = (bf16[80,256]{1,0:T(8,128)(2,1)S(1)}, bf16[80,256]{1,0:T(8,128)(2,1)S(1)}, u32[]{:S(2)}, u32[]{:S(2)}) collective-permute-start(bf16[80,256]{1,0:T(8,128)(2,1)S(1)} %get-tuple-element.10), channel_id=1, source_target_pairs={{0,64},{16,80},{32,96},{48,112},{64,0},{80,16},{96,32},{112,48},{1... | collective-permute-start | bytes 122888 | tf_op jit(solution)/shard_map/ppermute | solution.py:293
  47.9 2.4 %collective-permute-done = bf16[80,256]{1,0:T(8,128)(2,1)S(1)} collective-permute-done((bf16[80,256]{1,0:T(8,128)(2,1)S(1)}, bf16[80,256]{1,0:T(8,128)(2,1)S(1)}, u32[]{:S(2)}, u32[]{:S(2)}) %collective-permute-start) | collective-permute-done | bytes 40992 | tf_op jit(solution)/shard_map/ppermute | solution.py:293
  50.3 5.2 %collective-permute-start.1 = (bf16[80,512]{1,0:T(8,128)(2,1)S(1)}, bf16[80,512]{1,0:T(8,128)(2,1)S(1)}, u32[]{:S(2)}, u32[]{:S(2)}) collective-permute-start(bf16[80,512]{1,0:T(8,128)(2,1)S(1)} %pad_maximum_fusion), channel_id=1, source_target_pairs={{0,32},{16,48},{32,0},{48,16},{64,96},{80,112},{96,64},{112,80},{1... | collective-permute-start | bytes 245768 | tf_op jit(solution)/shard_map/ppermute | solution.py:293
  55.5 4.1 %collective-permute-done.1 = bf16[80,512]{1,0:T(8,128)(2,1)S(1)} collective-permute-done((bf16[80,512]{1,0:T(8,128)(2,1)S(1)}, bf16[80,512]{1,0:T(8,128)(2,1)S(1)}, u32[]{:S(2)}, u32[]{:S(2)}) %collective-permute-start.1) | collective-permute-done | bytes 81952 | tf_op jit(solution)/shard_map/ppermute | solution.py:293
  59.5 2.1 %collective-permute-start.2 = (bf16[80,1024]{1,0:T(8,128)(2,1)S(1)}, bf16[80,1024]{1,0:T(8,128)(2,1)S(1)}, u32[]{:S(2)}, u32[]{:S(2)}) collective-permute-start(bf16[80,1024]{1,0:T(8,128)(2,1)S(1)} %constant_dynamic-update-slice_fusion.refs_0_), channel_id=1, source_target_pairs={{0,16},{16,0},{32,48},{48,32},{64,80},{80,64},{96,112},{112,96},{1... | collective-permute-start | bytes 491528 | tf_op jit(solution)/shard_map/ppermute | solution.py:293
  61.7 5.0 %shard_map.70 = (bf16[1024,128]{1,0:T(8,128)(2,1)S(1)}, f32[4,2048]{1,0:T(4,128)S(1)}) custom-call(bf16[80,1024]{1,0:T(8,128)(2,1)S(1)} %constant_dynamic-update-slice_fusion.refs_0_, bf16[4,64,2048]{2,1,0:T(8,128)(2,1)S(1)} %all-to-all-done.refs_1_.x_ref), custom_call_target="tpu_custom_call" | custom-call | flops 2147483648 | bytes 4194304 | tf_op jit(solution)/shard_map/pallas_call | solution.py:258
  66.7 0.1 collective-permute-done.2.refs_0_
  66.8 5.0 %shard_map.71 = (bf16[1024,128]{1,0:T(8,128)(2,1)S(1)}, f32[4,2560]{1,0:T(4,128)S(1)}) custom-call(bf16[80,1024]{1,0:T(8,128)(2,1)S(1)} %collective-permute-done.2.refs_0_, bf16[4,64,2048]{2,1,0:T(8,128)(2,1)S(1)} %all-to-all-done.refs_1_.x_ref, f32[4,2048]{1,0:T(4,128)S(1)} %get-tuple-element.11.refs_2_, f32[1,2048]{1,0:T(1,128)S(1)} %bitcast.22), custom_call_target="tpu_custom_call" | custom-call | flops 2147483648 | bytes 4194304 | tf_op jit(solution)/shard_map/pallas_call | solution.py:258
  71.8 10.6 %all_to_all.27.logw_ref = f32[4,4,2560]{2,1,0:T(4,128)S(1)} all-to-all(f32[4,4,2560]{2,1,0:T(4,128)S(1)} %broadcast_in_dim.6), channel_id=1, replica_groups={{0,128,256,384},{16,144,272,400},{32,160,288,416},{48,176,304,432},{64,..., dimensions={0} | all-to-all | bytes 327680 | tf_op jit(solution)/shard_map/all_to_all | solution.py:300
  82.5 10.1 %all_to_all.28 = f32[8,4,2048]{2,1,0:T(4,128)S(1)} all-to-all(f32[8,4,2048]{2,1,0:T(4,128)S(1)} %broadcast_in_dim.7), channel_id=1, replica_groups={{0,1,2,3,4,5,6,7},{8,9,10,11,12,13,14,15},{16,17,18,19,20,21,22,23},{24..., dimensions={0} | all-to-all | bytes 524288 | tf_op jit(solution)/shard_map/all_to_all | solution.py:300
  92.6 0.1 exponential_reduce_fusion
  92.8 13.6 %collective-permute-start.3 = (f32[4,2048]{1,0:T(4,128)S(1)}, f32[4,2048]{1,0:T(4,128)S(1)}, u32[]{:S(2)}, u32[]{:S(2)}) collective-permute-start(f32[4,2048]{1,0:T(4,128)S(1)} %log_add_fusion.1), channel_id=1, source_target_pairs={{0,8},{1,9},{2,10},{3,11},{4,12},{5,13},{6,14},{7,15},{8,0},{9,1},... | collective-permute-start | bytes 98312 | tf_op jit(solution)/shard_map/ppermute | solution.py:296
  106.5 1.8 collective-permute-done.3
  108.3 33.7 %shard_map.72 = f32[4,256]{1,0:T(4,128)S(1)} custom-call(s32[1]{0:T(128)} %bitcast.7.place_ref, bf16[1024,128]{1,0:T(8,128)(2,1)S(1)} %get-tuple-element.15.near_ref, bf16[1024,128]{1,0:T(8,128)(2,1)S(1)} %get-tuple-element.14.far_ref, bf16[4,64,2048]{2,1,0:T(8,128)(2,1)S(1)} %all-to-all-done.refs_1_.x_ref, f32[4,2048]{1,0:T(4,128)S(1)} %log_add_fusion.total_ref, ...), custom_call_target="tpu_custom_call" | custom-call | flops 2147483648 | bytes 4194304 | tf_op jit(solution)/shard_map/pallas_call | solution.py:258
  142.0 7.0 %collective-permute-start.4 = (f32[4,256]{1,0:T(4,128)S(1)}, f32[4,256]{1,0:T(4,128)S(1)}, u32[]{:S(2)}, u32[]{:S(2)}) collective-permute-start(f32[4,256]{1,0:T(4,128)S(1)} %shard_map.72), channel_id=1, source_target_pairs={{0,64},{16,80},{32,96},{48,112},{64,0},{80,16},{96,32},{112,48},{1... | collective-permute-start | bytes 12296 | tf_op jit(solution)/shard_map/ppermute | solution.py:293
  149.0 33.7 %shard_map.73 = f32[4,256]{1,0:T(4,128)S(1)} custom-call(s32[1]{0:T(128)} %bitcast.7.place_ref, bf16[1024,128]{1,0:T(8,128)(2,1)S(1)} %get-tuple-element.15.near_ref, bf16[1024,128]{1,0:T(8,128)(2,1)S(1)} %get-tuple-element.14.far_ref, bf16[4,64,2048]{2,1,0:T(8,128)(2,1)S(1)} %all-to-all-done.refs_1_.x_ref, f32[4,2048]{1,0:T(4,128)S(1)} %log_add_fusion.total_ref, ...), custom_call_target="tpu_custom_call" | custom-call | flops 2147483648 | bytes 4194304 | tf_op jit(solution)/shard_map/pallas_call | solution.py:258
  182.8 0.6 copy.11
  183.4 4.7 %all-to-all-start.3 = ((f32[4,1,256]{2,1,0:T(1,128)}), f32[4,1,256]{2,1,0:T(1,128)S(1)}, u32[]{:S(2)}, u32[]{:S(2)}) async-start(f32[4,1,256]{2,1,0:T(1,128)} %copy.11), calls=%async_computation.3 | async-start | bytes 8192 | tf_op jit(solution)/shard_map/all_to_all | solution.py:390
  188.1 0.6 subtract_multiply_fusion
  188.7 5.0 %all-to-all-done.3 = f32[4,1,256]{2,1,0:T(1,128)S(1)} async-done(((f32[4,1,256]{2,1,0:T(1,128)}), f32[4,1,256]{2,1,0:T(1,128)S(1)}, u32[]{:S(2)}, u32[]{:S(2)}) %all-to-all-start.3) | async-done | bytes 4128 | tf_op jit(solution)/shard_map/all_to_all | solution.py:390
  193.7 0.6 subtract_multiply_fusion.1
  (28 shorter events, 0.5 us)
Async XLA Ops:
  33.5 4.5 %copy-start = (bf16[256,64]{0,1:T(8,128)(2,1)S(1)}, bf16[256,64]{0,1:T(8,128)(2,1)}, u32[]{:S(2)}) copy-start(bf16[256,64]{0,1:T(8,128)(2,1)} %param.7) | copy-start | bytes 98308
  33.6 4.5 %copy-start.2 = (f32[256]{0:T(256)S(1)}, f32[256]{0:T(256)}, u32[]{:S(2)}) copy-start(f32[256]{0:T(256)} %param.9) | copy-start | bytes 3076
  33.6 28.1 %all-to-all-start = ((bf16[4,64,2048]{2,1,0:T(8,128)(2,1)}), bf16[4,64,2048]{2,1,0:T(8,128)(2,1)S(1)}, u32[]{:S(2)}, u32[]{:S(2)}) async-start(bf16[4,64,2048]{2,1,0:T(8,128)(2,1)} %shard_map.69), calls=%async_computation | async-start | bytes 2097152 | tf_op jit(solution)/shard_map/all_to_all | solution.py:324
  38.0 0.7 copy-start.1
  38.8 11.5 %collective-permute-start = (bf16[80,256]{1,0:T(8,128)(2,1)S(1)}, bf16[80,256]{1,0:T(8,128)(2,1)S(1)}, u32[]{:S(2)}, u32[]{:S(2)}) collective-permute-start(bf16[80,256]{1,0:T(8,128)(2,1)S(1)} %get-tuple-element.10), channel_id=1, source_target_pairs={{0,64},{16,80},{32,96},{48,112},{64,0},{80,16},{96,32},{112,48},{1... | collective-permute-start | bytes 122888 | tf_op jit(solution)/shard_map/ppermute | solution.py:293
  50.3 9.3 %collective-permute-start.1 = (bf16[80,512]{1,0:T(8,128)(2,1)S(1)}, bf16[80,512]{1,0:T(8,128)(2,1)S(1)}, u32[]{:S(2)}, u32[]{:S(2)}) collective-permute-start(bf16[80,512]{1,0:T(8,128)(2,1)S(1)} %pad_maximum_fusion), channel_id=1, source_target_pairs={{0,32},{16,48},{32,0},{48,16},{64,96},{80,112},{96,64},{112,80},{1... | collective-permute-start | bytes 245768 | tf_op jit(solution)/shard_map/ppermute | solution.py:293
  59.5 7.2 %copy-start.3 = (f32[2048]{0:T(1024)S(1)}, f32[2048]{0:T(1024)}, u32[]{:S(2)}) copy-start(f32[2048]{0:T(1024)} %param.6) | copy-start | bytes 24580
  59.5 7.2 %collective-permute-start.2 = (bf16[80,1024]{1,0:T(8,128)(2,1)S(1)}, bf16[80,1024]{1,0:T(8,128)(2,1)S(1)}, u32[]{:S(2)}, u32[]{:S(2)}) collective-permute-start(bf16[80,1024]{1,0:T(8,128)(2,1)S(1)} %constant_dynamic-update-slice_fusion.refs_0_), channel_id=1, source_target_pairs={{0,16},{16,0},{32,48},{48,32},{64,80},{80,64},{96,112},{112,96},{1... | collective-permute-start | bytes 491528 | tf_op jit(solution)/shard_map/ppermute | solution.py:293
  92.6 13.7 %copy-start.4 = (bf16[2048,64]{0,1:T(8,128)(2,1)S(1)}, bf16[2048,64]{0,1:T(8,128)(2,1)}, u32[]{:S(2)}) copy-start(bf16[2048,64]{0,1:T(8,128)(2,1)} %param.5) | copy-start | bytes 786436
  92.8 15.5 %collective-permute-start.3 = (f32[4,2048]{1,0:T(4,128)S(1)}, f32[4,2048]{1,0:T(4,128)S(1)}, u32[]{:S(2)}, u32[]{:S(2)}) collective-permute-start(f32[4,2048]{1,0:T(4,128)S(1)} %log_add_fusion.1), channel_id=1, source_target_pairs={{0,8},{1,9},{2,10},{3,11},{4,12},{5,13},{6,14},{7,15},{8,0},{9,1},... | collective-permute-start | bytes 98312 | tf_op jit(solution)/shard_map/ppermute | solution.py:296
  142.0 40.7 %collective-permute-start.4 = (f32[4,256]{1,0:T(4,128)S(1)}, f32[4,256]{1,0:T(4,128)S(1)}, u32[]{:S(2)}, u32[]{:S(2)}) collective-permute-start(f32[4,256]{1,0:T(4,128)S(1)} %shard_map.72), channel_id=1, source_target_pairs={{0,64},{16,80},{32,96},{48,112},{64,0},{80,16},{96,32},{112,48},{1... | collective-permute-start | bytes 12296 | tf_op jit(solution)/shard_map/ppermute | solution.py:293
  183.4 10.3 %all-to-all-start.3 = ((f32[4,1,256]{2,1,0:T(1,128)}), f32[4,1,256]{2,1,0:T(1,128)S(1)}, u32[]{:S(2)}, u32[]{:S(2)}) async-start(f32[4,1,256]{2,1,0:T(1,128)} %copy.11), calls=%async_computation.3 | async-start | bytes 8192 | tf_op jit(solution)/shard_map/all_to_all | solution.py:390

commit v7 on v6

--- a/solution.py
+++ b/solution.py
@@ -39,7 +39,23 @@
     return one, one, one
 
 
-def prepare_kernel(y_ref, logw_ref, potential_ref, out_ref, offset_ref):
+def prepare_kernel(
+    x_in, y_in, logw_in, potential_in, out_ref, offset_ref, copies_ref, x_ref, y_ref, logw_ref, potential_ref, sem
+):
+    count = copies_ref.shape[0]
+    pairs = [(x_in, x_ref), (y_in, y_ref), (logw_in, logw_ref), (potential_in, potential_ref)]
+    pairs += [(x_ref, copies_ref.at[k]) for k in range(count)]
+    moves = [
+        pltpu.make_async_copy(source, target, sem.at[k])
+        for k, (source, target) in enumerate(pairs)
+    ]
+    for move in moves[:4]:
+        move.start()
+    moves[0].wait()
+    for move in moves[4:]:
+        move.start()
+    for move in moves[1:4]:
+        move.wait()
     y = y_ref[...].astype(jnp.float32)
     offset = potential_ref[...] * 2.0 + logw_ref[...]
     bias = offset - jnp.sum(y * y, axis=0, keepdims=True)
@@ -48,15 +64,7 @@
         three_parts(bias), ones_of(bias.shape[1])
     ).astype(jnp.bfloat16)
     offset_ref[...] = offset
-
-
-def copies_kernel(x_ref, out_ref, sem):
-    moves = [
-        pltpu.make_async_copy(x_ref, out_ref.at[k], sem.at[k]) for k in range(out_ref.shape[0])
-    ]
-    for move in moves:
-        move.start()
-    for move in moves:
+    for move in moves[4:]:
         move.wait()
 
 
@@ -255,13 +263,14 @@
 
 
 def call(kernel, outs, scratch, flops, exps, *args, spaces=None, out=None, limit=40):
+    out = out or jax.tree.map(lambda _: pltpu.VMEM, outs)
     return pl.pallas_call(
         kernel,
         out_shape=outs,
         in_specs=[
             pl.BlockSpec(memory_space=space) for space in spaces or [pltpu.VMEM] * len(args)
         ],
-        out_specs=jax.tree.map(lambda _: pl.BlockSpec(memory_space=out or pltpu.VMEM), outs),
+        out_specs=jax.tree.map(lambda space: pl.BlockSpec(memory_space=space), out),
         scratch_shapes=scratch,
         compiler_params=pltpu.CompilerParams(vmem_limit_bytes=limit * 2**20),
         cost_estimate=pl.CostEstimate(
@@ -299,26 +308,29 @@
         spread = jnp.broadcast_to(value[None], (len(groups[0]),) + value.shape)
         return lax.all_to_all(spread, axis, 0, 0, axis_index_groups=groups, tiled=True)
 
-    y, offset = call(
+    x = source_latent.T
+    y, offset, copies = call(
         prepare_kernel,
-        (jax.ShapeDtypeStruct((depth, each), bf16), jax.ShapeDtypeStruct((1, each), f32)),
-        [],
+        (
+            jax.ShapeDtypeStruct((depth, each), bf16),
+            jax.ShapeDtypeStruct((1, each), f32),
+            jax.ShapeDtypeStruct((ny, FEATURES, per), bf16),
+        ),
+        [
+            pltpu.VMEM((FEATURES, per), bf16),
+            pltpu.VMEM((FEATURES, each), bf16),
+            pltpu.VMEM((1, each), f32),
+            pltpu.VMEM((1, each), f32),
+            pltpu.SemaphoreType.DMA((4 + ny,)),
+        ],
         each * FEATURES * 4,
         0,
+        x,
         target_latent.T,
         target_logw.reshape(1, each),
         target_potential.reshape(1, each),
-    )
-    x = source_latent.T
-    copies = call(
-        copies_kernel,
-        jax.ShapeDtypeStruct((ny, FEATURES, per), bf16),
-        [pltpu.SemaphoreType.DMA((ny,))],
-        0,
-        0,
-        x,
-        spaces=[pl.ANY],
-        out=pl.ANY,
+        spaces=[pl.ANY] * 4,
+        out=(pltpu.VMEM, pltpu.VMEM, pl.ANY),
         limit=60,
     )
     xs = lax.all_to_all(copies, "blk", 0, 0, axis_index_groups=y_groups, tiled=True)

time: 195 us -> 165 us (0.85)
  Pallas kernels: 110 us -> 79.9 us
    pallas_call x6 -> x5, Pallas kernels: 110 us -> 79.9 us  [call(): pl.pallas_call(kernel, out_shape=outs, in_specs=[pl.BlockSpec(memory_spac...]
  transfers between devices with their start and end apart: 7 -> 7, of which waited for: 5 -> 5; matrix products, arithmetic and copies ran while one was open for 0% -> 0% of each run, Pallas kernels for 20% -> 24%
where the time goes in v7:
time: 165 us; the launch traced here: 164 us
  Pallas kernels  79.9 us (48%)
  starting transfers between devices  46.1 us (28%)
  blocking collectives  20.6 us (12%)
  waiting for transfers between devices  13.3 us (8%)
    pallas_call x5, Pallas kernels, call(): pl.pallas_call(kernel, out_shape=outs, in_specs=[pl.BlockSpec(memory_spac...  79.9 us
    ppermute x4, starting transfers between devices, along_z(): return lax.ppermute(value, 'blk', perm)  23.3 us
    all_to_all x2, blocking collectives, shared(): lax.all_to_all(spread, axis, 0, 0, axis_index_groups=groups, tiled=True)  20.6 us
    ppermute x1, starting transfers between devices, along_wide(): return lax.ppermute(value, 'wide', [(w, w ^ k) for w in range(nw)])  13.6 us
    ppermute x4, waiting for transfers between devices, along_z(): return lax.ppermute(value, 'blk', perm)  6.57 us
    all_to_all x1, waiting for transfers between devices, per_device(): lax.all_to_all(sums, 'blk', 0, 0, axis_index_groups=quarters, tiled=True)  4.96 us
    all_to_all x1, starting transfers between devices, per_device(): lax.all_to_all(sums, 'blk', 0, 0, axis_index_groups=quarters, tiled=True)  4.74 us
    all_to_all x1, starting transfers between devices, per_device(): lax.all_to_all(copies, 'blk', 0, 0, axis_index_groups=y_groups, tiled=True)  4.48 us
  transfers between devices with their start and end apart: 7, of which 5 were waited for; matrix products, arithmetic and copies ran while one was open for 0% of the time, Pallas kernels for 24%

profile of v7, /device:TPU:6, one launch (start us, length us, event | category | flops | bytes accessed | tf_op | source)
XLA Modules:
  0.0 163.9 jit_solution(14675145247707226894)
XLA Ops:
  0.6 2.6 %shard_map.68 = (bf16[80,256]{1,0:T(8,128)(2,1)}, f32[1,256]{1,0:T(1,128)}, bf16[4,64,2048]{2,1,0:T(8,128)(2,1)}) custom-call(bf16[64,2048]{1,0:T(8,128)(2,1)} %bitcast.19, bf16[64,256]{1,0:T(8,128)(2,1)} %bitcast.20, f32[1,256]{1,0:T(1,128)} %bitcast.23, f32[1,256]{1,0:T(1,128)} %bitcast.24), custom_call_target="tpu_custom_call" | custom-call | flops 65536 | bytes 4194304 | tf_op jit(solution)/shard_map/pallas_call | solution.py:267
  3.3 4.5 %all-to-all-start = ((bf16[4,64,2048]{2,1,0:T(8,128)(2,1)}), bf16[4,64,2048]{2,1,0:T(8,128)(2,1)S(1)}, u32[]{:S(2)}, u32[]{:S(2)}) async-start(bf16[4,64,2048]{2,1,0:T(8,128)(2,1)} %get-tuple-element.12), calls=%async_computation | async-start | bytes 2097152 | tf_op jit(solution)/shard_map/all_to_all | solution.py:336
  7.8 9.1 %collective-permute-start = (bf16[80,256]{1,0:T(8,128)(2,1)S(1)}, bf16[80,256]{1,0:T(8,128)(2,1)S(1)}, u32[]{:S(2)}, u32[]{:S(2)}) collective-permute-start(bf16[80,256]{1,0:T(8,128)(2,1)S(1)} %copy-done.2), channel_id=1, source_target_pairs={{0,64},{16,80},{32,96},{48,112},{64,0},{80,16},{96,32},{112,48},{1... | collective-permute-start | bytes 122888 | tf_op jit(solution)/shard_map/ppermute | solution.py:302
  16.9 2.4 %collective-permute-done = bf16[80,256]{1,0:T(8,128)(2,1)S(1)} collective-permute-done((bf16[80,256]{1,0:T(8,128)(2,1)S(1)}, bf16[80,256]{1,0:T(8,128)(2,1)S(1)}, u32[]{:S(2)}, u32[]{:S(2)}) %collective-permute-start) | collective-permute-done | bytes 40992 | tf_op jit(solution)/shard_map/ppermute | solution.py:302
  19.3 5.2 %collective-permute-start.1 = (bf16[80,512]{1,0:T(8,128)(2,1)S(1)}, bf16[80,512]{1,0:T(8,128)(2,1)S(1)}, u32[]{:S(2)}, u32[]{:S(2)}) collective-permute-start(bf16[80,512]{1,0:T(8,128)(2,1)S(1)} %pad_maximum_fusion), channel_id=1, source_target_pairs={{0,32},{16,48},{32,0},{48,16},{64,96},{80,112},{96,64},{112,80},{1... | collective-permute-start | bytes 245768 | tf_op jit(solution)/shard_map/ppermute | solution.py:302
  24.4 4.1 %collective-permute-done.1 = bf16[80,512]{1,0:T(8,128)(2,1)S(1)} collective-permute-done((bf16[80,512]{1,0:T(8,128)(2,1)S(1)}, bf16[80,512]{1,0:T(8,128)(2,1)S(1)}, u32[]{:S(2)}, u32[]{:S(2)}) %collective-permute-start.1) | collective-permute-done | bytes 81952 | tf_op jit(solution)/shard_map/ppermute | solution.py:302
  28.5 2.1 %collective-permute-start.2 = (bf16[80,1024]{1,0:T(8,128)(2,1)S(1)}, bf16[80,1024]{1,0:T(8,128)(2,1)S(1)}, u32[]{:S(2)}, u32[]{:S(2)}) collective-permute-start(bf16[80,1024]{1,0:T(8,128)(2,1)S(1)} %constant_dynamic-update-slice_fusion.refs_0_), channel_id=1, source_target_pairs={{0,16},{16,0},{32,48},{48,32},{64,80},{80,64},{96,112},{112,96},{1... | collective-permute-start | bytes 491528 | tf_op jit(solution)/shard_map/ppermute | solution.py:302
  30.6 5.0 %shard_map.69 = (bf16[1024,128]{1,0:T(8,128)(2,1)S(1)}, f32[4,2048]{1,0:T(4,128)S(1)}) custom-call(bf16[80,1024]{1,0:T(8,128)(2,1)S(1)} %constant_dynamic-update-slice_fusion.refs_0_, bf16[4,64,2048]{2,1,0:T(8,128)(2,1)S(1)} %all-to-all-done.refs_1_.x_ref), custom_call_target="tpu_custom_call" | custom-call | flops 2147483648 | bytes 4194304 | tf_op jit(solution)/shard_map/pallas_call | solution.py:267
  35.6 0.1 collective-permute-done.2.refs_0_
  35.7 5.0 %shard_map.70 = (bf16[1024,128]{1,0:T(8,128)(2,1)S(1)}, f32[4,2560]{1,0:T(4,128)S(1)}) custom-call(bf16[80,1024]{1,0:T(8,128)(2,1)S(1)} %collective-permute-done.2.refs_0_, bf16[4,64,2048]{2,1,0:T(8,128)(2,1)S(1)} %all-to-all-done.refs_1_.x_ref, f32[4,2048]{1,0:T(4,128)S(1)} %get-tuple-element.13.refs_2_, f32[1,2048]{1,0:T(1,128)S(1)} %bitcast.18), custom_call_target="tpu_custom_call" | custom-call | flops 2147483648 | bytes 4194304 | tf_op jit(solution)/shard_map/pallas_call | solution.py:267
  40.8 10.6 %all_to_all.27.logw_ref = f32[4,4,2560]{2,1,0:T(4,128)S(1)} all-to-all(f32[4,4,2560]{2,1,0:T(4,128)S(1)} %broadcast_in_dim.6), channel_id=1, replica_groups={{0,128,256,384},{16,144,272,400},{32,160,288,416},{48,176,304,432},{64,..., dimensions={0} | all-to-all | bytes 327680 | tf_op jit(solution)/shard_map/all_to_all | solution.py:309
  51.5 10.0 %all_to_all.28 = f32[8,4,2048]{2,1,0:T(4,128)S(1)} all-to-all(f32[8,4,2048]{2,1,0:T(4,128)S(1)} %broadcast_in_dim.7), channel_id=1, replica_groups={{0,1,2,3,4,5,6,7},{8,9,10,11,12,13,14,15},{16,17,18,19,20,21,22,23},{24..., dimensions={0} | all-to-all | bytes 524288 | tf_op jit(solution)/shard_map/all_to_all | solution.py:309
  61.6 0.1 exponential_reduce_fusion
  61.8 13.6 %collective-permute-start.3 = (f32[4,2048]{1,0:T(4,128)S(1)}, f32[4,2048]{1,0:T(4,128)S(1)}, u32[]{:S(2)}, u32[]{:S(2)}) collective-permute-start(f32[4,2048]{1,0:T(4,128)S(1)} %log_add_fusion.1), channel_id=1, source_target_pairs={{0,8},{1,9},{2,10},{3,11},{4,12},{5,13},{6,14},{7,15},{8,0},{9,1},... | collective-permute-start | bytes 98312 | tf_op jit(solution)/shard_map/ppermute | solution.py:305
  75.5 1.8 %collective-permute-done.3 = f32[4,2048]{1,0:T(4,128)S(1)} collective-permute-done((f32[4,2048]{1,0:T(4,128)S(1)}, f32[4,2048]{1,0:T(4,128)S(1)}, u32[]{:S(2)}, u32[]{:S(2)}) %collective-permute-start.3) | collective-permute-done | bytes 32800 | tf_op jit(solution)/shard_map/ppermute | solution.py:305
  77.3 33.7 %shard_map.71 = f32[4,256]{1,0:T(4,128)S(1)} custom-call(s32[1]{0:T(128)} %bitcast.7.place_ref, bf16[1024,128]{1,0:T(8,128)(2,1)S(1)} %get-tuple-element.17.near_ref, bf16[1024,128]{1,0:T(8,128)(2,1)S(1)} %get-tuple-element.16.far_ref, bf16[4,64,2048]{2,1,0:T(8,128)(2,1)S(1)} %all-to-all-done.refs_1_.x_ref, f32[4,2048]{1,0:T(4,128)S(1)} %log_add_fusion.total_ref, ...), custom_call_target="tpu_custom_call" | custom-call | flops 2147483648 | bytes 4194304 | tf_op jit(solution)/shard_map/pallas_call | solution.py:267
  111.0 7.0 %collective-permute-start.4 = (f32[4,256]{1,0:T(4,128)S(1)}, f32[4,256]{1,0:T(4,128)S(1)}, u32[]{:S(2)}, u32[]{:S(2)}) collective-permute-start(f32[4,256]{1,0:T(4,128)S(1)} %shard_map.71), channel_id=1, source_target_pairs={{0,64},{16,80},{32,96},{48,112},{64,0},{80,16},{96,32},{112,48},{1... | collective-permute-start | bytes 12296 | tf_op jit(solution)/shard_map/ppermute | solution.py:302
  118.0 33.7 %shard_map.72 = f32[4,256]{1,0:T(4,128)S(1)} custom-call(s32[1]{0:T(128)} %bitcast.7.place_ref, bf16[1024,128]{1,0:T(8,128)(2,1)S(1)} %get-tuple-element.17.near_ref, bf16[1024,128]{1,0:T(8,128)(2,1)S(1)} %get-tuple-element.16.far_ref, bf16[4,64,2048]{2,1,0:T(8,128)(2,1)S(1)} %all-to-all-done.refs_1_.x_ref, f32[4,2048]{1,0:T(4,128)S(1)} %log_add_fusion.total_ref, ...), custom_call_target="tpu_custom_call" | custom-call | flops 2147483648 | bytes 4194304 | tf_op jit(solution)/shard_map/pallas_call | solution.py:267
  151.7 0.6 copy.11
  152.3 4.7 %all-to-all-start.3 = ((f32[4,1,256]{2,1,0:T(1,128)}), f32[4,1,256]{2,1,0:T(1,128)S(1)}, u32[]{:S(2)}, u32[]{:S(2)}) async-start(f32[4,1,256]{2,1,0:T(1,128)} %copy.11), calls=%async_computation.3 | async-start | bytes 8192 | tf_op jit(solution)/shard_map/all_to_all | solution.py:402
  157.0 0.6 subtract_multiply_fusion
  157.6 5.0 %all-to-all-done.3 = f32[4,1,256]{2,1,0:T(1,128)S(1)} async-done(((f32[4,1,256]{2,1,0:T(1,128)}), f32[4,1,256]{2,1,0:T(1,128)S(1)}, u32[]{:S(2)}, u32[]{:S(2)}) %all-to-all-start.3) | async-done | bytes 4128 | tf_op jit(solution)/shard_map/all_to_all | solution.py:402
  162.6 0.7 copy-done.3
  163.3 0.6 subtract_multiply_fusion.1
  (25 shorter events, 0.4 us)
Async XLA Ops:
  3.3 4.5 %copy-start.2 = (bf16[80,256]{1,0:T(8,128)(2,1)S(1)}, bf16[80,256]{1,0:T(8,128)(2,1)}, u32[]{:S(2)}) copy-start(bf16[80,256]{1,0:T(8,128)(2,1)} %get-tuple-element.11) | copy-start | bytes 122884
  3.3 27.4 %all-to-all-start = ((bf16[4,64,2048]{2,1,0:T(8,128)(2,1)}), bf16[4,64,2048]{2,1,0:T(8,128)(2,1)S(1)}, u32[]{:S(2)}, u32[]{:S(2)}) async-start(bf16[4,64,2048]{2,1,0:T(8,128)(2,1)} %get-tuple-element.12), calls=%async_computation | async-start | bytes 2097152 | tf_op jit(solution)/shard_map/all_to_all | solution.py:336
  7.8 11.5 %collective-permute-start = (bf16[80,256]{1,0:T(8,128)(2,1)S(1)}, bf16[80,256]{1,0:T(8,128)(2,1)S(1)}, u32[]{:S(2)}, u32[]{:S(2)}) collective-permute-start(bf16[80,256]{1,0:T(8,128)(2,1)S(1)} %copy-done.2), channel_id=1, source_target_pairs={{0,64},{16,80},{32,96},{48,112},{64,0},{80,16},{96,32},{112,48},{1... | collective-permute-start | bytes 122888 | tf_op jit(solution)/shard_map/ppermute | solution.py:302
  19.3 9.3 %collective-permute-start.1 = (bf16[80,512]{1,0:T(8,128)(2,1)S(1)}, bf16[80,512]{1,0:T(8,128)(2,1)S(1)}, u32[]{:S(2)}, u32[]{:S(2)}) collective-permute-start(bf16[80,512]{1,0:T(8,128)(2,1)S(1)} %pad_maximum_fusion), channel_id=1, source_target_pairs={{0,32},{16,48},{32,0},{48,16},{64,96},{80,112},{96,64},{112,80},{1... | collective-permute-start | bytes 245768 | tf_op jit(solution)/shard_map/ppermute | solution.py:302
  28.5 7.2 %copy-start = (f32[2048]{0:T(1024)S(1)}, f32[2048]{0:T(1024)}, u32[]{:S(2)}) copy-start(f32[2048]{0:T(1024)} %param.6) | copy-start | bytes 24580
  28.5 7.2 %collective-permute-start.2 = (bf16[80,1024]{1,0:T(8,128)(2,1)S(1)}, bf16[80,1024]{1,0:T(8,128)(2,1)S(1)}, u32[]{:S(2)}, u32[]{:S(2)}) collective-permute-start(bf16[80,1024]{1,0:T(8,128)(2,1)S(1)} %constant_dynamic-update-slice_fusion.refs_0_), channel_id=1, source_target_pairs={{0,16},{16,0},{32,48},{48,32},{64,80},{80,64},{96,112},{112,96},{1... | collective-permute-start | bytes 491528 | tf_op jit(solution)/shard_map/ppermute | solution.py:302
  61.6 13.7 %copy-start.1 = (bf16[2048,64]{0,1:T(8,128)(2,1)S(1)}, bf16[2048,64]{0,1:T(8,128)(2,1)}, u32[]{:S(2)}) copy-start(bf16[2048,64]{0,1:T(8,128)(2,1)} %param.5) | copy-start | bytes 786436
  61.8 15.5 %collective-permute-start.3 = (f32[4,2048]{1,0:T(4,128)S(1)}, f32[4,2048]{1,0:T(4,128)S(1)}, u32[]{:S(2)}, u32[]{:S(2)}) collective-permute-start(f32[4,2048]{1,0:T(4,128)S(1)} %log_add_fusion.1), channel_id=1, source_target_pairs={{0,8},{1,9},{2,10},{3,11},{4,12},{5,13},{6,14},{7,15},{8,0},{9,1},... | collective-permute-start | bytes 98312 | tf_op jit(solution)/shard_map/ppermute | solution.py:305
  111.0 40.7 %collective-permute-start.4 = (f32[4,256]{1,0:T(4,128)S(1)}, f32[4,256]{1,0:T(4,128)S(1)}, u32[]{:S(2)}, u32[]{:S(2)}) collective-permute-start(f32[4,256]{1,0:T(4,128)S(1)} %shard_map.71), channel_id=1, source_target_pairs={{0,64},{16,80},{32,96},{48,112},{64,0},{80,16},{96,32},{112,48},{1... | collective-permute-start | bytes 12296 | tf_op jit(solution)/shard_map/ppermute | solution.py:302
  152.3 10.3 %all-to-all-start.3 = ((f32[4,1,256]{2,1,0:T(1,128)}), f32[4,1,256]{2,1,0:T(1,128)S(1)}, u32[]{:S(2)}, u32[]{:S(2)}) async-start(f32[4,1,256]{2,1,0:T(1,128)} %copy.11), calls=%async_computation.3 | async-start | bytes 8192 | tf_op jit(solution)/shard_map/all_to_all | solution.py:402
  162.6 0.7 copy-start.3

commit v8 on v7

--- a/solution.py
+++ b/solution.py
@@ -40,11 +40,25 @@
 
 
 def prepare_kernel(
-    x_in, y_in, logw_in, potential_in, out_ref, offset_ref, copies_ref, x_ref, y_ref, logw_ref, potential_ref, sem
+    x_in,
+    y_in,
+    logw_in,
+    potential_in,
+    out_ref,
+    offset_ref,
+    upper_ref,
+    lower_ref,
+    x_ref,
+    y_ref,
+    logw_ref,
+    potential_ref,
+    sem,
 ):
-    count = copies_ref.shape[0]
+    count = upper_ref.shape[0]
+    half = FEATURES // 2
     pairs = [(x_in, x_ref), (y_in, y_ref), (logw_in, logw_ref), (potential_in, potential_ref)]
-    pairs += [(x_ref, copies_ref.at[k]) for k in range(count)]
+    pairs += [(x_ref.at[0:half], upper_ref.at[k]) for k in range(count)]
+    pairs += [(x_ref.at[half:FEATURES], lower_ref.at[k]) for k in range(count)]
     moves = [
         pltpu.make_async_copy(source, target, sem.at[k])
         for k, (source, target) in enumerate(pairs)
@@ -68,9 +82,9 @@
         move.wait()
 
 
-def weights_of(features, extra):
-    rest = jnp.zeros((DEPTH - FEATURES - EXTRA, features.shape[1]), features.dtype)
-    return jnp.concatenate([features, extra, rest], axis=0)
+def weights_of(upper_ref, lower_ref, r, at, extra):
+    rest = jnp.zeros((DEPTH - FEATURES - EXTRA, extra.shape[1]), extra.dtype)
+    return jnp.concatenate([upper_ref[r, :, at], lower_ref[r, :, at], extra, rest], axis=0)
 
 
 def product(a, b):
@@ -88,12 +102,14 @@
 
 
 def first_kernel(last, *refs):
-    y_ref, x_ref, refs = refs[0], refs[1], refs[2:]
+    y_ref, upper_ref, lower_ref, refs = refs[0], refs[1], refs[2], refs[3:]
     if last:
-        before_ref, logw_ref, refs = refs[0], refs[1], refs[2:]
-    yt_ref, l_ref, sums_ref = refs
+        before_ref, logw_ref, yt_ref, l_ref, sums_ref = refs
+    else:
+        offset_ref, yt_ref, l_ref, kept_ref, sums_ref = refs
+        kept_ref[...] = offset_ref[...]
     rows = yt_ref.shape[0]
-    ny, _, per = x_ref.shape
+    ny, _, per = upper_ref.shape
     row_step = min(ROWS, rows)
     col_step = min(LANES, per)
     together = 2
@@ -128,7 +144,7 @@
         for s in range(together):
             r = g * together + s
             for t in range(0, per, col_step):
-                weights = weights_of(x_ref[r, :, t : t + col_step], extra)
+                weights = weights_of(upper_ref, lower_ref, r, slice(t, t + col_step), extra)
                 total = jnp.zeros((8, col_step), jnp.float32)
                 for j in range(0, rows, row_step):
                     score = product(yt_ref[j : j + row_step, :], weights)
@@ -147,7 +163,7 @@
         def again(g, carry):
             at = pl.ds(pl.multiple_of(g * col_step, col_step), col_step)
             for r in range(ny):
-                weights = weights_of(x_ref[r, :, at], extra)
+                weights = weights_of(upper_ref, lower_ref, r, at, extra)
 
                 def advance(j, state):
                     top, total = state
@@ -177,7 +193,8 @@
     place_ref,
     near_ref,
     far_ref,
-    x_ref,
+    upper_ref,
+    lower_ref,
     total_ref,
     logw_ref,
     s_ref,
@@ -188,7 +205,7 @@
 ):
     nz, each = s_ref.shape
     rows = nz * each
-    ny, _, per = x_ref.shape
+    ny, _, per = upper_ref.shape
     row_step = min(ROWS, rows)
     col_step = min(LANES, per)
 
@@ -212,7 +229,7 @@
         for r in range(ny):
             for t in range(0, per, col_step):
                 at = slice(t, t + col_step)
-                score = product(left, weights_of(x_ref[r, :, at], extra_ref[r, :, at]))
+                score = product(left, weights_of(upper_ref, lower_ref, r, at, extra_ref[r, :, at]))
                 part = lanes_folded(jnp.exp(score), jnp.add)
                 if r == 0 and t == 0:
                     acc_ref[here, :] = part
@@ -243,7 +260,7 @@
                 def advance(t, state):
                     top, total = state
                     at = pl.ds(pl.multiple_of(t * col_step, col_step), col_step)
-                    score = product(left, weights_of(x_ref[r, :, at], extra_ref[r, :, at]))
+                    score = product(left, weights_of(upper_ref, lower_ref, r, at, extra_ref[r, :, at]))
                     new = jnp.maximum(top, lanes_folded(score, jnp.maximum))
                     total = total * jnp.exp(top - new)
                     for k in range(col_step // 128):
@@ -309,19 +326,20 @@
         return lax.all_to_all(spread, axis, 0, 0, axis_index_groups=groups, tiled=True)
 
     x = source_latent.T
-    y, offset, copies = call(
+    y, offset, *copies = call(
         prepare_kernel,
         (
             jax.ShapeDtypeStruct((depth, each), bf16),
             jax.ShapeDtypeStruct((1, each), f32),
-            jax.ShapeDtypeStruct((ny, FEATURES, per), bf16),
+            jax.ShapeDtypeStruct((ny, FEATURES // 2, per), bf16),
+            jax.ShapeDtypeStruct((ny, FEATURES // 2, per), bf16),
         ),
         [
             pltpu.VMEM((FEATURES, per), bf16),
             pltpu.VMEM((FEATURES, each), bf16),
             pltpu.VMEM((1, each), f32),
             pltpu.VMEM((1, each), f32),
-            pltpu.SemaphoreType.DMA((4 + ny,)),
+            pltpu.SemaphoreType.DMA((4 + 2 * ny,)),
         ],
         each * FEATURES * 4,
         0,
@@ -330,10 +348,12 @@
         target_logw.reshape(1, each),
         target_potential.reshape(1, each),
         spaces=[pl.ANY] * 4,
-        out=(pltpu.VMEM, pltpu.VMEM, pl.ANY),
+        out=(pltpu.VMEM, pltpu.VMEM, pl.ANY, pl.ANY),
         limit=60,
     )
-    xs = lax.all_to_all(copies, "blk", 0, 0, axis_index_groups=y_groups, tiled=True)
+    xs = [
+        lax.all_to_all(part, "blk", 0, 0, axis_index_groups=y_groups, tiled=True) for part in copies
+    ]
     bit = nz // 2
     while bit > 1:
         y = jnp.concatenate([y, along_z(y, bit)], axis=1)
@@ -341,22 +361,23 @@
     far = along_z(y, 1)
 
     def first(block, *more):
-        last = len(more) > 0
+        last = len(more) > 1
         return call(
             functools.partial(first_kernel, last),
             (
                 jax.ShapeDtypeStruct((half, DEPTH), bf16),
                 jax.ShapeDtypeStruct((ny, per + per // ny if last else per), f32),
-            ),
+            )
+            + (() if last else (jax.ShapeDtypeStruct((1, each), f32),)),
             [pltpu.VMEM((ny, 8, per), f32)],
             2 * pairs * DEPTH,
             pairs,
             block,
-            xs,
+            *xs,
             *more,
         )
 
-    yt_near, total = first(y)
+    yt_near, total, offset = first(y, offset)
     yt_far, total = first(far, total, source_logw.reshape(1, per))
     got = shared(total, "blk", y_groups)
     total = log_sum(got[:, :, :per])
@@ -389,10 +410,10 @@
             place_in,
             near,
             yt_far,
-            xs,
+            *xs,
             total,
             got,
-            spaces=[pltpu.SMEM] + [pltpu.VMEM] * 5,
+            spaces=[pltpu.SMEM] + [pltpu.VMEM] * 6,
         )
 
     sent = second(tuple((h, k, a - count) for h, k, a in blocks if a >= count), yt_near)

time: 165 us -> 167 us (1.012)
  starting transfers between devices: 46.1 us -> 52.1 us
  waiting for transfers between devices: 13.3 us -> 10 us
    all_to_all x1 -> x2, starting transfers between devices: 4.48 us -> 8.91 us  [per_device(): lax.all_to_all(part, 'blk', 0, 0, axis_index_groups=y_groups, tiled=True)]
    ppermute x4, waiting for transfers between devices: 6.57 us -> 2.66 us  [along_z(): return lax.ppermute(value, 'blk', perm)]
    ppermute x4, starting transfers between devices: 23.3 us -> 25.6 us  [along_z(): return lax.ppermute(value, 'blk', perm)]
  transfers between devices with their start and end apart: 7 -> 8, of which waited for: 5 -> 4; matrix products, arithmetic and copies ran while one was open for 0% -> 0% of each run, Pallas kernels for 24% -> 23%
where the time goes in v8:
time: 167 us; the launch traced here: 166 us
  Pallas kernels  80 us (48%)
  starting transfers between devices  52.1 us (31%)
  blocking collectives  20.8 us (12%)
  waiting for transfers between devices  10 us (6%)
    pallas_call x5, Pallas kernels, call(): pl.pallas_call(kernel, out_shape=outs, in_specs=[pl.BlockSpec(memory_spac...  80 us
    ppermute x4, starting transfers between devices, along_z(): return lax.ppermute(value, 'blk', perm)  25.6 us
    all_to_all x2, blocking collectives, shared(): lax.all_to_all(spread, axis, 0, 0, axis_index_groups=groups, tiled=True)  20.8 us
    ppermute x1, starting transfers between devices, along_wide(): return lax.ppermute(value, 'wide', [(w, w ^ k) for w in range(nw)])  13.6 us
    all_to_all x2, starting transfers between devices, per_device(): lax.all_to_all(part, 'blk', 0, 0, axis_index_groups=y_groups, tiled=True)  8.91 us
    all_to_all x1, waiting for transfers between devices, per_device(): lax.all_to_all(sums, 'blk', 0, 0, axis_index_groups=quarters, tiled=True)  4.96 us
    all_to_all x1, starting transfers between devices, per_device(): lax.all_to_all(sums, 'blk', 0, 0, axis_index_groups=quarters, tiled=True)  3.97 us
  transfers between devices with their start and end apart: 8, of which 4 were waited for; matrix products, arithmetic and copies ran while one was open for 0% of the time, Pallas kernels for 23%

profile of v8, /device:TPU:6, one launch (start us, length us, event | category | flops | bytes accessed | tf_op | source)
XLA Modules:
  0.0 166.1 jit_solution(9691544667934442146)
XLA Ops:
  0.6 2.7 %shard_map.68 = (bf16[80,256]{1,0:T(8,128)(2,1)}, f32[1,256]{1,0:T(1,128)}, bf16[4,32,2048]{2,1,0:T(8,128)(2,1)}, bf16[4,32,2048]{2,1,0:T(8,128)(2,1)}) custom-call(bf16[64,2048]{1,0:T(8,128)(2,1)} %bitcast.20, bf16[64,256]{1,0:T(8,128)(2,1)} %bitcast.21, f32[1,256]{1,0:T(1,128)} %bitcast.24, f32[1,256]{1,0:T(1,128)} %bitcast.25), custom_call_target="tpu_custom_call" | custom-call | flops 65536 | bytes 4194304 | tf_op jit(solution)/shard_map/pallas_call | solution.py:284
  3.3 4.5 %all-to-all-start = ((bf16[4,32,2048]{2,1,0:T(8,128)(2,1)}), bf16[4,32,2048]{2,1,0:T(8,128)(2,1)S(1)}, u32[]{:S(2)}, u32[]{:S(2)}) async-start(bf16[4,32,2048]{2,1,0:T(8,128)(2,1)} %get-tuple-element.14), calls=%async_computation | async-start | bytes 1048576 | tf_op jit(solution)/shard_map/all_to_all | solution.py:355
  7.8 9.1 %collective-permute-start = (bf16[80,256]{1,0:T(8,128)(2,1)S(1)}, bf16[80,256]{1,0:T(8,128)(2,1)S(1)}, u32[]{:S(2)}, u32[]{:S(2)}) collective-permute-start(bf16[80,256]{1,0:T(8,128)(2,1)S(1)} %copy-done.3), channel_id=1, source_target_pairs={{0,64},{16,80},{32,96},{48,112},{64,0},{80,16},{96,32},{112,48},{1... | collective-permute-start | bytes 122888 | tf_op jit(solution)/shard_map/ppermute | solution.py:319
  16.9 0.4 all-to-all-done.refs_1_.upper_ref
  17.3 4.4 %all-to-all-start.1 = ((bf16[4,32,2048]{2,1,0:T(8,128)(2,1)}), bf16[4,32,2048]{2,1,0:T(8,128)(2,1)S(1)}, u32[]{:S(2)}, u32[]{:S(2)}) async-start(bf16[4,32,2048]{2,1,0:T(8,128)(2,1)} %get-tuple-element.15), calls=%async_computation.1 | async-start | bytes 1048576 | tf_op jit(solution)/shard_map/all_to_all | solution.py:355
  21.7 5.2 %collective-permute-start.1 = (bf16[80,512]{1,0:T(8,128)(2,1)S(1)}, bf16[80,512]{1,0:T(8,128)(2,1)S(1)}, u32[]{:S(2)}, u32[]{:S(2)}) collective-permute-start(bf16[80,512]{1,0:T(8,128)(2,1)S(1)} %pad_maximum_fusion), channel_id=1, source_target_pairs={{0,32},{16,48},{32,0},{48,16},{64,96},{80,112},{96,64},{112,80},{1... | collective-permute-start | bytes 245768 | tf_op jit(solution)/shard_map/ppermute | solution.py:319
  26.9 2.6 %collective-permute-done.1 = bf16[80,512]{1,0:T(8,128)(2,1)S(1)} collective-permute-done((bf16[80,512]{1,0:T(8,128)(2,1)S(1)}, bf16[80,512]{1,0:T(8,128)(2,1)S(1)}, u32[]{:S(2)}, u32[]{:S(2)}) %collective-permute-start.1) | collective-permute-done | bytes 81952 | tf_op jit(solution)/shard_map/ppermute | solution.py:319
  29.6 3.6 %collective-permute-start.2 = (bf16[80,1024]{1,0:T(8,128)(2,1)S(1)}, bf16[80,1024]{1,0:T(8,128)(2,1)S(1)}, u32[]{:S(2)}, u32[]{:S(2)}) collective-permute-start(bf16[80,1024]{1,0:T(8,128)(2,1)S(1)} %constant_dynamic-update-slice_fusion.refs_0_), channel_id=1, source_target_pairs={{0,16},{16,0},{32,48},{48,32},{64,80},{80,64},{96,112},{112,96},{1... | collective-permute-start | bytes 491528 | tf_op jit(solution)/shard_map/ppermute | solution.py:319
  33.2 5.0 %shard_map.69 = (bf16[1024,128]{1,0:T(8,128)(2,1)S(1)}, f32[4,2048]{1,0:T(4,128)S(1)}, f32[1,256]{1,0:T(1,128)S(1)}) custom-call(bf16[80,1024]{1,0:T(8,128)(2,1)S(1)} %constant_dynamic-update-slice_fusion.refs_0_, bf16[4,32,2048]{2,1,0:T(8,128)(2,1)S(1)} %all-to-all-done.refs_1_.upper_ref, bf16[4,32,2048]{2,1,0:T(8,128)(2,1)S(1)} %all-to-all-done.1.refs_2_.lower_ref, ...), custom_call_target="tpu_custom_call" | custom-call | flops 2147483648 | bytes 4194304 | tf_op jit(solution)/shard_map/pallas_call | solution.py:284
  38.2 5.0 %shard_map.70 = (bf16[1024,128]{1,0:T(8,128)(2,1)S(1)}, f32[4,2560]{1,0:T(4,128)S(1)}) custom-call(bf16[80,1024]{1,0:T(8,128)(2,1)S(1)} %collective-permute-done.2.refs_0_, bf16[4,32,2048]{2,1,0:T(8,128)(2,1)S(1)} %all-to-all-done.refs_1_.upper_ref, bf16[4,32,2048]{2,1,0:T(8,128)(2,1)S(1)} %all-to-all-done.1.refs_2_.lower_ref, ...), custom_call_target="tpu_custom_call" | custom-call | flops 2147483648 | bytes 4194304 | tf_op jit(solution)/shard_map/pallas_call | solution.py:284
  43.2 10.8 %all_to_all.32.logw_ref = f32[4,4,2560]{2,1,0:T(4,128)S(1)} all-to-all(f32[4,4,2560]{2,1,0:T(4,128)S(1)} %broadcast_in_dim.6), channel_id=1, replica_groups={{0,128,256,384},{16,144,272,400},{32,160,288,416},{48,176,304,432},{64,..., dimensions={0} | all-to-all | bytes 327680 | tf_op jit(solution)/shard_map/all_to_all | solution.py:326
  54.2 10.0 %all_to_all.33 = f32[8,4,2048]{2,1,0:T(4,128)S(1)} all-to-all(f32[8,4,2048]{2,1,0:T(4,128)S(1)} %broadcast_in_dim.7), channel_id=1, replica_groups={{0,1,2,3,4,5,6,7},{8,9,10,11,12,13,14,15},{16,17,18,19,20,21,22,23},{24..., dimensions={0} | all-to-all | bytes 524288 | tf_op jit(solution)/shard_map/all_to_all | solution.py:326
  64.3 0.1 exponential_reduce_fusion
  64.4 13.6 %collective-permute-start.3 = (f32[4,2048]{1,0:T(4,128)S(1)}, f32[4,2048]{1,0:T(4,128)S(1)}, u32[]{:S(2)}, u32[]{:S(2)}) collective-permute-start(f32[4,2048]{1,0:T(4,128)S(1)} %log_add_fusion.1), channel_id=1, source_target_pairs={{0,8},{1,9},{2,10},{3,11},{4,12},{5,13},{6,14},{7,15},{8,0},{9,1},... | collective-permute-start | bytes 98312 | tf_op jit(solution)/shard_map/ppermute | solution.py:322
  78.0 0.1 multiply_reduce_fusion
  78.1 2.0 %collective-permute-done.3 = f32[4,2048]{1,0:T(4,128)S(1)} collective-permute-done((f32[4,2048]{1,0:T(4,128)S(1)}, f32[4,2048]{1,0:T(4,128)S(1)}, u32[]{:S(2)}, u32[]{:S(2)}) %collective-permute-start.3) | collective-permute-done | bytes 32800 | tf_op jit(solution)/shard_map/ppermute | solution.py:322
  80.2 33.7 %shard_map.71 = f32[4,256]{1,0:T(4,128)S(1)} custom-call(s32[1]{0:T(128)} %bitcast.7.place_ref, bf16[1024,128]{1,0:T(8,128)(2,1)S(1)} %get-tuple-element.21.near_ref, bf16[1024,128]{1,0:T(8,128)(2,1)S(1)} %get-tuple-element.20.far_ref, bf16[4,32,2048]{2,1,0:T(8,128)(2,1)S(1)} %all-to-all-done.refs_1_.upper_ref, ...), custom_call_target="tpu_custom_call" | custom-call | flops 2147483648 | bytes 4194304 | tf_op jit(solution)/shard_map/pallas_call | solution.py:284
  113.8 7.8 %collective-permute-start.4 = (f32[4,256]{1,0:T(4,128)S(1)}, f32[4,256]{1,0:T(4,128)S(1)}, u32[]{:S(2)}, u32[]{:S(2)}) collective-permute-start(f32[4,256]{1,0:T(4,128)S(1)} %shard_map.71), channel_id=1, source_target_pairs={{0,64},{16,80},{32,96},{48,112},{64,0},{80,16},{96,32},{112,48},{1... | collective-permute-start | bytes 12296 | tf_op jit(solution)/shard_map/ppermute | solution.py:319
  121.6 33.7 %shard_map.72 = f32[4,256]{1,0:T(4,128)S(1)} custom-call(s32[1]{0:T(128)} %bitcast.7.place_ref, bf16[1024,128]{1,0:T(8,128)(2,1)S(1)} %get-tuple-element.21.near_ref, bf16[1024,128]{1,0:T(8,128)(2,1)S(1)} %get-tuple-element.20.far_ref, bf16[4,32,2048]{2,1,0:T(8,128)(2,1)S(1)} %all-to-all-done.refs_1_.upper_ref, ...), custom_call_target="tpu_custom_call" | custom-call | flops 2147483648 | bytes 4194304 | tf_op jit(solution)/shard_map/pallas_call | solution.py:284
  155.3 0.6 copy.11
  155.9 4.0 %all-to-all-start.4 = ((f32[4,1,256]{2,1,0:T(1,128)}), f32[4,1,256]{2,1,0:T(1,128)S(1)}, u32[]{:S(2)}, u32[]{:S(2)}) async-start(f32[4,1,256]{2,1,0:T(1,128)} %copy.11), calls=%async_computation.4 | async-start | bytes 8192 | tf_op jit(solution)/shard_map/all_to_all | solution.py:423
  159.9 0.6 subtract_multiply_fusion
  160.5 5.0 %all-to-all-done.4 = f32[4,1,256]{2,1,0:T(1,128)S(1)} async-done(((f32[4,1,256]{2,1,0:T(1,128)}), f32[4,1,256]{2,1,0:T(1,128)S(1)}, u32[]{:S(2)}, u32[]{:S(2)}) %all-to-all-start.4) | async-done | bytes 4128 | tf_op jit(solution)/shard_map/all_to_all | solution.py:423
  165.5 0.6 subtract_multiply_fusion.1
  (27 shorter events, 0.4 us)
Async XLA Ops:
  3.3 4.5 %copy-start.3 = (bf16[80,256]{1,0:T(8,128)(2,1)S(1)}, bf16[80,256]{1,0:T(8,128)(2,1)}, u32[]{:S(2)}) copy-start(bf16[80,256]{1,0:T(8,128)(2,1)} %get-tuple-element.13) | copy-start | bytes 122884
  3.3 14.0 %all-to-all-start = ((bf16[4,32,2048]{2,1,0:T(8,128)(2,1)}), bf16[4,32,2048]{2,1,0:T(8,128)(2,1)S(1)}, u32[]{:S(2)}, u32[]{:S(2)}) async-start(bf16[4,32,2048]{2,1,0:T(8,128)(2,1)} %get-tuple-element.14), calls=%async_computation | async-start | bytes 1048576 | tf_op jit(solution)/shard_map/all_to_all | solution.py:355
  7.8 13.9 %collective-permute-start = (bf16[80,256]{1,0:T(8,128)(2,1)S(1)}, bf16[80,256]{1,0:T(8,128)(2,1)S(1)}, u32[]{:S(2)}, u32[]{:S(2)}) collective-permute-start(bf16[80,256]{1,0:T(8,128)(2,1)S(1)} %copy-done.3), channel_id=1, source_target_pairs={{0,64},{16,80},{32,96},{48,112},{64,0},{80,16},{96,32},{112,48},{1... | collective-permute-start | bytes 122888 | tf_op jit(solution)/shard_map/ppermute | solution.py:319
  17.3 15.9 %all-to-all-start.1 = ((bf16[4,32,2048]{2,1,0:T(8,128)(2,1)}), bf16[4,32,2048]{2,1,0:T(8,128)(2,1)S(1)}, u32[]{:S(2)}, u32[]{:S(2)}) async-start(bf16[4,32,2048]{2,1,0:T(8,128)(2,1)} %get-tuple-element.15), calls=%async_computation.1 | async-start | bytes 1048576 | tf_op jit(solution)/shard_map/all_to_all | solution.py:355
  21.7 7.8 %collective-permute-start.1 = (bf16[80,512]{1,0:T(8,128)(2,1)S(1)}, bf16[80,512]{1,0:T(8,128)(2,1)S(1)}, u32[]{:S(2)}, u32[]{:S(2)}) collective-permute-start(bf16[80,512]{1,0:T(8,128)(2,1)S(1)} %pad_maximum_fusion), channel_id=1, source_target_pairs={{0,32},{16,48},{32,0},{48,16},{64,96},{80,112},{96,64},{112,80},{1... | collective-permute-start | bytes 245768 | tf_op jit(solution)/shard_map/ppermute | solution.py:319
  29.6 3.6 %copy-start.1 = (f32[1,256]{1,0:T(1,128)S(1)}, f32[1,256]{1,0:T(1,128)}, u32[]{:S(2)}) copy-start(f32[1,256]{1,0:T(1,128)} %get-tuple-element.16.refs_3_) | copy-start | bytes 3076
  29.6 8.6 %collective-permute-start.2 = (bf16[80,1024]{1,0:T(8,128)(2,1)S(1)}, bf16[80,1024]{1,0:T(8,128)(2,1)S(1)}, u32[]{:S(2)}, u32[]{:S(2)}) collective-permute-start(bf16[80,1024]{1,0:T(8,128)(2,1)S(1)} %constant_dynamic-update-slice_fusion.refs_0_), channel_id=1, source_target_pairs={{0,16},{16,0},{32,48},{48,32},{64,80},{80,64},{96,112},{112,96},{1... | collective-permute-start | bytes 491528 | tf_op jit(solution)/shard_map/ppermute | solution.py:319
  33.2 5.0 %copy-start = (f32[2048]{0:T(1024)S(1)}, f32[2048]{0:T(1024)}, u32[]{:S(2)}) copy-start(f32[2048]{0:T(1024)} %param.6) | copy-start | bytes 24580
  64.2 13.7 %copy-start.2 = (bf16[2048,64]{0,1:T(8,128)(2,1)S(1)}, bf16[2048,64]{0,1:T(8,128)(2,1)}, u32[]{:S(2)}) copy-start(bf16[2048,64]{0,1:T(8,128)(2,1)} %param.5) | copy-start | bytes 786436
  64.4 15.8 %collective-permute-start.3 = (f32[4,2048]{1,0:T(4,128)S(1)}, f32[4,2048]{1,0:T(4,128)S(1)}, u32[]{:S(2)}, u32[]{:S(2)}) collective-permute-start(f32[4,2048]{1,0:T(4,128)S(1)} %log_add_fusion.1), channel_id=1, source_target_pairs={{0,8},{1,9},{2,10},{3,11},{4,12},{5,13},{6,14},{7,15},{8,0},{9,1},... | collective-permute-start | bytes 98312 | tf_op jit(solution)/shard_map/ppermute | solution.py:322
  113.8 41.4 %collective-permute-start.4 = (f32[4,256]{1,0:T(4,128)S(1)}, f32[4,256]{1,0:T(4,128)S(1)}, u32[]{:S(2)}, u32[]{:S(2)}) collective-permute-start(f32[4,256]{1,0:T(4,128)S(1)} %shard_map.71), channel_id=1, source_target_pairs={{0,64},{16,80},{32,96},{48,112},{64,0},{80,16},{96,32},{112,48},{1... | collective-permute-start | bytes 12296 | tf_op jit(solution)/shard_map/ppermute | solution.py:319
  155.9 9.5 %all-to-all-start.4 = ((f32[4,1,256]{2,1,0:T(1,128)}), f32[4,1,256]{2,1,0:T(1,128)S(1)}, u32[]{:S(2)}, u32[]{:S(2)}) async-start(f32[4,1,256]{2,1,0:T(1,128)} %copy.11), calls=%async_computation.4 | async-start | bytes 8192 | tf_op jit(solution)/shard_map/all_to_all | solution.py:423

commit v9 on v7

--- a/solution.py
+++ b/solution.py
@@ -87,20 +87,9 @@
     return top + jnp.log(1.0 + jnp.exp(jnp.minimum(a, b) - top))
 
 
-def first_kernel(last, *refs):
-    y_ref, x_ref, refs = refs[0], refs[1], refs[2:]
-    if last:
-        before_ref, logw_ref, refs = refs[0], refs[1], refs[2:]
-    yt_ref, l_ref, sums_ref = refs
+def turn_kernel(y_ref, yt_ref):
     rows = yt_ref.shape[0]
-    ny, _, per = x_ref.shape
     row_step = min(ROWS, rows)
-    col_step = min(LANES, per)
-    together = 2
-
-    extra = y_ref[FEATURES : FEATURES + EXTRA, :].astype(jnp.float32)
-    bias = extra[0:1, :] + extra[1:2, :] + extra[2:3, :]
-    shift = jnp.max(bias, axis=1, keepdims=True)
     for k in range(0, rows, row_step):
         block = jnp.concatenate(
             [
@@ -110,6 +99,25 @@
             axis=0,
         )
         yt_ref[k : k + row_step, :] = block.T.astype(jnp.bfloat16)
+
+
+def first_kernel(last, *refs):
+    y_ref, x_ref, refs = refs[0], refs[1], refs[2:]
+    if last:
+        before_ref, logw_ref, yt_ref, l_ref, sums_ref = refs
+        turn_kernel(y_ref, yt_ref)
+    else:
+        offset_ref, yt_ref, l_ref, kept_ref, sums_ref = refs
+        kept_ref[...] = offset_ref[...]
+    rows = yt_ref.shape[0]
+    ny, _, per = x_ref.shape
+    row_step = min(ROWS, rows)
+    col_step = min(LANES, per)
+    together = 2
+
+    extra = y_ref[FEATURES : FEATURES + EXTRA, :].astype(jnp.float32)
+    bias = extra[0:1, :] + extra[1:2, :] + extra[2:3, :]
+    shift = jnp.max(bias, axis=1, keepdims=True)
     extra = extra_block(
         ones_of(col_step), three_parts(jnp.broadcast_to(-shift, (1, col_step)))
     ).astype(jnp.bfloat16)
@@ -262,7 +270,9 @@
         store(top + jnp.log(total))
 
 
-def call(kernel, outs, scratch, flops, exps, *args, spaces=None, out=None, limit=40):
+def call(
+    kernel, outs, scratch, flops, exps, *args, spaces=None, out=None, limit=40, moved=4 * 2**20
+):
     out = out or jax.tree.map(lambda _: pltpu.VMEM, outs)
     return pl.pallas_call(
         kernel,
@@ -274,7 +284,7 @@
         scratch_shapes=scratch,
         compiler_params=pltpu.CompilerParams(vmem_limit_bytes=limit * 2**20),
         cost_estimate=pl.CostEstimate(
-            flops=flops, bytes_accessed=4 * 2**20, transcendentals=exps
+            flops=flops, bytes_accessed=moved, transcendentals=exps
         ),
     )(*args)
 
@@ -341,13 +351,15 @@
     far = along_z(y, 1)
 
     def first(block, *more):
-        last = len(more) > 0
+        last = len(more) == 2 and more[0].shape[0] == ny
         return call(
             functools.partial(first_kernel, last),
             (
                 jax.ShapeDtypeStruct((half, DEPTH), bf16),
-                jax.ShapeDtypeStruct((ny, per + per // ny if last else per), f32),
-            ),
+                jax.ShapeDtypeStruct((ny, per + per // ny), f32),
+            )
+            if last
+            else (jax.ShapeDtypeStruct((ny, per), f32), jax.ShapeDtypeStruct((1, each), f32)),
             [pltpu.VMEM((ny, 8, per), f32)],
             2 * pairs * DEPTH,
             pairs,
@@ -356,7 +368,16 @@
             *more,
         )
 
-    yt_near, total = first(y)
+    yt_near = call(
+        turn_kernel,
+        jax.ShapeDtypeStruct((half, DEPTH), bf16),
+        [],
+        0,
+        0,
+        y,
+        moved=11 * 10**6,
+    )
+    total, offset = first(y, offset, yt_near)
     yt_far, total = first(far, total, source_logw.reshape(1, per))
     got = shared(total, "blk", y_groups)
     total = log_sum(got[:, :, :per])

time: 165 us -> 165 us (level)
    pallas_call x5 -> x6, Pallas kernels: 79.9 us -> 80.1 us  [call(): pl.pallas_call(kernel, out_shape=outs, in_specs=[pl.BlockSpec(memory_spac...]
  transfers between devices with their start and end apart: 7 -> 7, of which waited for: 5 -> 4; matrix products, arithmetic and copies ran while one was open for 0% -> 0% of each run, Pallas kernels for 24% -> 24%
where the time goes in v9:
time: 165 us; the launch traced here: 164 us
  Pallas kernels  80.1 us (49%)
  starting transfers between devices  45.8 us (28%)
  blocking collectives  20.7 us (13%)
  waiting for transfers between devices  13.4 us (8%)
    pallas_call x6, Pallas kernels, call(): pl.pallas_call(kernel, out_shape=outs, in_specs=[pl.BlockSpec(memory_spac...  80.1 us
    ppermute x4, starting transfers between devices, along_z(): return lax.ppermute(value, 'blk', perm)  23.3 us
    all_to_all x2, blocking collectives, shared(): lax.all_to_all(spread, axis, 0, 0, axis_index_groups=groups, tiled=True)  20.7 us
    ppermute x1, starting transfers between devices, along_wide(): return lax.ppermute(value, 'wide', [(w, w ^ k) for w in range(nw)])  13.3 us
    ppermute x4, waiting for transfers between devices, along_z(): return lax.ppermute(value, 'blk', perm)  6.46 us
    all_to_all x1, waiting for transfers between devices, per_device(): lax.all_to_all(sums, 'blk', 0, 0, axis_index_groups=quarters, tiled=True)  4.96 us
    all_to_all x1, starting transfers between devices, per_device(): lax.all_to_all(sums, 'blk', 0, 0, axis_index_groups=quarters, tiled=True)  4.77 us
    all_to_all x1, starting transfers between devices, per_device(): lax.all_to_all(copies, 'blk', 0, 0, axis_index_groups=y_groups, tiled=True)  4.48 us
  transfers between devices with their start and end apart: 7, of which 4 were waited for; matrix products, arithmetic and copies ran while one was open for 0% of the time, Pallas kernels for 24%

profile of v9, /device:TPU:6, one launch (start us, length us, event | category | flops | bytes accessed | tf_op | source)
XLA Modules:
  0.0 164.0 jit_solution(2708159545667526324)
XLA Ops:
  0.6 2.6 %shard_map.68 = (bf16[80,256]{1,0:T(8,128)(2,1)}, f32[1,256]{1,0:T(1,128)}, bf16[4,64,2048]{2,1,0:T(8,128)(2,1)}) custom-call(bf16[64,2048]{1,0:T(8,128)(2,1)} %bitcast.20, bf16[64,256]{1,0:T(8,128)(2,1)} %bitcast.21, f32[1,256]{1,0:T(1,128)} %bitcast.24, f32[1,256]{1,0:T(1,128)} %bitcast.25), custom_call_target="tpu_custom_call" | custom-call | flops 65536 | bytes 4194304 | tf_op jit(solution)/shard_map/pallas_call | solution.py:277
  3.3 4.5 %all-to-all-start = ((bf16[4,64,2048]{2,1,0:T(8,128)(2,1)}), bf16[4,64,2048]{2,1,0:T(8,128)(2,1)S(1)}, u32[]{:S(2)}, u32[]{:S(2)}) async-start(bf16[4,64,2048]{2,1,0:T(8,128)(2,1)} %get-tuple-element.12), calls=%async_computation | async-start | bytes 2097152 | tf_op jit(solution)/shard_map/all_to_all | solution.py:346
  7.8 9.1 %collective-permute-start = (bf16[80,256]{1,0:T(8,128)(2,1)S(1)}, bf16[80,256]{1,0:T(8,128)(2,1)S(1)}, u32[]{:S(2)}, u32[]{:S(2)}) collective-permute-start(bf16[80,256]{1,0:T(8,128)(2,1)S(1)} %copy-done.3), channel_id=1, source_target_pairs={{0,64},{16,80},{32,96},{48,112},{64,0},{80,16},{96,32},{112,48},{1... | collective-permute-start | bytes 122888 | tf_op jit(solution)/shard_map/ppermute | solution.py:312
  16.9 2.4 %collective-permute-done = bf16[80,256]{1,0:T(8,128)(2,1)S(1)} collective-permute-done((bf16[80,256]{1,0:T(8,128)(2,1)S(1)}, bf16[80,256]{1,0:T(8,128)(2,1)S(1)}, u32[]{:S(2)}, u32[]{:S(2)}) %collective-permute-start) | collective-permute-done | bytes 40992 | tf_op jit(solution)/shard_map/ppermute | solution.py:312
  19.3 5.2 %collective-permute-start.1 = (bf16[80,512]{1,0:T(8,128)(2,1)S(1)}, bf16[80,512]{1,0:T(8,128)(2,1)S(1)}, u32[]{:S(2)}, u32[]{:S(2)}) collective-permute-start(bf16[80,512]{1,0:T(8,128)(2,1)S(1)} %pad_maximum_fusion), channel_id=1, source_target_pairs={{0,32},{16,48},{32,0},{48,16},{64,96},{80,112},{96,64},{112,80},{1... | collective-permute-start | bytes 245768 | tf_op jit(solution)/shard_map/ppermute | solution.py:312
  24.4 4.1 %collective-permute-done.1 = bf16[80,512]{1,0:T(8,128)(2,1)S(1)} collective-permute-done((bf16[80,512]{1,0:T(8,128)(2,1)S(1)}, bf16[80,512]{1,0:T(8,128)(2,1)S(1)}, u32[]{:S(2)}, u32[]{:S(2)}) %collective-permute-start.1) | collective-permute-done | bytes 81952 | tf_op jit(solution)/shard_map/ppermute | solution.py:312
  28.5 2.1 %collective-permute-start.2 = (bf16[80,1024]{1,0:T(8,128)(2,1)S(1)}, bf16[80,1024]{1,0:T(8,128)(2,1)S(1)}, u32[]{:S(2)}, u32[]{:S(2)}) collective-permute-start(bf16[80,1024]{1,0:T(8,128)(2,1)S(1)} %constant_dynamic-update-slice_fusion.y_ref.refs_0_), channel_id=1, source_target_pairs={{0,16},{16,0},{32,48},{48,32},{64,80},{80,64},{96,112},{112,96},{1... | collective-permute-start | bytes 491528 | tf_op jit(solution)/shard_map/ppermute | solution.py:312
  30.6 0.1 shard_map.69.refs_3_.near_ref
  30.8 0.7 copy-done.1
  31.4 4.9 %shard_map.70 = (f32[4,2048]{1,0:T(4,128)S(1)}, f32[1,256]{1,0:T(1,128)S(1)}) custom-call(bf16[80,1024]{1,0:T(8,128)(2,1)S(1)} %constant_dynamic-update-slice_fusion.y_ref.refs_0_, bf16[4,64,2048]{2,1,0:T(8,128)(2,1)S(1)} %all-to-all-done.refs_1_.x_ref, f32[1,256]{1,0:T(1,128)S(1)} %copy-done.1, bf16[1024,128]{1,0:T(8,128)(2,1)S(1)} %shard_map.69.refs_3_.near_ref), custom_call_target="tpu_custom_call" | custom-call | flops 2147483648 | bytes 4194304 | tf_op jit(solution)/shard_map/pallas_call | solution.py:277
  36.4 5.0 %shard_map.71 = (bf16[1024,128]{1,0:T(8,128)(2,1)S(1)}, f32[4,2560]{1,0:T(4,128)S(1)}) custom-call(bf16[80,1024]{1,0:T(8,128)(2,1)S(1)} %collective-permute-done.2.refs_0_, bf16[4,64,2048]{2,1,0:T(8,128)(2,1)S(1)} %all-to-all-done.refs_1_.x_ref, f32[4,2048]{1,0:T(4,128)S(1)} %get-tuple-element.14.refs_2_, f32[1,2048]{1,0:T(1,128)S(1)} %bitcast.19), custom_call_target="tpu_custom_call" | custom-call | flops 2147483648 | bytes 4194304 | tf_op jit(solution)/shard_map/pallas_call | solution.py:277
  41.4 10.7 %all_to_all.27.logw_ref = f32[4,4,2560]{2,1,0:T(4,128)S(1)} all-to-all(f32[4,4,2560]{2,1,0:T(4,128)S(1)} %broadcast_in_dim.6), channel_id=1, replica_groups={{0,128,256,384},{16,144,272,400},{32,160,288,416},{48,176,304,432},{64,..., dimensions={0} | all-to-all | bytes 327680 | tf_op jit(solution)/shard_map/all_to_all | solution.py:319
  52.3 10.1 %all_to_all.28 = f32[8,4,2048]{2,1,0:T(4,128)S(1)} all-to-all(f32[8,4,2048]{2,1,0:T(4,128)S(1)} %broadcast_in_dim.7), channel_id=1, replica_groups={{0,1,2,3,4,5,6,7},{8,9,10,11,12,13,14,15},{16,17,18,19,20,21,22,23},{24..., dimensions={0} | all-to-all | bytes 524288 | tf_op jit(solution)/shard_map/all_to_all | solution.py:319
  62.4 0.1 exponential_reduce_fusion
  62.5 13.3 %collective-permute-start.3 = (f32[4,2048]{1,0:T(4,128)S(1)}, f32[4,2048]{1,0:T(4,128)S(1)}, u32[]{:S(2)}, u32[]{:S(2)}) collective-permute-start(f32[4,2048]{1,0:T(4,128)S(1)} %log_add_fusion.1), channel_id=1, source_target_pairs={{0,8},{1,9},{2,10},{3,11},{4,12},{5,13},{6,14},{7,15},{8,0},{9,1},... | collective-permute-start | bytes 98312 | tf_op jit(solution)/shard_map/ppermute | solution.py:315
  75.9 2.0 %collective-permute-done.3 = f32[4,2048]{1,0:T(4,128)S(1)} collective-permute-done((f32[4,2048]{1,0:T(4,128)S(1)}, f32[4,2048]{1,0:T(4,128)S(1)}, u32[]{:S(2)}, u32[]{:S(2)}) %collective-permute-start.3) | collective-permute-done | bytes 32800 | tf_op jit(solution)/shard_map/ppermute | solution.py:315
  78.0 33.7 %shard_map.72 = f32[4,256]{1,0:T(4,128)S(1)} custom-call(s32[1]{0:T(128)} %bitcast.7.place_ref, bf16[1024,128]{1,0:T(8,128)(2,1)S(1)} %shard_map.69.refs_3_.near_ref, bf16[1024,128]{1,0:T(8,128)(2,1)S(1)} %get-tuple-element.16.far_ref, bf16[4,64,2048]{2,1,0:T(8,128)(2,1)S(1)} %all-to-all-done.refs_1_.x_ref, f32[4,2048]{1,0:T(4,128)S(1)} %log_add_fusion.total_ref, ...), custom_call_target="tpu_custom_call" | custom-call | flops 2147483648 | bytes 4194304 | tf_op jit(solution)/shard_map/pallas_call | solution.py:277
  111.7 7.0 %collective-permute-start.4 = (f32[4,256]{1,0:T(4,128)S(1)}, f32[4,256]{1,0:T(4,128)S(1)}, u32[]{:S(2)}, u32[]{:S(2)}) collective-permute-start(f32[4,256]{1,0:T(4,128)S(1)} %shard_map.72), channel_id=1, source_target_pairs={{0,64},{16,80},{32,96},{48,112},{64,0},{80,16},{96,32},{112,48},{1... | collective-permute-start | bytes 12296 | tf_op jit(solution)/shard_map/ppermute | solution.py:312
  118.6 33.7 %shard_map.73 = f32[4,256]{1,0:T(4,128)S(1)} custom-call(s32[1]{0:T(128)} %bitcast.7.place_ref, bf16[1024,128]{1,0:T(8,128)(2,1)S(1)} %shard_map.69.refs_3_.near_ref, bf16[1024,128]{1,0:T(8,128)(2,1)S(1)} %get-tuple-element.16.far_ref, bf16[4,64,2048]{2,1,0:T(8,128)(2,1)S(1)} %all-to-all-done.refs_1_.x_ref, f32[4,2048]{1,0:T(4,128)S(1)} %log_add_fusion.total_ref, ...), custom_call_target="tpu_custom_call" | custom-call | flops 2147483648 | bytes 4194304 | tf_op jit(solution)/shard_map/pallas_call | solution.py:277
  152.4 0.6 copy.11
  153.0 4.8 %all-to-all-start.3 = ((f32[4,1,256]{2,1,0:T(1,128)}), f32[4,1,256]{2,1,0:T(1,128)S(1)}, u32[]{:S(2)}, u32[]{:S(2)}) async-start(f32[4,1,256]{2,1,0:T(1,128)} %copy.11), calls=%async_computation.3 | async-start | bytes 8192 | tf_op jit(solution)/shard_map/all_to_all | solution.py:423
  157.8 0.6 subtract_multiply_fusion
  158.4 5.0 %all-to-all-done.3 = f32[4,1,256]{2,1,0:T(1,128)S(1)} async-done(((f32[4,1,256]{2,1,0:T(1,128)}), f32[4,1,256]{2,1,0:T(1,128)S(1)}, u32[]{:S(2)}, u32[]{:S(2)}) %all-to-all-start.3) | async-done | bytes 4128 | tf_op jit(solution)/shard_map/all_to_all | solution.py:423
  163.4 0.6 subtract_multiply_fusion.1
  (26 shorter events, 0.5 us)
Async XLA Ops:
  3.3 4.5 %copy-start.3 = (bf16[80,256]{1,0:T(8,128)(2,1)S(1)}, bf16[80,256]{1,0:T(8,128)(2,1)}, u32[]{:S(2)}) copy-start(bf16[80,256]{1,0:T(8,128)(2,1)} %get-tuple-element.11) | copy-start | bytes 122884
  3.3 27.5 %all-to-all-start = ((bf16[4,64,2048]{2,1,0:T(8,128)(2,1)}), bf16[4,64,2048]{2,1,0:T(8,128)(2,1)S(1)}, u32[]{:S(2)}, u32[]{:S(2)}) async-start(bf16[4,64,2048]{2,1,0:T(8,128)(2,1)} %get-tuple-element.12), calls=%async_computation | async-start | bytes 2097152 | tf_op jit(solution)/shard_map/all_to_all | solution.py:346
  7.8 11.5 %collective-permute-start = (bf16[80,256]{1,0:T(8,128)(2,1)S(1)}, bf16[80,256]{1,0:T(8,128)(2,1)S(1)}, u32[]{:S(2)}, u32[]{:S(2)}) collective-permute-start(bf16[80,256]{1,0:T(8,128)(2,1)S(1)} %copy-done.3), channel_id=1, source_target_pairs={{0,64},{16,80},{32,96},{48,112},{64,0},{80,16},{96,32},{112,48},{1... | collective-permute-start | bytes 122888 | tf_op jit(solution)/shard_map/ppermute | solution.py:312
  19.3 9.3 %collective-permute-start.1 = (bf16[80,512]{1,0:T(8,128)(2,1)S(1)}, bf16[80,512]{1,0:T(8,128)(2,1)S(1)}, u32[]{:S(2)}, u32[]{:S(2)}) collective-permute-start(bf16[80,512]{1,0:T(8,128)(2,1)S(1)} %pad_maximum_fusion), channel_id=1, source_target_pairs={{0,32},{16,48},{32,0},{48,16},{64,96},{80,112},{96,64},{112,80},{1... | collective-permute-start | bytes 245768 | tf_op jit(solution)/shard_map/ppermute | solution.py:312
  28.5 7.8 %collective-permute-start.2 = (bf16[80,1024]{1,0:T(8,128)(2,1)S(1)}, bf16[80,1024]{1,0:T(8,128)(2,1)S(1)}, u32[]{:S(2)}, u32[]{:S(2)}) collective-permute-start(bf16[80,1024]{1,0:T(8,128)(2,1)S(1)} %constant_dynamic-update-slice_fusion.y_ref.refs_0_), channel_id=1, source_target_pairs={{0,16},{16,0},{32,48},{48,32},{64,80},{80,64},{96,112},{112,96},{1... | collective-permute-start | bytes 491528 | tf_op jit(solution)/shard_map/ppermute | solution.py:312
  30.8 0.7 copy-start.1
  31.4 4.9 %copy-start = (f32[2048]{0:T(1024)S(1)}, f32[2048]{0:T(1024)}, u32[]{:S(2)}) copy-start(f32[2048]{0:T(1024)} %param.6) | copy-start | bytes 24580
  62.4 13.4 %copy-start.2 = (bf16[2048,64]{0,1:T(8,128)(2,1)S(1)}, bf16[2048,64]{0,1:T(8,128)(2,1)}, u32[]{:S(2)}) copy-start(bf16[2048,64]{0,1:T(8,128)(2,1)} %param.5) | copy-start | bytes 786436
  62.5 15.4 %collective-permute-start.3 = (f32[4,2048]{1,0:T(4,128)S(1)}, f32[4,2048]{1,0:T(4,128)S(1)}, u32[]{:S(2)}, u32[]{:S(2)}) collective-permute-start(f32[4,2048]{1,0:T(4,128)S(1)} %log_add_fusion.1), channel_id=1, source_target_pairs={{0,8},{1,9},{2,10},{3,11},{4,12},{5,13},{6,14},{7,15},{8,0},{9,1},... | collective-permute-start | bytes 98312 | tf_op jit(solution)/shard_map/ppermute | solution.py:315
  111.7 40.7 %collective-permute-start.4 = (f32[4,256]{1,0:T(4,128)S(1)}, f32[4,256]{1,0:T(4,128)S(1)}, u32[]{:S(2)}, u32[]{:S(2)}) collective-permute-start(f32[4,256]{1,0:T(4,128)S(1)} %shard_map.72), channel_id=1, source_target_pairs={{0,64},{16,80},{32,96},{48,112},{64,0},{80,16},{96,32},{112,48},{1... | collective-permute-start | bytes 12296 | tf_op jit(solution)/shard_map/ppermute | solution.py:312
  153.0 10.3 %all-to-all-start.3 = ((f32[4,1,256]{2,1,0:T(1,128)}), f32[4,1,256]{2,1,0:T(1,128)S(1)}, u32[]{:S(2)}, u32[]{:S(2)}) async-start(f32[4,1,256]{2,1,0:T(1,128)} %copy.11), calls=%async_computation.3 | async-start | bytes 8192 | tf_op jit(solution)/shard_map/all_to_all | solution.py:423

commit v10 on v9

--- a/solution.py
+++ b/solution.py
@@ -40,7 +40,7 @@
 
 
 def prepare_kernel(
-    x_in, y_in, logw_in, potential_in, out_ref, offset_ref, copies_ref, x_ref, y_ref, logw_ref, potential_ref, sem
+    x_in, y_in, logw_in, potential_in, out_ref, copies_ref, x_ref, y_ref, logw_ref, potential_ref, sem
 ):
     count = copies_ref.shape[0]
     pairs = [(x_in, x_ref), (y_in, y_ref), (logw_in, logw_ref), (potential_in, potential_ref)]
@@ -57,13 +57,11 @@
     for move in moves[1:4]:
         move.wait()
     y = y_ref[...].astype(jnp.float32)
-    offset = potential_ref[...] * 2.0 + logw_ref[...]
-    bias = offset - jnp.sum(y * y, axis=0, keepdims=True)
+    bias = potential_ref[...] * 2.0 + logw_ref[...] - jnp.sum(y * y, axis=0, keepdims=True)
     out_ref[0:FEATURES, :] = (y * 2.0).astype(jnp.bfloat16)
     out_ref[FEATURES : FEATURES + EXTRA, :] = extra_block(
         three_parts(bias), ones_of(bias.shape[1])
     ).astype(jnp.bfloat16)
-    offset_ref[...] = offset
     for move in moves[4:]:
         move.wait()
 
@@ -107,8 +105,7 @@
         before_ref, logw_ref, yt_ref, l_ref, sums_ref = refs
         turn_kernel(y_ref, yt_ref)
     else:
-        offset_ref, yt_ref, l_ref, kept_ref, sums_ref = refs
-        kept_ref[...] = offset_ref[...]
+        yt_ref, l_ref, sums_ref = refs
     rows = yt_ref.shape[0]
     ny, _, per = x_ref.shape
     row_step = min(ROWS, rows)
@@ -319,11 +316,10 @@
         return lax.all_to_all(spread, axis, 0, 0, axis_index_groups=groups, tiled=True)
 
     x = source_latent.T
-    y, offset, copies = call(
+    y, copies = call(
         prepare_kernel,
         (
             jax.ShapeDtypeStruct((depth, each), bf16),
-            jax.ShapeDtypeStruct((1, each), f32),
             jax.ShapeDtypeStruct((ny, FEATURES, per), bf16),
         ),
         [
@@ -340,7 +336,7 @@
         target_logw.reshape(1, each),
         target_potential.reshape(1, each),
         spaces=[pl.ANY] * 4,
-        out=(pltpu.VMEM, pltpu.VMEM, pl.ANY),
+        out=(pltpu.VMEM, pl.ANY),
         limit=60,
     )
     xs = lax.all_to_all(copies, "blk", 0, 0, axis_index_groups=y_groups, tiled=True)
@@ -351,7 +347,7 @@
     far = along_z(y, 1)
 
     def first(block, *more):
-        last = len(more) == 2 and more[0].shape[0] == ny
+        last = len(more) == 2
         return call(
             functools.partial(first_kernel, last),
             (
@@ -359,7 +355,7 @@
                 jax.ShapeDtypeStruct((ny, per + per // ny), f32),
             )
             if last
-            else (jax.ShapeDtypeStruct((ny, per), f32), jax.ShapeDtypeStruct((1, each), f32)),
+            else jax.ShapeDtypeStruct((ny, per), f32),
             [pltpu.VMEM((ny, 8, per), f32)],
             2 * pairs * DEPTH,
             pairs,
@@ -375,13 +371,15 @@
         0,
         0,
         y,
-        moved=11 * 10**6,
+        moved=27 * 10**6,
     )
-    total, offset = first(y, offset, yt_near)
+    total = first(y, yt_near)
     yt_far, total = first(far, total, source_logw.reshape(1, per))
     got = shared(total, "blk", y_groups)
     total = log_sum(got[:, :, :per])
     total = log_sum(shared(total, "wide", x_groups))
+    potential, total = lax.optimization_barrier((target_potential, total))
+    offset = lax.optimization_barrier(potential * 2.0 + target_logw)
     total = join(total, along_wide(total, nw // 2))
     sq = jnp.sum(jnp.square(x.astype(f32)), axis=0, keepdims=True)
     mine = lax.dynamic_slice(total, (my_y, 0), (1, per))
@@ -421,7 +419,7 @@
     arrived = along_z(sent, count)
     sums = join(second(tuple(b for b in blocks if b[2] < count), yt_near), arrived)
     sums = lax.all_to_all(sums, "blk", 0, 0, axis_index_groups=quarters, tiled=True)
-    new_target_potential = -0.5 * (log_sum(sums) - offset[0])
+    new_target_potential = -0.5 * (log_sum(sums) - offset)
     return source_potential.reshape(per), new_target_potential
 
 

time: 165 us -> 166 us (level)
  blocking collectives: 20.7 us -> 10.7 us
  waiting for transfers between devices: 13.4 us -> 18.8 us
  starting transfers between devices: 45.8 us -> 51 us
    all_to_all x2 -> x1, blocking collectives: 20.7 us -> 10.7 us  [shared(): lax.all_to_all(spread, axis, 0, 0, axis_index_groups=groups, tiled=True)]
    all_to_all x0 -> x1, waiting for transfers between devices: none -> 5.37 us  [shared(): lax.all_to_all(spread, axis, 0, 0, axis_index_groups=groups, tiled=True)]
    all_to_all x0 -> x1, starting transfers between devices: none -> 5.18 us  [shared(): lax.all_to_all(spread, axis, 0, 0, axis_index_groups=groups, tiled=True)]
  transfers between devices with their start and end apart: 7 -> 8, of which waited for: 4 -> 5; matrix products, arithmetic and copies ran while one was open for 0% -> 0% of each run, Pallas kernels for 24% -> 24%
where the time goes in v10:
time: 166 us; the launch traced here: 164 us
  Pallas kernels  79.9 us (48%)
  starting transfers between devices  51 us (31%)
  waiting for transfers between devices  18.8 us (11%)
  blocking collectives  10.7 us (6%)
    pallas_call x6, Pallas kernels, call(): pl.pallas_call(kernel, out_shape=outs, in_specs=[pl.BlockSpec(memory_spac...  79.9 us
    ppermute x4, starting transfers between devices, along_z(): return lax.ppermute(value, 'blk', perm)  23.3 us
    ppermute x1, starting transfers between devices, along_wide(): return lax.ppermute(value, 'wide', [(w, w ^ k) for w in range(nw)])  13.2 us
    all_to_all x1, blocking collectives, shared(): lax.all_to_all(spread, axis, 0, 0, axis_index_groups=groups, tiled=True)  10.7 us
    ppermute x4, waiting for transfers between devices, along_z(): return lax.ppermute(value, 'blk', perm)  6.49 us
    all_to_all x1, waiting for transfers between devices, shared(): lax.all_to_all(spread, axis, 0, 0, axis_index_groups=groups, tiled=True)  5.37 us
    all_to_all x1, starting transfers between devices, shared(): lax.all_to_all(spread, axis, 0, 0, axis_index_groups=groups, tiled=True)  5.18 us
    all_to_all x1, waiting for transfers between devices, per_device(): lax.all_to_all(sums, 'blk', 0, 0, axis_index_groups=quarters, tiled=True)  4.96 us
  transfers between devices with their start and end apart: 8, of which 5 were waited for; matrix products, arithmetic and copies ran while one was open for 0% of the time, Pallas kernels for 24%

profile of v10, /device:TPU:6, one launch (start us, length us, event | category | flops | bytes accessed | tf_op | source)
XLA Modules:
  0.0 164.3 jit_solution(17153226604171251772)
XLA Ops:
  0.6 2.6 %shard_map.68 = (bf16[80,256]{1,0:T(8,128)(2,1)}, bf16[4,64,2048]{2,1,0:T(8,128)(2,1)}) custom-call(bf16[64,2048]{1,0:T(8,128)(2,1)} %bitcast.18, bf16[64,256]{1,0:T(8,128)(2,1)} %bitcast.19, f32[1,256]{1,0:T(1,128)} %bitcast.22, f32[1,256]{1,0:T(1,128)} %bitcast.23), custom_call_target="tpu_custom_call" | custom-call | flops 65536 | bytes 4194304 | tf_op jit(solution)/shard_map/pallas_call | solution.py:274
  3.3 4.5 %all-to-all-start = ((bf16[4,64,2048]{2,1,0:T(8,128)(2,1)}), bf16[4,64,2048]{2,1,0:T(8,128)(2,1)S(1)}, u32[]{:S(2)}, u32[]{:S(2)}) async-start(bf16[4,64,2048]{2,1,0:T(8,128)(2,1)} %get-tuple-element.11), calls=%async_computation | async-start | bytes 2097152 | tf_op jit(solution)/shard_map/all_to_all | solution.py:342
  7.7 9.1 %collective-permute-start = (bf16[80,256]{1,0:T(8,128)(2,1)S(1)}, bf16[80,256]{1,0:T(8,128)(2,1)S(1)}, u32[]{:S(2)}, u32[]{:S(2)}) collective-permute-start(bf16[80,256]{1,0:T(8,128)(2,1)S(1)} %copy-done.2), channel_id=1, source_target_pairs={{0,64},{16,80},{32,96},{48,112},{64,0},{80,16},{96,32},{112,48},{1... | collective-permute-start | bytes 122888 | tf_op jit(solution)/shard_map/ppermute | solution.py:309
  16.9 2.4 %collective-permute-done = bf16[80,256]{1,0:T(8,128)(2,1)S(1)} collective-permute-done((bf16[80,256]{1,0:T(8,128)(2,1)S(1)}, bf16[80,256]{1,0:T(8,128)(2,1)S(1)}, u32[]{:S(2)}, u32[]{:S(2)}) %collective-permute-start) | collective-permute-done | bytes 40992 | tf_op jit(solution)/shard_map/ppermute | solution.py:309
  19.3 5.2 %collective-permute-start.1 = (bf16[80,512]{1,0:T(8,128)(2,1)S(1)}, bf16[80,512]{1,0:T(8,128)(2,1)S(1)}, u32[]{:S(2)}, u32[]{:S(2)}) collective-permute-start(bf16[80,512]{1,0:T(8,128)(2,1)S(1)} %pad_maximum_fusion), channel_id=1, source_target_pairs={{0,32},{16,48},{32,0},{48,16},{64,96},{80,112},{96,64},{112,80},{1... | collective-permute-start | bytes 245768 | tf_op jit(solution)/shard_map/ppermute | solution.py:309
  24.4 4.1 %collective-permute-done.1 = bf16[80,512]{1,0:T(8,128)(2,1)S(1)} collective-permute-done((bf16[80,512]{1,0:T(8,128)(2,1)S(1)}, bf16[80,512]{1,0:T(8,128)(2,1)S(1)}, u32[]{:S(2)}, u32[]{:S(2)}) %collective-permute-start.1) | collective-permute-done | bytes 81952 | tf_op jit(solution)/shard_map/ppermute | solution.py:309
  28.5 2.1 %collective-permute-start.2 = (bf16[80,1024]{1,0:T(8,128)(2,1)S(1)}, bf16[80,1024]{1,0:T(8,128)(2,1)S(1)}, u32[]{:S(2)}, u32[]{:S(2)}) collective-permute-start(bf16[80,1024]{1,0:T(8,128)(2,1)S(1)} %constant_dynamic-update-slice_fusion.y_ref.refs_0_), channel_id=1, source_target_pairs={{0,16},{16,0},{32,48},{48,32},{64,80},{80,64},{96,112},{112,96},{1... | collective-permute-start | bytes 491528 | tf_op jit(solution)/shard_map/ppermute | solution.py:309
  30.6 0.1 shard_map.69.refs_2_.near_ref
  30.8 4.9 %shard_map.70.refs_2_ = f32[4,2048]{1,0:T(4,128)S(1)} custom-call(bf16[80,1024]{1,0:T(8,128)(2,1)S(1)} %constant_dynamic-update-slice_fusion.y_ref.refs_0_, bf16[4,64,2048]{2,1,0:T(8,128)(2,1)S(1)} %all-to-all-done.refs_1_.x_ref, bf16[1024,128]{1,0:T(8,128)(2,1)S(1)} %shard_map.69.refs_2_.near_ref), custom_call_target="tpu_custom_call" | custom-call | flops 2147483648 | bytes 4194304 | tf_op jit(solution)/shard_map/pallas_call | solution.py:274
  35.7 5.0 %shard_map.71 = (bf16[1024,128]{1,0:T(8,128)(2,1)S(1)}, f32[4,2560]{1,0:T(4,128)S(1)}) custom-call(bf16[80,1024]{1,0:T(8,128)(2,1)S(1)} %collective-permute-done.2.refs_0_, bf16[4,64,2048]{2,1,0:T(8,128)(2,1)S(1)} %all-to-all-done.refs_1_.x_ref, f32[4,2048]{1,0:T(4,128)S(1)} %shard_map.70.refs_2_, f32[1,2048]{1,0:T(1,128)S(1)} %bitcast.17), custom_call_target="tpu_custom_call" | custom-call | flops 2147483648 | bytes 4194304 | tf_op jit(solution)/shard_map/pallas_call | solution.py:274
  40.7 10.7 %all_to_all.27.logw_ref = f32[4,4,2560]{2,1,0:T(4,128)S(1)} all-to-all(f32[4,4,2560]{2,1,0:T(4,128)S(1)} %broadcast_in_dim.6), channel_id=1, replica_groups={{0,128,256,384},{16,144,272,400},{32,160,288,416},{48,176,304,432},{64,..., dimensions={0} | all-to-all | bytes 327680 | tf_op jit(solution)/shard_map/all_to_all | solution.py:316
  51.5 0.7 broadcast_in_dim.7
  52.3 5.2 %all-to-all-start.2 = ((f32[8,4,2048]{2,1,0:T(4,128)}), f32[8,4,2048]{2,1,0:T(4,128)S(1)}, u32[]{:S(2)}, u32[]{:S(2)}) async-start(f32[8,4,2048]{2,1,0:T(4,128)} %broadcast_in_dim.7), calls=%async_computation.2 | async-start | bytes 524288 | tf_op jit(solution)/shard_map/all_to_all | solution.py:316
  57.5 5.4 %all-to-all-done.2 = f32[8,4,2048]{2,1,0:T(4,128)S(1)} async-done(((f32[8,4,2048]{2,1,0:T(4,128)}), f32[8,4,2048]{2,1,0:T(4,128)S(1)}, u32[]{:S(2)}, u32[]{:S(2)}) %all-to-all-start.2) | async-done | bytes 262176 | tf_op jit(solution)/shard_map/all_to_all | solution.py:316
  63.1 13.2 %collective-permute-start.3 = (f32[4,2048]{1,0:T(4,128)S(1)}, f32[4,2048]{1,0:T(4,128)S(1)}, u32[]{:S(2)}, u32[]{:S(2)}) collective-permute-start(f32[4,2048]{1,0:T(4,128)S(1)} %log_add_fusion.1), channel_id=1, source_target_pairs={{0,8},{1,9},{2,10},{3,11},{4,12},{5,13},{6,14},{7,15},{8,0},{9,1},... | collective-permute-start | bytes 98312 | tf_op jit(solution)/shard_map/ppermute | solution.py:312
  76.4 2.0 %collective-permute-done.3 = f32[4,2048]{1,0:T(4,128)S(1)} collective-permute-done((f32[4,2048]{1,0:T(4,128)S(1)}, f32[4,2048]{1,0:T(4,128)S(1)}, u32[]{:S(2)}, u32[]{:S(2)}) %collective-permute-start.3) | collective-permute-done | bytes 32800 | tf_op jit(solution)/shard_map/ppermute | solution.py:312
  78.4 33.7 %shard_map.72 = f32[4,256]{1,0:T(4,128)S(1)} custom-call(s32[1]{0:T(128)} %bitcast.7.place_ref, bf16[1024,128]{1,0:T(8,128)(2,1)S(1)} %shard_map.69.refs_2_.near_ref, bf16[1024,128]{1,0:T(8,128)(2,1)S(1)} %get-tuple-element.14.far_ref, bf16[4,64,2048]{2,1,0:T(8,128)(2,1)S(1)} %all-to-all-done.refs_1_.x_ref, f32[4,2048]{1,0:T(4,128)S(1)} %log_add_fusion.total_ref, ...), custom_call_target="tpu_custom_call" | custom-call | flops 2147483648 | bytes 4194304 | tf_op jit(solution)/shard_map/pallas_call | solution.py:274
  112.1 6.9 %collective-permute-start.4 = (f32[4,256]{1,0:T(4,128)S(1)}, f32[4,256]{1,0:T(4,128)S(1)}, u32[]{:S(2)}, u32[]{:S(2)}) collective-permute-start(f32[4,256]{1,0:T(4,128)S(1)} %shard_map.72), channel_id=1, source_target_pairs={{0,64},{16,80},{32,96},{48,112},{64,0},{80,16},{96,32},{112,48},{1... | collective-permute-start | bytes 12296 | tf_op jit(solution)/shard_map/ppermute | solution.py:309
  119.0 33.7 %shard_map.73 = f32[4,256]{1,0:T(4,128)S(1)} custom-call(s32[1]{0:T(128)} %bitcast.7.place_ref, bf16[1024,128]{1,0:T(8,128)(2,1)S(1)} %shard_map.69.refs_2_.near_ref, bf16[1024,128]{1,0:T(8,128)(2,1)S(1)} %get-tuple-element.14.far_ref, bf16[4,64,2048]{2,1,0:T(8,128)(2,1)S(1)} %all-to-all-done.refs_1_.x_ref, f32[4,2048]{1,0:T(4,128)S(1)} %log_add_fusion.total_ref, ...), custom_call_target="tpu_custom_call" | custom-call | flops 2147483648 | bytes 4194304 | tf_op jit(solution)/shard_map/pallas_call | solution.py:274
  152.7 0.6 copy.11
  153.3 4.8 %all-to-all-start.3 = ((f32[4,1,256]{2,1,0:T(1,128)}), f32[4,1,256]{2,1,0:T(1,128)S(1)}, u32[]{:S(2)}, u32[]{:S(2)}) async-start(f32[4,1,256]{2,1,0:T(1,128)} %copy.11), calls=%async_computation.3 | async-start | bytes 8192 | tf_op jit(solution)/shard_map/all_to_all | solution.py:421
  158.1 0.6 subtract_multiply_fusion
  158.7 5.0 %all-to-all-done.3 = f32[4,1,256]{2,1,0:T(1,128)S(1)} async-done(((f32[4,1,256]{2,1,0:T(1,128)}), f32[4,1,256]{2,1,0:T(1,128)S(1)}, u32[]{:S(2)}, u32[]{:S(2)}) %all-to-all-start.3) | async-done | bytes 4128 | tf_op jit(solution)/shard_map/all_to_all | solution.py:421
  163.7 0.6 subtract_multiply_fusion.1
  (30 shorter events, 0.6 us)
Async XLA Ops:
  3.3 4.5 %copy-start.2 = (bf16[80,256]{1,0:T(8,128)(2,1)S(1)}, bf16[80,256]{1,0:T(8,128)(2,1)}, u32[]{:S(2)}) copy-start(bf16[80,256]{1,0:T(8,128)(2,1)} %get-tuple-element.10) | copy-start | bytes 122884
  3.3 27.5 %all-to-all-start = ((bf16[4,64,2048]{2,1,0:T(8,128)(2,1)}), bf16[4,64,2048]{2,1,0:T(8,128)(2,1)S(1)}, u32[]{:S(2)}, u32[]{:S(2)}) async-start(bf16[4,64,2048]{2,1,0:T(8,128)(2,1)} %get-tuple-element.11), calls=%async_computation | async-start | bytes 2097152 | tf_op jit(solution)/shard_map/all_to_all | solution.py:342
  7.7 11.5 %collective-permute-start = (bf16[80,256]{1,0:T(8,128)(2,1)S(1)}, bf16[80,256]{1,0:T(8,128)(2,1)S(1)}, u32[]{:S(2)}, u32[]{:S(2)}) collective-permute-start(bf16[80,256]{1,0:T(8,128)(2,1)S(1)} %copy-done.2), channel_id=1, source_target_pairs={{0,64},{16,80},{32,96},{48,112},{64,0},{80,16},{96,32},{112,48},{1... | collective-permute-start | bytes 122888 | tf_op jit(solution)/shard_map/ppermute | solution.py:309
  19.3 9.3 %collective-permute-start.1 = (bf16[80,512]{1,0:T(8,128)(2,1)S(1)}, bf16[80,512]{1,0:T(8,128)(2,1)S(1)}, u32[]{:S(2)}, u32[]{:S(2)}) collective-permute-start(bf16[80,512]{1,0:T(8,128)(2,1)S(1)} %pad_maximum_fusion), channel_id=1, source_target_pairs={{0,32},{16,48},{32,0},{48,16},{64,96},{80,112},{96,64},{112,80},{1... | collective-permute-start | bytes 245768 | tf_op jit(solution)/shard_map/ppermute | solution.py:309
  28.5 7.2 %collective-permute-start.2 = (bf16[80,1024]{1,0:T(8,128)(2,1)S(1)}, bf16[80,1024]{1,0:T(8,128)(2,1)S(1)}, u32[]{:S(2)}, u32[]{:S(2)}) collective-permute-start(bf16[80,1024]{1,0:T(8,128)(2,1)S(1)} %constant_dynamic-update-slice_fusion.y_ref.refs_0_), channel_id=1, source_target_pairs={{0,16},{16,0},{32,48},{48,32},{64,80},{80,64},{96,112},{112,96},{1... | collective-permute-start | bytes 491528 | tf_op jit(solution)/shard_map/ppermute | solution.py:309
  30.8 5.0 %copy-start = (f32[2048]{0:T(1024)S(1)}, f32[2048]{0:T(1024)}, u32[]{:S(2)}) copy-start(f32[2048]{0:T(1024)} %param.6) | copy-start | bytes 24580
  52.3 5.2 %copy-start.1 = (bf16[2048,64]{0,1:T(8,128)(2,1)S(1)}, bf16[2048,64]{0,1:T(8,128)(2,1)}, u32[]{:S(2)}) copy-start(bf16[2048,64]{0,1:T(8,128)(2,1)} %param.5) | copy-start | bytes 786436
  52.3 10.6 %all-to-all-start.2 = ((f32[8,4,2048]{2,1,0:T(4,128)}), f32[8,4,2048]{2,1,0:T(4,128)S(1)}, u32[]{:S(2)}, u32[]{:S(2)}) async-start(f32[8,4,2048]{2,1,0:T(4,128)} %broadcast_in_dim.7), calls=%async_computation.2 | async-start | bytes 524288 | tf_op jit(solution)/shard_map/all_to_all | solution.py:316
  63.1 13.3 %copy-start.3 = (f32[256]{0:T(256)S(1)}, f32[256]{0:T(256)}, u32[]{:S(2)}) copy-start(f32[256]{0:T(256)} %param.8) | copy-start | bytes 3076
  63.1 13.3 %copy-start.4 = (f32[256]{0:T(256)S(1)}, f32[256]{0:T(256)}, u32[]{:S(2)}) copy-start(f32[256]{0:T(256)} %param.9) | copy-start | bytes 3076
  63.1 15.3 %collective-permute-start.3 = (f32[4,2048]{1,0:T(4,128)S(1)}, f32[4,2048]{1,0:T(4,128)S(1)}, u32[]{:S(2)}, u32[]{:S(2)}) collective-permute-start(f32[4,2048]{1,0:T(4,128)S(1)} %log_add_fusion.1), channel_id=1, source_target_pairs={{0,8},{1,9},{2,10},{3,11},{4,12},{5,13},{6,14},{7,15},{8,0},{9,1},... | collective-permute-start | bytes 98312 | tf_op jit(solution)/shard_map/ppermute | solution.py:312
  112.1 40.6 %collective-permute-start.4 = (f32[4,256]{1,0:T(4,128)S(1)}, f32[4,256]{1,0:T(4,128)S(1)}, u32[]{:S(2)}, u32[]{:S(2)}) collective-permute-start(f32[4,256]{1,0:T(4,128)S(1)} %shard_map.72), channel_id=1, source_target_pairs={{0,64},{16,80},{32,96},{48,112},{64,0},{80,16},{96,32},{112,48},{1... | collective-permute-start | bytes 12296 | tf_op jit(solution)/shard_map/ppermute | solution.py:309
  153.3 10.4 %all-to-all-start.3 = ((f32[4,1,256]{2,1,0:T(1,128)}), f32[4,1,256]{2,1,0:T(1,128)S(1)}, u32[]{:S(2)}, u32[]{:S(2)}) async-start(f32[4,1,256]{2,1,0:T(1,128)} %copy.11), calls=%async_computation.3 | async-start | bytes 8192 | tf_op jit(solution)/shard_map/all_to_all | solution.py:421

commit v11 on v10

--- a/solution.py
+++ b/solution.py
@@ -371,17 +371,17 @@
         0,
         0,
         y,
-        moved=27 * 10**6,
+        moved=60 * 10**6,
     )
     total = first(y, yt_near)
     yt_far, total = first(far, total, source_logw.reshape(1, per))
     got = shared(total, "blk", y_groups)
     total = log_sum(got[:, :, :per])
     total = log_sum(shared(total, "wide", x_groups))
-    potential, total = lax.optimization_barrier((target_potential, total))
+    potential, mine, total = lax.optimization_barrier((target_potential, x, total))
     offset = lax.optimization_barrier(potential * 2.0 + target_logw)
+    sq = lax.optimization_barrier(jnp.sum(jnp.square(mine.astype(f32)), axis=0, keepdims=True))
     total = join(total, along_wide(total, nw // 2))
-    sq = jnp.sum(jnp.square(x.astype(f32)), axis=0, keepdims=True)
     mine = lax.dynamic_slice(total, (my_y, 0), (1, per))
     source_potential = -0.5 * (mine - sq)
 

time: 166 us -> 166 us (level)
  transfers between devices with their start and end apart: 8 -> 8, of which waited for: 5 -> 5; matrix products, arithmetic and copies ran while one was open for 0% -> 0% of each run, Pallas kernels for 24% -> 23%
where the time goes in v11:
time: 166 us; the launch traced here: 165 us
  Pallas kernels  79.9 us (48%)
  starting transfers between devices  50.8 us (31%)
  waiting for transfers between devices  18.8 us (11%)
  blocking collectives  10.7 us (6%)
  local copies, waits for them, and re-layouts  2.04 us (1%)
    pallas_call x6, Pallas kernels, call(): pl.pallas_call(kernel, out_shape=outs, in_specs=[pl.BlockSpec(memory_spac...  79.9 us
    ppermute x4, starting transfers between devices, along_z(): return lax.ppermute(value, 'blk', perm)  23.3 us
    ppermute x1, starting transfers between devices, along_wide(): return lax.ppermute(value, 'wide', [(w, w ^ k) for w in range(nw)])  13.2 us
    all_to_all x1, blocking collectives, shared(): lax.all_to_all(spread, axis, 0, 0, axis_index_groups=groups, tiled=True)  10.7 us
    ppermute x4, waiting for transfers between devices, along_z(): return lax.ppermute(value, 'blk', perm)  6.49 us
    all_to_all x1, waiting for transfers between devices, shared(): lax.all_to_all(spread, axis, 0, 0, axis_index_groups=groups, tiled=True)  5.45 us
    all_to_all x1, starting transfers between devices, shared(): lax.all_to_all(spread, axis, 0, 0, axis_index_groups=groups, tiled=True)  5.05 us
    all_to_all x1, waiting for transfers between devices, per_device(): lax.all_to_all(sums, 'blk', 0, 0, axis_index_groups=quarters, tiled=True)  4.96 us
  transfers between devices with their start and end apart: 8, of which 5 were waited for; matrix products, arithmetic and copies ran while one was open for 0% of the time, Pallas kernels for 23%

profile of v11, /device:TPU:6, one launch (start us, length us, event | category | flops | bytes accessed | tf_op | source)
XLA Modules:
  0.0 164.8 jit_solution(18292998083949479308)
XLA Ops:
  0.6 2.6 %shard_map.68 = (bf16[80,256]{1,0:T(8,128)(2,1)}, bf16[4,64,2048]{2,1,0:T(8,128)(2,1)}) custom-call(bf16[64,2048]{1,0:T(8,128)(2,1)} %bitcast.17, bf16[64,256]{1,0:T(8,128)(2,1)} %bitcast.19, f32[1,256]{1,0:T(1,128)} %bitcast.22, f32[1,256]{1,0:T(1,128)} %bitcast.23), custom_call_target="tpu_custom_call" | custom-call | flops 65536 | bytes 4194304 | tf_op jit(solution)/shard_map/pallas_call | solution.py:274
  3.3 4.5 %all-to-all-start = ((bf16[4,64,2048]{2,1,0:T(8,128)(2,1)}), bf16[4,64,2048]{2,1,0:T(8,128)(2,1)S(1)}, u32[]{:S(2)}, u32[]{:S(2)}) async-start(bf16[4,64,2048]{2,1,0:T(8,128)(2,1)} %get-tuple-element.12), calls=%async_computation | async-start | bytes 2097152 | tf_op jit(solution)/shard_map/all_to_all | solution.py:342
  7.7 9.1 %collective-permute-start = (bf16[80,256]{1,0:T(8,128)(2,1)S(1)}, bf16[80,256]{1,0:T(8,128)(2,1)S(1)}, u32[]{:S(2)}, u32[]{:S(2)}) collective-permute-start(bf16[80,256]{1,0:T(8,128)(2,1)S(1)} %copy-done.2), channel_id=1, source_target_pairs={{0,64},{16,80},{32,96},{48,112},{64,0},{80,16},{96,32},{112,48},{1... | collective-permute-start | bytes 122888 | tf_op jit(solution)/shard_map/ppermute | solution.py:309
  16.9 2.4 %collective-permute-done = bf16[80,256]{1,0:T(8,128)(2,1)S(1)} collective-permute-done((bf16[80,256]{1,0:T(8,128)(2,1)S(1)}, bf16[80,256]{1,0:T(8,128)(2,1)S(1)}, u32[]{:S(2)}, u32[]{:S(2)}) %collective-permute-start) | collective-permute-done | bytes 40992 | tf_op jit(solution)/shard_map/ppermute | solution.py:309
  19.3 5.2 %collective-permute-start.1 = (bf16[80,512]{1,0:T(8,128)(2,1)S(1)}, bf16[80,512]{1,0:T(8,128)(2,1)S(1)}, u32[]{:S(2)}, u32[]{:S(2)}) collective-permute-start(bf16[80,512]{1,0:T(8,128)(2,1)S(1)} %pad_maximum_fusion), channel_id=1, source_target_pairs={{0,32},{16,48},{32,0},{48,16},{64,96},{80,112},{96,64},{112,80},{1... | collective-permute-start | bytes 245768 | tf_op jit(solution)/shard_map/ppermute | solution.py:309
  24.4 4.1 %collective-permute-done.1 = bf16[80,512]{1,0:T(8,128)(2,1)S(1)} collective-permute-done((bf16[80,512]{1,0:T(8,128)(2,1)S(1)}, bf16[80,512]{1,0:T(8,128)(2,1)S(1)}, u32[]{:S(2)}, u32[]{:S(2)}) %collective-permute-start.1) | collective-permute-done | bytes 81952 | tf_op jit(solution)/shard_map/ppermute | solution.py:309
  28.5 2.1 %collective-permute-start.2 = (bf16[80,1024]{1,0:T(8,128)(2,1)S(1)}, bf16[80,1024]{1,0:T(8,128)(2,1)S(1)}, u32[]{:S(2)}, u32[]{:S(2)}) collective-permute-start(bf16[80,1024]{1,0:T(8,128)(2,1)S(1)} %constant_dynamic-update-slice_fusion.y_ref.refs_0_), channel_id=1, source_target_pairs={{0,16},{16,0},{32,48},{48,32},{64,80},{80,64},{96,112},{112,96},{1... | collective-permute-start | bytes 491528 | tf_op jit(solution)/shard_map/ppermute | solution.py:309
  30.8 4.9 %shard_map.70.refs_2_ = f32[4,2048]{1,0:T(4,128)S(1)} custom-call(bf16[80,1024]{1,0:T(8,128)(2,1)S(1)} %constant_dynamic-update-slice_fusion.y_ref.refs_0_, bf16[4,64,2048]{2,1,0:T(8,128)(2,1)S(1)} %all-to-all-done.refs_1_.x_ref, bf16[1024,128]{1,0:T(8,128)(2,1)S(1)} %shard_map.69.refs_2_.near_ref), custom_call_target="tpu_custom_call" | custom-call | flops 2147483648 | bytes 4194304 | tf_op jit(solution)/shard_map/pallas_call | solution.py:274
  35.7 5.0 %shard_map.71 = (bf16[1024,128]{1,0:T(8,128)(2,1)S(1)}, f32[4,2560]{1,0:T(4,128)S(1)}) custom-call(bf16[80,1024]{1,0:T(8,128)(2,1)S(1)} %collective-permute-done.2.refs_0_, bf16[4,64,2048]{2,1,0:T(8,128)(2,1)S(1)} %all-to-all-done.refs_1_.x_ref, f32[4,2048]{1,0:T(4,128)S(1)} %shard_map.70.refs_2_, f32[1,2048]{1,0:T(1,128)S(1)} %bitcast.16), custom_call_target="tpu_custom_call" | custom-call | flops 2147483648 | bytes 4194304 | tf_op jit(solution)/shard_map/pallas_call | solution.py:274
  40.7 10.7 %all_to_all.27.logw_ref = f32[4,4,2560]{2,1,0:T(4,128)S(1)} all-to-all(f32[4,4,2560]{2,1,0:T(4,128)S(1)} %broadcast_in_dim.6), channel_id=1, replica_groups={{0,128,256,384},{16,144,272,400},{32,160,288,416},{48,176,304,432},{64,..., dimensions={0} | all-to-all | bytes 327680 | tf_op jit(solution)/shard_map/all_to_all | solution.py:316
  51.5 0.7 broadcast_in_dim.7
  52.3 5.1 %all-to-all-start.2 = ((f32[8,4,2048]{2,1,0:T(4,128)}), f32[8,4,2048]{2,1,0:T(4,128)S(1)}, u32[]{:S(2)}, u32[]{:S(2)}) async-start(f32[8,4,2048]{2,1,0:T(4,128)} %broadcast_in_dim.7), calls=%async_computation.2 | async-start | bytes 524288 | tf_op jit(solution)/shard_map/all_to_all | solution.py:316
  57.3 5.4 %all-to-all-done.2 = f32[8,4,2048]{2,1,0:T(4,128)S(1)} async-done(((f32[8,4,2048]{2,1,0:T(4,128)}), f32[8,4,2048]{2,1,0:T(4,128)S(1)}, u32[]{:S(2)}, u32[]{:S(2)}) %all-to-all-start.2) | async-done | bytes 262176 | tf_op jit(solution)/shard_map/all_to_all | solution.py:316
  63.0 0.6 copy-done.3
  63.6 13.2 %collective-permute-start.3 = (f32[4,2048]{1,0:T(4,128)S(1)}, f32[4,2048]{1,0:T(4,128)S(1)}, u32[]{:S(2)}, u32[]{:S(2)}) collective-permute-start(f32[4,2048]{1,0:T(4,128)S(1)} %log_add_fusion.1), channel_id=1, source_target_pairs={{0,8},{1,9},{2,10},{3,11},{4,12},{5,13},{6,14},{7,15},{8,0},{9,1},... | collective-permute-start | bytes 98312 | tf_op jit(solution)/shard_map/ppermute | solution.py:312
  76.9 1.9 %collective-permute-done.3 = f32[4,2048]{1,0:T(4,128)S(1)} collective-permute-done((f32[4,2048]{1,0:T(4,128)S(1)}, f32[4,2048]{1,0:T(4,128)S(1)}, u32[]{:S(2)}, u32[]{:S(2)}) %collective-permute-start.3) | collective-permute-done | bytes 32800 | tf_op jit(solution)/shard_map/ppermute | solution.py:312
  78.9 33.7 %shard_map.72 = f32[4,256]{1,0:T(4,128)S(1)} custom-call(s32[1]{0:T(128)} %bitcast.7.place_ref, bf16[1024,128]{1,0:T(8,128)(2,1)S(1)} %shard_map.69.refs_2_.near_ref, bf16[1024,128]{1,0:T(8,128)(2,1)S(1)} %get-tuple-element.16.far_ref, bf16[4,64,2048]{2,1,0:T(8,128)(2,1)S(1)} %all-to-all-done.refs_1_.x_ref, f32[4,2048]{1,0:T(4,128)S(1)} %log_add_fusion.total_ref, ...), custom_call_target="tpu_custom_call" | custom-call | flops 2147483648 | bytes 4194304 | tf_op jit(solution)/shard_map/pallas_call | solution.py:274
  112.6 6.9 %collective-permute-start.4 = (f32[4,256]{1,0:T(4,128)S(1)}, f32[4,256]{1,0:T(4,128)S(1)}, u32[]{:S(2)}, u32[]{:S(2)}) collective-permute-start(f32[4,256]{1,0:T(4,128)S(1)} %shard_map.72), channel_id=1, source_target_pairs={{0,64},{16,80},{32,96},{48,112},{64,0},{80,16},{96,32},{112,48},{1... | collective-permute-start | bytes 12296 | tf_op jit(solution)/shard_map/ppermute | solution.py:309
  119.5 33.7 %shard_map.73 = f32[4,256]{1,0:T(4,128)S(1)} custom-call(s32[1]{0:T(128)} %bitcast.7.place_ref, bf16[1024,128]{1,0:T(8,128)(2,1)S(1)} %shard_map.69.refs_2_.near_ref, bf16[1024,128]{1,0:T(8,128)(2,1)S(1)} %get-tuple-element.16.far_ref, bf16[4,64,2048]{2,1,0:T(8,128)(2,1)S(1)} %all-to-all-done.refs_1_.x_ref, f32[4,2048]{1,0:T(4,128)S(1)} %log_add_fusion.total_ref, ...), custom_call_target="tpu_custom_call" | custom-call | flops 2147483648 | bytes 4194304 | tf_op jit(solution)/shard_map/pallas_call | solution.py:274
  153.2 0.6 copy.11
  153.8 4.8 %all-to-all-start.3 = ((f32[4,1,256]{2,1,0:T(1,128)}), f32[4,1,256]{2,1,0:T(1,128)S(1)}, u32[]{:S(2)}, u32[]{:S(2)}) async-start(f32[4,1,256]{2,1,0:T(1,128)} %copy.11), calls=%async_computation.3 | async-start | bytes 8192 | tf_op jit(solution)/shard_map/all_to_all | solution.py:421
  158.6 0.6 subtract_multiply_fusion
  159.2 5.0 %all-to-all-done.3 = f32[4,1,256]{2,1,0:T(1,128)S(1)} async-done(((f32[4,1,256]{2,1,0:T(1,128)}), f32[4,1,256]{2,1,0:T(1,128)S(1)}, u32[]{:S(2)}, u32[]{:S(2)}) %all-to-all-start.3) | async-done | bytes 4128 | tf_op jit(solution)/shard_map/all_to_all | solution.py:421
  164.2 0.6 subtract_multiply_fusion.1
  (30 shorter events, 0.7 us)
Async XLA Ops:
  3.3 4.5 %copy-start.2 = (bf16[80,256]{1,0:T(8,128)(2,1)S(1)}, bf16[80,256]{1,0:T(8,128)(2,1)}, u32[]{:S(2)}) copy-start(bf16[80,256]{1,0:T(8,128)(2,1)} %get-tuple-element.11) | copy-start | bytes 122884
  3.3 27.5 %all-to-all-start = ((bf16[4,64,2048]{2,1,0:T(8,128)(2,1)}), bf16[4,64,2048]{2,1,0:T(8,128)(2,1)S(1)}, u32[]{:S(2)}, u32[]{:S(2)}) async-start(bf16[4,64,2048]{2,1,0:T(8,128)(2,1)} %get-tuple-element.12), calls=%async_computation | async-start | bytes 2097152 | tf_op jit(solution)/shard_map/all_to_all | solution.py:342
  7.7 11.5 %collective-permute-start = (bf16[80,256]{1,0:T(8,128)(2,1)S(1)}, bf16[80,256]{1,0:T(8,128)(2,1)S(1)}, u32[]{:S(2)}, u32[]{:S(2)}) collective-permute-start(bf16[80,256]{1,0:T(8,128)(2,1)S(1)} %copy-done.2), channel_id=1, source_target_pairs={{0,64},{16,80},{32,96},{48,112},{64,0},{80,16},{96,32},{112,48},{1... | collective-permute-start | bytes 122888 | tf_op jit(solution)/shard_map/ppermute | solution.py:309
  19.3 9.3 %collective-permute-start.1 = (bf16[80,512]{1,0:T(8,128)(2,1)S(1)}, bf16[80,512]{1,0:T(8,128)(2,1)S(1)}, u32[]{:S(2)}, u32[]{:S(2)}) collective-permute-start(bf16[80,512]{1,0:T(8,128)(2,1)S(1)} %pad_maximum_fusion), channel_id=1, source_target_pairs={{0,32},{16,48},{32,0},{48,16},{64,96},{80,112},{96,64},{112,80},{1... | collective-permute-start | bytes 245768 | tf_op jit(solution)/shard_map/ppermute | solution.py:309
  28.5 7.2 %collective-permute-start.2 = (bf16[80,1024]{1,0:T(8,128)(2,1)S(1)}, bf16[80,1024]{1,0:T(8,128)(2,1)S(1)}, u32[]{:S(2)}, u32[]{:S(2)}) collective-permute-start(bf16[80,1024]{1,0:T(8,128)(2,1)S(1)} %constant_dynamic-update-slice_fusion.y_ref.refs_0_), channel_id=1, source_target_pairs={{0,16},{16,0},{32,48},{48,32},{64,80},{80,64},{96,112},{112,96},{1... | collective-permute-start | bytes 491528 | tf_op jit(solution)/shard_map/ppermute | solution.py:309
  30.8 5.0 %copy-start = (f32[2048]{0:T(1024)S(1)}, f32[2048]{0:T(1024)}, u32[]{:S(2)}) copy-start(f32[2048]{0:T(1024)} %param.6) | copy-start | bytes 24580
  52.3 10.5 %all-to-all-start.2 = ((f32[8,4,2048]{2,1,0:T(4,128)}), f32[8,4,2048]{2,1,0:T(4,128)S(1)}, u32[]{:S(2)}, u32[]{:S(2)}) async-start(f32[8,4,2048]{2,1,0:T(4,128)} %broadcast_in_dim.7), calls=%async_computation.2 | async-start | bytes 524288 | tf_op jit(solution)/shard_map/all_to_all | solution.py:316
  62.8 14.0 %copy-start.1 = (bf16[2048,64]{0,1:T(8,128)(2,1)S(1)}, bf16[2048,64]{0,1:T(8,128)(2,1)}, u32[]{:S(2)}) copy-start(bf16[2048,64]{0,1:T(8,128)(2,1)} %param.5) | copy-start | bytes 786436
  62.9 0.7 copy-start.3
  63.0 0.7 copy-start.4
  63.6 15.2 %collective-permute-start.3 = (f32[4,2048]{1,0:T(4,128)S(1)}, f32[4,2048]{1,0:T(4,128)S(1)}, u32[]{:S(2)}, u32[]{:S(2)}) collective-permute-start(f32[4,2048]{1,0:T(4,128)S(1)} %log_add_fusion.1), channel_id=1, source_target_pairs={{0,8},{1,9},{2,10},{3,11},{4,12},{5,13},{6,14},{7,15},{8,0},{9,1},... | collective-permute-start | bytes 98312 | tf_op jit(solution)/shard_map/ppermute | solution.py:312
  112.6 40.6 %collective-permute-start.4 = (f32[4,256]{1,0:T(4,128)S(1)}, f32[4,256]{1,0:T(4,128)S(1)}, u32[]{:S(2)}, u32[]{:S(2)}) collective-permute-start(f32[4,256]{1,0:T(4,128)S(1)} %shard_map.72), channel_id=1, source_target_pairs={{0,64},{16,80},{32,96},{48,112},{64,0},{80,16},{96,32},{112,48},{1... | collective-permute-start | bytes 12296 | tf_op jit(solution)/shard_map/ppermute | solution.py:309
  153.8 10.4 %all-to-all-start.3 = ((f32[4,1,256]{2,1,0:T(1,128)}), f32[4,1,256]{2,1,0:T(1,128)S(1)}, u32[]{:S(2)}, u32[]{:S(2)}) async-start(f32[4,1,256]{2,1,0:T(1,128)} %copy.11), calls=%async_computation.3 | async-start | bytes 8192 | tf_op jit(solution)/shard_map/all_to_all | solution.py:421

commit v12 on v9

--- a/solution.py
+++ b/solution.py
@@ -104,11 +104,11 @@
 def first_kernel(last, *refs):
     y_ref, x_ref, refs = refs[0], refs[1], refs[2:]
     if last:
-        before_ref, logw_ref, yt_ref, l_ref, sums_ref = refs
+        before_ref, logw_ref, offset_ref, yt_ref, l_ref, kept_ref, sums_ref = refs
         turn_kernel(y_ref, yt_ref)
+        kept_ref[...] = offset_ref[...]
     else:
-        offset_ref, yt_ref, l_ref, kept_ref, sums_ref = refs
-        kept_ref[...] = offset_ref[...]
+        yt_ref, l_ref, sums_ref = refs
     rows = yt_ref.shape[0]
     ny, _, per = x_ref.shape
     row_step = min(ROWS, rows)
@@ -270,9 +270,7 @@
         store(top + jnp.log(total))
 
 
-def call(
-    kernel, outs, scratch, flops, exps, *args, spaces=None, out=None, limit=40, moved=4 * 2**20
-):
+def call(kernel, outs, scratch, flops, exps, *args, spaces=None, out=None, limit=40):
     out = out or jax.tree.map(lambda _: pltpu.VMEM, outs)
     return pl.pallas_call(
         kernel,
@@ -284,7 +282,7 @@
         scratch_shapes=scratch,
         compiler_params=pltpu.CompilerParams(vmem_limit_bytes=limit * 2**20),
         cost_estimate=pl.CostEstimate(
-            flops=flops, bytes_accessed=moved, transcendentals=exps
+            flops=flops, bytes_accessed=4 * 2**20, transcendentals=exps
         ),
     )(*args)
 
@@ -351,15 +349,16 @@
     far = along_z(y, 1)
 
     def first(block, *more):
-        last = len(more) == 2 and more[0].shape[0] == ny
+        last = len(more) == 3
         return call(
             functools.partial(first_kernel, last),
             (
                 jax.ShapeDtypeStruct((half, DEPTH), bf16),
                 jax.ShapeDtypeStruct((ny, per + per // ny), f32),
+                jax.ShapeDtypeStruct((1, each), f32),
             )
             if last
-            else (jax.ShapeDtypeStruct((ny, per), f32), jax.ShapeDtypeStruct((1, each), f32)),
+            else jax.ShapeDtypeStruct((ny, per), f32),
             [pltpu.VMEM((ny, 8, per), f32)],
             2 * pairs * DEPTH,
             pairs,
@@ -375,10 +374,9 @@
         0,
         0,
         y,
-        moved=11 * 10**6,
     )
-    total, offset = first(y, offset, yt_near)
-    yt_far, total = first(far, total, source_logw.reshape(1, per))
+    total = first(y, yt_near)
+    yt_far, total, offset = first(far, total, source_logw.reshape(1, per), offset)
     got = shared(total, "blk", y_groups)
     total = log_sum(got[:, :, :per])
     total = log_sum(shared(total, "wide", x_groups))

time: 165 us -> 165 us (level)
  no operation moved by 1% of the time
where the time goes in v12:
time: 165 us; the launch traced here: 164 us
  Pallas kernels  80.1 us (49%)
  starting transfers between devices  46 us (28%)
  blocking collectives  20.7 us (13%)
  waiting for transfers between devices  13.3 us (8%)
    pallas_call x6, Pallas kernels, call(): pl.pallas_call(kernel, out_shape=outs, in_specs=[pl.BlockSpec(memory_spac...  80.1 us
    ppermute x4, starting transfers between devices, along_z(): return lax.ppermute(value, 'blk', perm)  23.3 us
    all_to_all x2, blocking collectives, shared(): lax.all_to_all(spread, axis, 0, 0, axis_index_groups=groups, tiled=True)  20.7 us
    ppermute x1, starting transfers between devices, along_wide(): return lax.ppermute(value, 'wide', [(w, w ^ k) for w in range(nw)])  13.5 us
    ppermute x4, waiting for transfers between devices, along_z(): return lax.ppermute(value, 'blk', perm)  6.47 us
    all_to_all x1, waiting for transfers between devices, per_device(): lax.all_to_all(sums, 'blk', 0, 0, axis_index_groups=quarters, tiled=True)  4.96 us
    all_to_all x1, starting transfers between devices, per_device(): lax.all_to_all(sums, 'blk', 0, 0, axis_index_groups=quarters, tiled=True)  4.81 us
    all_to_all x1, starting transfers between devices, per_device(): lax.all_to_all(copies, 'blk', 0, 0, axis_index_groups=y_groups, tiled=True)  4.48 us
  transfers between devices with their start and end apart: 7, of which 4 were waited for; matrix products, arithmetic and copies ran while one was open for 0% of the time, Pallas kernels for 24%

profile of v12, /device:TPU:6, one launch (start us, length us, event | category | flops | bytes accessed | tf_op | source)
XLA Modules:
  0.0 164.1 jit_solution(2083078644795901200)
XLA Ops:
  0.6 2.6 %shard_map.68 = (bf16[80,256]{1,0:T(8,128)(2,1)}, f32[1,256]{1,0:T(1,128)}, bf16[4,64,2048]{2,1,0:T(8,128)(2,1)}) custom-call(bf16[64,2048]{1,0:T(8,128)(2,1)} %bitcast.20, bf16[64,256]{1,0:T(8,128)(2,1)} %bitcast.21, f32[1,256]{1,0:T(1,128)} %bitcast.24, f32[1,256]{1,0:T(1,128)} %bitcast.25), custom_call_target="tpu_custom_call" | custom-call | flops 65536 | bytes 4194304 | tf_op jit(solution)/shard_map/pallas_call | solution.py:275
  3.3 4.5 %all-to-all-start = ((bf16[4,64,2048]{2,1,0:T(8,128)(2,1)}), bf16[4,64,2048]{2,1,0:T(8,128)(2,1)S(1)}, u32[]{:S(2)}, u32[]{:S(2)}) async-start(bf16[4,64,2048]{2,1,0:T(8,128)(2,1)} %get-tuple-element.11), calls=%async_computation | async-start | bytes 2097152 | tf_op jit(solution)/shard_map/all_to_all | solution.py:344
  7.8 9.1 %collective-permute-start = (bf16[80,256]{1,0:T(8,128)(2,1)S(1)}, bf16[80,256]{1,0:T(8,128)(2,1)S(1)}, u32[]{:S(2)}, u32[]{:S(2)}) collective-permute-start(bf16[80,256]{1,0:T(8,128)(2,1)S(1)} %copy-done.3), channel_id=1, source_target_pairs={{0,64},{16,80},{32,96},{48,112},{64,0},{80,16},{96,32},{112,48},{1... | collective-permute-start | bytes 122888 | tf_op jit(solution)/shard_map/ppermute | solution.py:310
  16.9 2.4 %collective-permute-done = bf16[80,256]{1,0:T(8,128)(2,1)S(1)} collective-permute-done((bf16[80,256]{1,0:T(8,128)(2,1)S(1)}, bf16[80,256]{1,0:T(8,128)(2,1)S(1)}, u32[]{:S(2)}, u32[]{:S(2)}) %collective-permute-start) | collective-permute-done | bytes 40992 | tf_op jit(solution)/shard_map/ppermute | solution.py:310
  19.3 5.2 %collective-permute-start.1 = (bf16[80,512]{1,0:T(8,128)(2,1)S(1)}, bf16[80,512]{1,0:T(8,128)(2,1)S(1)}, u32[]{:S(2)}, u32[]{:S(2)}) collective-permute-start(bf16[80,512]{1,0:T(8,128)(2,1)S(1)} %pad_maximum_fusion), channel_id=1, source_target_pairs={{0,32},{16,48},{32,0},{48,16},{64,96},{80,112},{96,64},{112,80},{1... | collective-permute-start | bytes 245768 | tf_op jit(solution)/shard_map/ppermute | solution.py:310
  24.4 4.1 %collective-permute-done.1 = bf16[80,512]{1,0:T(8,128)(2,1)S(1)} collective-permute-done((bf16[80,512]{1,0:T(8,128)(2,1)S(1)}, bf16[80,512]{1,0:T(8,128)(2,1)S(1)}, u32[]{:S(2)}, u32[]{:S(2)}) %collective-permute-start.1) | collective-permute-done | bytes 81952 | tf_op jit(solution)/shard_map/ppermute | solution.py:310
  28.5 2.1 %collective-permute-start.2 = (bf16[80,1024]{1,0:T(8,128)(2,1)S(1)}, bf16[80,1024]{1,0:T(8,128)(2,1)S(1)}, u32[]{:S(2)}, u32[]{:S(2)}) collective-permute-start(bf16[80,1024]{1,0:T(8,128)(2,1)S(1)} %constant_dynamic-update-slice_fusion.y_ref.refs_0_), channel_id=1, source_target_pairs={{0,16},{16,0},{32,48},{48,32},{64,80},{80,64},{96,112},{112,96},{1... | collective-permute-start | bytes 491528 | tf_op jit(solution)/shard_map/ppermute | solution.py:310
  30.6 0.1 shard_map.69.refs_2_.near_ref
  30.8 4.9 %shard_map.70.refs_2_ = f32[4,2048]{1,0:T(4,128)S(1)} custom-call(bf16[80,1024]{1,0:T(8,128)(2,1)S(1)} %constant_dynamic-update-slice_fusion.y_ref.refs_0_, bf16[4,64,2048]{2,1,0:T(8,128)(2,1)S(1)} %all-to-all-done.refs_1_.x_ref, bf16[1024,128]{1,0:T(8,128)(2,1)S(1)} %shard_map.69.refs_2_.near_ref), custom_call_target="tpu_custom_call" | custom-call | flops 2147483648 | bytes 4194304 | tf_op jit(solution)/shard_map/pallas_call | solution.py:275
  35.7 0.7 copy-done.1
  36.4 5.0 %shard_map.71 = (bf16[1024,128]{1,0:T(8,128)(2,1)S(1)}, f32[4,2560]{1,0:T(4,128)S(1)}, f32[1,256]{1,0:T(1,128)S(1)}) custom-call(bf16[80,1024]{1,0:T(8,128)(2,1)S(1)} %collective-permute-done.2.refs_0_, bf16[4,64,2048]{2,1,0:T(8,128)(2,1)S(1)} %all-to-all-done.refs_1_.x_ref, f32[4,2048]{1,0:T(4,128)S(1)} %shard_map.70.refs_2_, f32[1,2048]{1,0:T(1,128)S(1)} %bitcast.19, ...), custom_call_target="tpu_custom_call" | custom-call | flops 2147483648 | bytes 4194304 | tf_op jit(solution)/shard_map/pallas_call | solution.py:275
  41.4 10.7 %all_to_all.27.logw_ref = f32[4,4,2560]{2,1,0:T(4,128)S(1)} all-to-all(f32[4,4,2560]{2,1,0:T(4,128)S(1)} %broadcast_in_dim.6), channel_id=1, replica_groups={{0,128,256,384},{16,144,272,400},{32,160,288,416},{48,176,304,432},{64,..., dimensions={0} | all-to-all | bytes 327680 | tf_op jit(solution)/shard_map/all_to_all | solution.py:317
  52.3 10.0 %all_to_all.28 = f32[8,4,2048]{2,1,0:T(4,128)S(1)} all-to-all(f32[8,4,2048]{2,1,0:T(4,128)S(1)} %broadcast_in_dim.7), channel_id=1, replica_groups={{0,1,2,3,4,5,6,7},{8,9,10,11,12,13,14,15},{16,17,18,19,20,21,22,23},{24..., dimensions={0} | all-to-all | bytes 524288 | tf_op jit(solution)/shard_map/all_to_all | solution.py:317
  62.4 0.1 exponential_reduce_fusion
  62.5 13.5 %collective-permute-start.3 = (f32[4,2048]{1,0:T(4,128)S(1)}, f32[4,2048]{1,0:T(4,128)S(1)}, u32[]{:S(2)}, u32[]{:S(2)}) collective-permute-start(f32[4,2048]{1,0:T(4,128)S(1)} %log_add_fusion.1), channel_id=1, source_target_pairs={{0,8},{1,9},{2,10},{3,11},{4,12},{5,13},{6,14},{7,15},{8,0},{9,1},... | collective-permute-start | bytes 98312 | tf_op jit(solution)/shard_map/ppermute | solution.py:313
  76.1 1.9 %collective-permute-done.3 = f32[4,2048]{1,0:T(4,128)S(1)} collective-permute-done((f32[4,2048]{1,0:T(4,128)S(1)}, f32[4,2048]{1,0:T(4,128)S(1)}, u32[]{:S(2)}, u32[]{:S(2)}) %collective-permute-start.3) | collective-permute-done | bytes 32800 | tf_op jit(solution)/shard_map/ppermute | solution.py:313
  78.1 33.7 %shard_map.72 = f32[4,256]{1,0:T(4,128)S(1)} custom-call(s32[1]{0:T(128)} %bitcast.7.place_ref, bf16[1024,128]{1,0:T(8,128)(2,1)S(1)} %shard_map.69.refs_2_.near_ref, bf16[1024,128]{1,0:T(8,128)(2,1)S(1)} %get-tuple-element.14.far_ref, bf16[4,64,2048]{2,1,0:T(8,128)(2,1)S(1)} %all-to-all-done.refs_1_.x_ref, f32[4,2048]{1,0:T(4,128)S(1)} %log_add_fusion.total_ref, ...), custom_call_target="tpu_custom_call" | custom-call | flops 2147483648 | bytes 4194304 | tf_op jit(solution)/shard_map/pallas_call | solution.py:275
  111.8 6.9 %collective-permute-start.4 = (f32[4,256]{1,0:T(4,128)S(1)}, f32[4,256]{1,0:T(4,128)S(1)}, u32[]{:S(2)}, u32[]{:S(2)}) collective-permute-start(f32[4,256]{1,0:T(4,128)S(1)} %shard_map.72), channel_id=1, source_target_pairs={{0,64},{16,80},{32,96},{48,112},{64,0},{80,16},{96,32},{112,48},{1... | collective-permute-start | bytes 12296 | tf_op jit(solution)/shard_map/ppermute | solution.py:310
  118.7 33.7 %shard_map.73 = f32[4,256]{1,0:T(4,128)S(1)} custom-call(s32[1]{0:T(128)} %bitcast.7.place_ref, bf16[1024,128]{1,0:T(8,128)(2,1)S(1)} %shard_map.69.refs_2_.near_ref, bf16[1024,128]{1,0:T(8,128)(2,1)S(1)} %get-tuple-element.14.far_ref, bf16[4,64,2048]{2,1,0:T(8,128)(2,1)S(1)} %all-to-all-done.refs_1_.x_ref, f32[4,2048]{1,0:T(4,128)S(1)} %log_add_fusion.total_ref, ...), custom_call_target="tpu_custom_call" | custom-call | flops 2147483648 | bytes 4194304 | tf_op jit(solution)/shard_map/pallas_call | solution.py:275
  152.4 0.6 copy.11
  153.0 4.8 %all-to-all-start.3 = ((f32[4,1,256]{2,1,0:T(1,128)}), f32[4,1,256]{2,1,0:T(1,128)S(1)}, u32[]{:S(2)}, u32[]{:S(2)}) async-start(f32[4,1,256]{2,1,0:T(1,128)} %copy.11), calls=%async_computation.3 | async-start | bytes 8192 | tf_op jit(solution)/shard_map/all_to_all | solution.py:421
  157.9 0.6 subtract_multiply_fusion
  158.5 5.0 %all-to-all-done.3 = f32[4,1,256]{2,1,0:T(1,128)S(1)} async-done(((f32[4,1,256]{2,1,0:T(1,128)}), f32[4,1,256]{2,1,0:T(1,128)S(1)}, u32[]{:S(2)}, u32[]{:S(2)}) %all-to-all-start.3) | async-done | bytes 4128 | tf_op jit(solution)/shard_map/all_to_all | solution.py:421
  163.5 0.6 subtract_multiply_fusion.1
  (26 shorter events, 0.5 us)
Async XLA Ops:
  3.3 4.5 %copy-start.3 = (bf16[80,256]{1,0:T(8,128)(2,1)S(1)}, bf16[80,256]{1,0:T(8,128)(2,1)}, u32[]{:S(2)}) copy-start(bf16[80,256]{1,0:T(8,128)(2,1)} %get-tuple-element.10) | copy-start | bytes 122884
  3.3 27.5 %all-to-all-start = ((bf16[4,64,2048]{2,1,0:T(8,128)(2,1)}), bf16[4,64,2048]{2,1,0:T(8,128)(2,1)S(1)}, u32[]{:S(2)}, u32[]{:S(2)}) async-start(bf16[4,64,2048]{2,1,0:T(8,128)(2,1)} %get-tuple-element.11), calls=%async_computation | async-start | bytes 2097152 | tf_op jit(solution)/shard_map/all_to_all | solution.py:344
  7.8 11.5 %collective-permute-start = (bf16[80,256]{1,0:T(8,128)(2,1)S(1)}, bf16[80,256]{1,0:T(8,128)(2,1)S(1)}, u32[]{:S(2)}, u32[]{:S(2)}) collective-permute-start(bf16[80,256]{1,0:T(8,128)(2,1)S(1)} %copy-done.3), channel_id=1, source_target_pairs={{0,64},{16,80},{32,96},{48,112},{64,0},{80,16},{96,32},{112,48},{1... | collective-permute-start | bytes 122888 | tf_op jit(solution)/shard_map/ppermute | solution.py:310
  19.3 9.3 %collective-permute-start.1 = (bf16[80,512]{1,0:T(8,128)(2,1)S(1)}, bf16[80,512]{1,0:T(8,128)(2,1)S(1)}, u32[]{:S(2)}, u32[]{:S(2)}) collective-permute-start(bf16[80,512]{1,0:T(8,128)(2,1)S(1)} %pad_maximum_fusion), channel_id=1, source_target_pairs={{0,32},{16,48},{32,0},{48,16},{64,96},{80,112},{96,64},{112,80},{1... | collective-permute-start | bytes 245768 | tf_op jit(solution)/shard_map/ppermute | solution.py:310
  28.5 7.2 %collective-permute-start.2 = (bf16[80,1024]{1,0:T(8,128)(2,1)S(1)}, bf16[80,1024]{1,0:T(8,128)(2,1)S(1)}, u32[]{:S(2)}, u32[]{:S(2)}) collective-permute-start(bf16[80,1024]{1,0:T(8,128)(2,1)S(1)} %constant_dynamic-update-slice_fusion.y_ref.refs_0_), channel_id=1, source_target_pairs={{0,16},{16,0},{32,48},{48,32},{64,80},{80,64},{96,112},{112,96},{1... | collective-permute-start | bytes 491528 | tf_op jit(solution)/shard_map/ppermute | solution.py:310
  30.8 5.0 %copy-start = (f32[2048]{0:T(1024)S(1)}, f32[2048]{0:T(1024)}, u32[]{:S(2)}) copy-start(f32[2048]{0:T(1024)} %param.6) | copy-start | bytes 24580
  35.7 0.7 copy-start.1
  62.4 13.6 %copy-start.2 = (bf16[2048,64]{0,1:T(8,128)(2,1)S(1)}, bf16[2048,64]{0,1:T(8,128)(2,1)}, u32[]{:S(2)}) copy-start(bf16[2048,64]{0,1:T(8,128)(2,1)} %param.5) | copy-start | bytes 786436
  62.5 15.5 %collective-permute-start.3 = (f32[4,2048]{1,0:T(4,128)S(1)}, f32[4,2048]{1,0:T(4,128)S(1)}, u32[]{:S(2)}, u32[]{:S(2)}) collective-permute-start(f32[4,2048]{1,0:T(4,128)S(1)} %log_add_fusion.1), channel_id=1, source_target_pairs={{0,8},{1,9},{2,10},{3,11},{4,12},{5,13},{6,14},{7,15},{8,0},{9,1},... | collective-permute-start | bytes 98312 | tf_op jit(solution)/shard_map/ppermute | solution.py:313
  111.8 40.6 %collective-permute-start.4 = (f32[4,256]{1,0:T(4,128)S(1)}, f32[4,256]{1,0:T(4,128)S(1)}, u32[]{:S(2)}, u32[]{:S(2)}) collective-permute-start(f32[4,256]{1,0:T(4,128)S(1)} %shard_map.72), channel_id=1, source_target_pairs={{0,64},{16,80},{32,96},{48,112},{64,0},{80,16},{96,32},{112,48},{1... | collective-permute-start | bytes 12296 | tf_op jit(solution)/shard_map/ppermute | solution.py:310
  153.0 10.4 %all-to-all-start.3 = ((f32[4,1,256]{2,1,0:T(1,128)}), f32[4,1,256]{2,1,0:T(1,128)S(1)}, u32[]{:S(2)}, u32[]{:S(2)}) async-start(f32[4,1,256]{2,1,0:T(1,128)} %copy.11), calls=%async_computation.3 | async-start | bytes 8192 | tf_op jit(solution)/shard_map/all_to_all | solution.py:421
